TPU v7x, 32 devices: a whole 2x2x4 slice. The times are simulated.
32 devices in a mesh: dp: 4 (over z), tensor: 8 (over y, x, core).
Axes of the slice: x: 2, y: 2, z: 4, core: 2. Of those that a mesh axis runs over, the one named last changes fastest.
Arguments:
- tokens: bfloat16 [256, 4096], P(('dp', 'tensor')), may hold values from -6 to 6
- out_grad: bfloat16 [256, 4096], P(('dp', 'tensor')), may hold values from -6 to 6
- gate_blocks: bfloat16 [1792, 128, 128], P('tensor'), may hold values from -0.125 to 0.125
- up_blocks: bfloat16 [1792, 128, 128], P('tensor'), may hold values from -0.125 to 0.125
- down_blocks: bfloat16 [1792, 128, 128], P('tensor'), may hold values from -0.0625 to 0.0625
- gate_index: int32 [8, 224], P('tensor'), may hold values from 0 to 447, as said below
- up_index: int32 [8, 224], P('tensor'), may hold values from 0 to 447, as said below
- down_index: int32 [8, 224], P('tensor'), may hold values from 0 to 447, as said below
- gate_slot: int32 [8, 224], P('tensor'), may hold values from 0 to 279, as said below
- up_slot: int32 [8, 224], P('tensor'), may hold values from 0 to 279, as said below
- down_slot: int32 [8, 224], P('tensor'), may hold values from 0 to 279, as said below
Outputs:
- layer_out: bfloat16 [256, 4096], P(('dp', 'tensor'))
- token_grad: bfloat16 [256, 4096], P(('dp', 'tensor'))
- gate_grad: float32 [8, 280, 128, 128], P('tensor', 'dp')
- up_grad: float32 [8, 280, 128, 128], P('tensor', 'dp')
- down_grad: float32 [8, 280, 128, 128], P('tensor', 'dp')
Inputs may be any that keep to these rules, and one draw needn't show every extreme that they name: `gate_index`: each row holds 224 distinct block numbers in increasing order. `up_index`: each row holds 224 distinct block numbers in increasing order. `down_index`: each row holds 224 distinct block numbers in increasing order. `gate_slot`: each row's 224 values are distinct; value v is slot v % 70 of data group v // 70; in every row some data group receives exactly 70 blocks. `up_slot`: each row's 224 values are distinct; value v is slot v % 70 of data group v // 70; in every row some data group receives exactly 70 blocks. `down_slot`: each row's 224 values are distinct; value v is slot v % 70 of data group v // 70; in every row some data group receives exactly 70 blocks.
All inputs are finite; a program needn't handle non-finite values.
Results may differ from a plain program's by a relative error of at most 0.019.
Values may be sent and summed in bfloat16 or wider, within the bound.
No kernel may reach another device: no remote copies, remote signals or barrier semaphores. Data moves between devices by JAX's collectives and lax.ppermute only.
A program may use at most 192 MiB of HBM per device.

v0:
```python
import math

import jax
import jax.numpy as jnp
from jax import lax
from jax.sharding import PartitionSpec as P

FF = 14336


def col_sums(picked, blocks, block_cols, out_count):
    product = jnp.einsum("tkd,kde->tke", picked, blocks, preferred_element_type=jnp.float32)
    onehot = (block_cols[:, None] == jnp.arange(out_count, dtype=jnp.int32)[None, :]).astype(
        jnp.float32
    )
    summed = jnp.einsum("tke,kc->tce", product, onehot, precision=lax.Precision.HIGHEST)
    return summed.reshape(summed.shape[0], out_count * blocks.shape[2])


def row_sums(picked, blocks, block_rows, out_count):
    product = jnp.einsum("tke,kde->tkd", picked, blocks, preferred_element_type=jnp.float32)
    onehot = (block_rows[:, None] == jnp.arange(out_count, dtype=jnp.int32)[None, :]).astype(
        jnp.float32
    )
    summed = jnp.einsum("tkd,kr->trd", product, onehot, precision=lax.Precision.HIGHEST)
    return summed.reshape(summed.shape[0], out_count * blocks.shape[1])


def block_terms(picked_left, picked_right, factor):
    return (
        jnp.einsum("tkd,tke->kde", picked_left, picked_right, preferred_element_type=jnp.float32)
        * factor
    )


def owner_buffer(terms, slots, slot_total):
    return jnp.zeros((slot_total,) + terms.shape[1:], jnp.float32).at[slots].set(terms)


def local(
    tokens,
    out_grad,
    gate_blocks,
    up_blocks,
    down_blocks,
    gate_index,
    up_index,
    down_index,
    gate_slot,
    up_slot,
    down_slot,
):
    model_width = tokens.shape[1]
    block_size = gate_blocks.shape[1]
    kept_count = gate_blocks.shape[0]
    group_count = lax.axis_size("dp")
    d_cols = model_width // block_size
    ff_cols = FF // (lax.axis_size("tensor") * block_size)
    capacity = (kept_count + group_count - 1) // group_count + kept_count // (4 * group_count)
    slot_total = group_count * capacity
    gate_ids, up_ids, down_ids = (gate_index[0], up_index[0], down_index[0])
    gate_rows, gate_cols = (gate_ids // ff_cols, gate_ids % ff_cols)
    up_rows, up_cols = (up_ids // ff_cols, up_ids % ff_cols)
    down_rows, down_cols = (down_ids // d_cols, down_ids % d_cols)
    gathered = lax.all_gather(tokens, "tensor", axis=0, tiled=True)
    row_total = gathered.shape[0]
    factor = 1.0 / math.sqrt(row_total * group_count)
    token_blocks = gathered.reshape(row_total, d_cols, block_size)
    tokens_gate = jnp.take(token_blocks, gate_rows, axis=1)
    tokens_up = jnp.take(token_blocks, up_rows, axis=1)
    gate_act = col_sums(tokens_gate, gate_blocks, gate_cols, ff_cols)
    up_act = col_sums(tokens_up, up_blocks, up_cols, ff_cols)
    sigma = jax.nn.sigmoid(gate_act)
    hidden = (gate_act * sigma * up_act).astype(jnp.bfloat16)
    hidden_blocks = hidden.reshape(row_total, ff_cols, block_size)
    hidden_picked = jnp.take(hidden_blocks, down_rows, axis=1)
    layer_out = lax.psum_scatter(
        col_sums(hidden_picked, down_blocks, down_cols, d_cols).astype(jnp.bfloat16),
        "tensor",
        scatter_dimension=0,
        tiled=True,
    )
    cot_rows = lax.all_gather(out_grad, "tensor", axis=0, tiled=True)
    cot_blocks = cot_rows.reshape(row_total, d_cols, block_size)
    cot_picked = jnp.take(cot_blocks, down_cols, axis=1)
    hidden_grad = row_sums(cot_picked, down_blocks, down_rows, ff_cols)
    down_terms = block_terms(hidden_picked, cot_picked, factor)
    gate_pre = (hidden_grad * up_act * sigma * (1.0 + gate_act * (1.0 - sigma))).astype(
        jnp.bfloat16
    )
    up_pre = (hidden_grad * gate_act * sigma).astype(jnp.bfloat16)
    gate_pre_picked = jnp.take(gate_pre.reshape(row_total, ff_cols, block_size), gate_cols, axis=1)
    up_pre_picked = jnp.take(up_pre.reshape(row_total, ff_cols, block_size), up_cols, axis=1)
    first_part = row_sums(gate_pre_picked, gate_blocks, gate_rows, d_cols)
    token_grad = lax.psum_scatter(
        (first_part + row_sums(up_pre_picked, up_blocks, up_rows, d_cols)).astype(jnp.bfloat16),
        "tensor",
        scatter_dimension=0,
        tiled=True,
    )
    gate_terms = block_terms(tokens_gate, gate_pre_picked, factor)
    up_terms = block_terms(tokens_up, up_pre_picked, factor)
    gate_out, up_out, down_out = (
        lax.psum_scatter(
            owner_buffer(gate_terms, gate_slot[0], slot_total).astype(jnp.bfloat16),
            "dp",
            scatter_dimension=0,
            tiled=True,
        ).astype(jnp.float32),
        lax.psum_scatter(
            owner_buffer(up_terms, up_slot[0], slot_total).astype(jnp.bfloat16),
            "dp",
            scatter_dimension=0,
            tiled=True,
        ).astype(jnp.float32),
        lax.psum_scatter(
            owner_buffer(down_terms, down_slot[0], slot_total).astype(jnp.bfloat16),
            "dp",
            scatter_dimension=0,
            tiled=True,
        ).astype(jnp.float32),
    )
    return (layer_out, token_grad, gate_out[None], up_out[None], down_out[None])


def solution(mesh):
    in_specs = (
        P(("dp", "tensor"), None),
        P(("dp", "tensor"), None),
        P("tensor", None, None),
        P("tensor", None, None),
        P("tensor", None, None),
        P("tensor", None),
        P("tensor", None),
        P("tensor", None),
        P("tensor", None),
        P("tensor", None),
        P("tensor", None),
    )
    out_specs = (
        P(("dp", "tensor"), None),
        P(("dp", "tensor"), None),
        P("tensor", "dp", None, None),
        P("tensor", "dp", None, None),
        P("tensor", "dp", None, None),
    )
    return jax.shard_map(local, mesh=mesh, in_specs=in_specs, out_specs=out_specs, check_vma=False)
```

profile of v0, /device:TPU:0, one launch (start us, length us, event | category | flops | bytes accessed | tf_op | source)
XLA Modules:
  0.0 715.5 jit_solution(13800893154906406538)
XLA Ops:
  10.6 11.6 %all_gather.6 = bf16[64,4096]{1,0:T(8,128)(2,1)S(1)} all-gather(bf16[8,4096]{1,0:T(8,128)(2,1)} %param.15), channel_id=1, replica_groups=mesh['dp'=4,'tensor'=8] {'tensor'}, dimensions={0}, use_global_device_ids=true | all-gather | bytes 589824 | tf_op jit(solution)/shard_map/all_gather | solution.py:65
  28.2 6.4 fusion.33
  34.7 6.6 fusion.8
  41.3 9.7 %all_gather.7 = bf16[64,4096]{1,0:T(8,128)(2,1)S(1)} all-gather(bf16[8,4096]{1,0:T(8,128)(2,1)S(1)} %copy-done.2), channel_id=1, replica_groups=mesh['dp'=4,'tensor'=8] {'tensor'}, dimensions={0}, use_global_device_ids=true | all-gather | bytes 589824 | tf_op jit(solution)/shard_map/all_gather | solution.py:83
  53.4 6.6 fusion.10
  62.9 9.6 %fusion.39 = f32[64,224,128]{2,0,1:T(8,128)S(1)} fusion(bf16[224,128,128]{2,1,0:T(8,128)(2,1)} %param.19, bf16[224,64,128]{2,1,0:T(8,128)(2,1)} %gather_fusion.3, pred[224]{0:T(512)(128)(4,1)S(1)} %get-tuple-element.11), kind=kOutput, calls=%fused_computation.51 | convolution fusion | flops 471597056 | bytes 18350304 | tf_op jit(solution)/shard_map/tke,kde->tkd/dot_general | solution.py:21
  72.5 6.6 fusion.4
  82.6 11.1 %convolution_multiply_fusion.1 = f32[224,128,128]{2,1,0:T(8,128)} fusion(bf16[224,64,128]{2,1,0:T(8,128)(2,1)} %gather_fusion.1, pred[224]{0:T(512)(128)(4,1)S(1)} %get-tuple-element.28, bf16[224,64,128]{2,1,0:T(8,128)(2,1)} %gather_fusion.5, pred[224]{0:T(512)(128)(4,1)S(1)} %get-tuple-element.9), kind=kOutput, calls=%fused_computation.10 | convolution fusion | flops 477102080 | bytes 22020544 | tf_op jit(solution)/shard_map/tkd,tke->kde/dot_general | solution.py:31
  93.7 8.8 %broadcast.208.clone.1 = f32[280,128,128]{2,1,0:T(8,128)} broadcast(f32[]{:T(128)} %constant.74.clone.1), dimensions={} | broadcast | bytes 18350084 | tf_op jit(solution)/shard_map/broadcast.9
  102.4 40.6 %scatter_fusion.1 = f32[280,128,128]{2,1,0:T(8,128)} fusion(f32[280,128,128]{2,1,0:T(8,128)} %broadcast.208.clone.1, s32[224]{0:T(256)S(1)} %bitcast.168, f32[224,128,128]{2,1,0:T(8,128)} %convolution_multiply_fusion.1), kind=kCustom, calls=%fused_computation.7 | custom fusion | bytes 44041088 | tf_op jit(solution)/shard_map/scatter | solution.py:37
  143.0 11.3 %convert_element_type.58 = bf16[280,128,128]{2,1,0:T(8,128)(2,1)} convert(f32[280,128,128]{2,1,0:T(8,128)} %scatter_fusion.1) | non-fusion elementwise | flops 4587520 | bytes 27525120 | tf_op jit(solution)/shard_map/convert_element_type | solution.py:111
  157.3 11.1 %convolution_multiply_fusion.2 = f32[224,128,128]{2,1,0:T(8,128)} fusion(bf16[224,64,128]{2,1,0:T(8,128)(2,1)} %gather_fusion, pred[224]{0:T(512)(128)(4,1)S(1)} %get-tuple-element.24, bf16[224,64,128]{2,1,0:T(8,128)(2,1)} %gather_fusion.4, pred[224]{0:T(512)(128)(4,1)S(1)} %get-tuple-element.7), kind=kOutput, calls=%fused_computation.11 | convolution fusion | flops 477102080 | bytes 22020544 | tf_op jit(solution)/shard_map/tkd,tke->kde/dot_general | solution.py:31
  168.5 8.6 %broadcast.208.clone = f32[280,128,128]{2,1,0:T(8,128)} broadcast(f32[]{:T(128)} %constant.74.clone.1), dimensions={} | broadcast | bytes 18350084 | tf_op jit(solution)/shard_map/broadcast.9
  177.1 40.8 %scatter_fusion = f32[280,128,128]{2,1,0:T(8,128)} fusion(f32[280,128,128]{2,1,0:T(8,128)} %broadcast.208.clone, s32[224]{0:T(256)S(1)} %bitcast.170, f32[224,128,128]{2,1,0:T(8,128)} %convolution_multiply_fusion.2), kind=kCustom, calls=%fused_computation.6 | custom fusion | bytes 44041088 | tf_op jit(solution)/shard_map/scatter | solution.py:37
  217.8 11.5 %convert_element_type.57 = bf16[280,128,128]{2,1,0:T(8,128)(2,1)} convert(f32[280,128,128]{2,1,0:T(8,128)} %scatter_fusion) | non-fusion elementwise | flops 4587520 | bytes 27525120 | tf_op jit(solution)/shard_map/convert_element_type | solution.py:105
  232.4 11.1 %convolution_multiply_fusion = f32[224,128,128]{2,1,0:T(8,128)} fusion(bf16[224,64,128]{2,1,0:T(8,128)(2,1)} %gather_fusion.2, pred[224]{0:T(512)(128)(4,1)S(1)} %get-tuple-element.22, bf16[224,64,128]{2,1,0:T(8,128)(2,1)} %gather_fusion.3, pred[224]{0:T(512)(128)(4,1)S(1)} %get-tuple-element.11), kind=kOutput, calls=%fused_computation.9 | convolution fusion | flops 477102080 | bytes 22020544 | tf_op jit(solution)/shard_map/tkd,tke->kde/dot_general | solution.py:31
  243.5 8.6 %broadcast.208.clone.2 = f32[280,128,128]{2,1,0:T(8,128)} broadcast(f32[]{:T(128)} %constant.74.clone.1), dimensions={} | broadcast | bytes 18350084 | tf_op jit(solution)/shard_map/broadcast.9
  252.1 40.7 %scatter_fusion.2 = f32[280,128,128]{2,1,0:T(8,128)} fusion(f32[280,128,128]{2,1,0:T(8,128)} %broadcast.208.clone.2, s32[224]{0:T(256)S(1)} %bitcast.169, f32[224,128,128]{2,1,0:T(8,128)} %convolution_multiply_fusion), kind=kCustom, calls=%fused_computation.8 | custom fusion | bytes 44041088 | tf_op jit(solution)/shard_map/scatter | solution.py:37
  292.9 11.4 %convert_element_type.59 = bf16[280,128,128]{2,1,0:T(8,128)(2,1)} convert(f32[280,128,128]{2,1,0:T(8,128)} %scatter_fusion.2) | non-fusion elementwise | flops 4587520 | bytes 27525120 | tf_op jit(solution)/shard_map/convert_element_type | solution.py:117
  304.5 9.3 %fusion.45 = f32[64,224,128]{2,0,1:T(8,128)S(1)} fusion(bf16[224,128,128]{2,1,0:T(8,128)(2,1)} %param.18, bf16[224,64,128]{2,1,0:T(8,128)(2,1)} %gather_fusion.5, pred[224]{0:T(512)(128)(4,1)S(1)} %get-tuple-element.9), kind=kOutput, calls=%fused_computation.53 | convolution fusion | flops 471597056 | bytes 18350304 | tf_op jit(solution)/shard_map/tke,kde->tkd/dot_general | solution.py:21
  313.9 6.8 fusion
  320.7 7.7 %fusion.42 = f32[64,224,128]{2,0,1:T(8,128)S(1)} fusion(bf16[224,128,128]{2,1,0:T(8,128)(2,1)} %param.17, bf16[224,64,128]{2,1,0:T(8,128)(2,1)S(1)} %copy-done.1, pred[224]{0:T(512)(128)(4,1)S(1)} %get-tuple-element.7), kind=kOutput, calls=%fused_computation.52 | convolution fusion | flops 471597056 | bytes 18350304 | tf_op jit(solution)/shard_map/tke,kde->tkd/dot_general | solution.py:21
  328.5 6.8 fusion.51
  336.5 6.3 fusion.36
  342.9 6.8 fusion.54
  350.8 4.4 bitcast_convert_fusion.1
  355.2 116.8 %reduce-scatter.10.cloned.1.call-done = bf16[70,128,128]{2,1,0:T(8,128)(2,1)} async-done(((bf16[280,128,128]{2,1,0:T(8,128)(2,1)}), bf16[70,128,128]{2,1,0:T(8,128)(2,1)}) %reduce-scatter.10.cloned.1.call-update) | async-done | bytes 2293776 | tf_op jit(solution)/shard_map/reduce_scatter | solution.py:104
  472.0 4.4 bitcast_convert_fusion.2
  476.4 155.9 %reduce-scatter.14.cloned.1.call-done = bf16[70,128,128]{2,1,0:T(8,128)(2,1)} async-done(((bf16[280,128,128]{2,1,0:T(8,128)(2,1)}), bf16[70,128,128]{2,1,0:T(8,128)(2,1)}) %reduce-scatter.14.cloned.1.call-update) | async-done | bytes 2293776 | tf_op jit(solution)/shard_map/reduce_scatter | solution.py:116
  632.3 4.4 bitcast_convert_fusion
  636.7 34.1 %reduce-scatter.8.cloned.1.call-done = bf16[8,4096]{1,0:T(8,128)(2,1)} async-done(((bf16[64,4096]{1,0:T(8,128)(2,1)}), bf16[8,4096]{1,0:T(8,128)(2,1)}) %reduce-scatter.8.cloned.1.call-update) | async-done | bytes 65552 | tf_op jit(solution)/shard_map/reduce_scatter | solution.py:95
  670.8 38.0 %reduce-scatter.6.cloned.1.call-done = bf16[8,4096]{1,0:T(8,128)(2,1)} async-done(((bf16[64,4096]{1,0:T(8,128)(2,1)}), bf16[8,4096]{1,0:T(8,128)(2,1)}) %reduce-scatter.6.cloned.1.call-update) | async-done | bytes 65552 | tf_op jit(solution)/shard_map/reduce_scatter | solution.py:77
  (68 shorter events, 26.6 us)
Async XLA Ops:
  7.2 343.6 %reduce-scatter.12.cloned.1.call-start = ((), (), s32[]{:S(2)}) async-start(), calls=%async_computation.8 | async-start | bytes 11468800 | tf_op jit(solution)/shard_map/reduce_scatter | solution.py:110
  10.0 0.6 copy-start.3
  28.2 23.0 %slice-start = ((s8[7340032]{0:T(1024)(128)(4,1)}), s8[4194304]{0:T(1024)(128)(4,1)S(1)}, s32[]{:S(2)}) async-start(s8[7340032]{0:T(1024)(128)(4,1)} %bitcast.162), calls=%async_computation.10 | async-start | bytes 8388608
  28.2 23.1 %slice-start.1 = ((s8[7340032]{0:T(1024)(128)(4,1)}), s8[3145728]{0:T(1024)(128)(4,1)S(1)}, s32[]{:S(2)}) async-start(s8[7340032]{0:T(1024)(128)(4,1)} %bitcast.162), calls=%async_computation.11 | async-start | bytes 6291456
  34.6 6.6 copy-start.8
  34.6 6.7 copy-start.2
  34.6 16.6 %copy-start.5 = (s32[1,224]{1,0:T(1,128)S(1)}, s32[1,224]{1,0:T(1,128)}, u32[]{:S(2)}) copy-start(s32[1,224]{1,0:T(1,128)} %param.24) | copy-start | bytes 2692
  34.7 16.6 %copy-start = (bf16[224,64,128]{2,1,0:T(8,128)(2,1)S(1)}, bf16[224,64,128]{2,1,0:T(8,128)(2,1)}, u32[]{:S(2)}) copy-start(bf16[224,64,128]{2,1,0:T(8,128)(2,1)} %gather_fusion) | copy-start | bytes 11010052
  154.4 317.7 %reduce-scatter.10.cloned.1.call-start = ((), (), s32[]{:S(2)}) async-start(), calls=%async_computation.7 | async-start | bytes 11468800 | tf_op jit(solution)/shard_map/reduce_scatter | solution.py:104
  154.4 2.9 copy-start.6
  229.4 402.9 %reduce-scatter.14.cloned.1.call-start = ((), (), s32[]{:S(2)}) async-start(), calls=%async_computation.9 | async-start | bytes 11468800 | tf_op jit(solution)/shard_map/reduce_scatter | solution.py:116
  229.5 2.9 copy-start.7
  304.3 366.5 %reduce-scatter.8.cloned.1.call-start = ((), (), s32[]{:S(2)}) async-start(), calls=%async_computation.6 | async-start | bytes 589824 | tf_op jit(solution)/shard_map/reduce_scatter | solution.py:95
  313.9 6.8 copy-start.1
  320.7 7.8 %copy-start.4 = (s32[224]{0:T(256)S(1)}, s32[224]{0:T(256)}, u32[]{:S(2)}) copy-start(s32[224]{0:T(256)} %copy-done.3) | copy-start | bytes 2692
  336.3 372.5 %reduce-scatter.6.cloned.1.call-start = ((), (), s32[]{:S(2)}) async-start(), calls=%async_computation.5 | async-start | bytes 589824 | tf_op jit(solution)/shard_map/reduce_scatter | solution.py:77
Sparse Core Ops, SparseCore 0:
  154.5 157.2 reduce-scatter.11
  314.1 157.8 reduce-scatter.9
  474.4 157.8 reduce-scatter.13
  635.8 34.9 reduce-scatter.7
  674.6 34.1 reduce-scatter.5
where the time goes:
time: 726 us; the launch traced here: 716 us
  waiting for transfers between devices  345 us (48%)
  local copies, waits for them, and re-layouts  168 us (23%)
  matrix products  115 us (16%)
  other arithmetic  50.8 us (7%)
  blocking collectives  21.3 us (3%)
  between operations  14.3 us (2%)
    reduce_scatter x1, waiting for transfers between devices, local(): lax.psum_scatter(owner_buffer(down_terms, down_slot[0], slot_total).astyp...  156 us
    scatter x3, local copies, waits for them, and re-layouts, owner_buffer(): jnp.zeros((slot_total,) + terms.shape[1:], jnp.float32).at[slots].set(terms)  122 us
    reduce_scatter x1, waiting for transfers between devices, local(): lax.psum_scatter(owner_buffer(gate_terms, gate_slot[0], slot_total).astyp...  117 us
    reduce_scatter x1, waiting for transfers between devices, local(): lax.psum_scatter(col_sums(hidden_picked, down_blocks, down_cols, d_cols)....  38 us
    reduce_scatter x1, waiting for transfers between devices, local(): lax.psum_scatter((first_part + row_sums(up_pre_picked, up_blocks, up_rows...  34.1 us
    dot_general x3, matrix products, block_terms(): jnp.einsum('tkd,tke->kde', picked_left, picked_right, preferred_element_t...  33.3 us
    dot_general x3, matrix products, row_sums(): jnp.einsum('tke,kde->tkd', picked, blocks, preferred_element_type=jnp.flo...  26.7 us
    another operation x3, local copies, waits for them, and re-layouts  26 us
  transfers between devices with their start and end apart: 5, of which 4 were waited for; matrix products, arithmetic and copies ran while one was open for 29% of the time, Pallas kernels for 0%

commit v1 on v0

v1 whole, which is shorter than its diff:
```python
import functools
import math

import jax
import jax.numpy as jnp
from jax import lax
from jax.experimental import pallas as pl
from jax.experimental.pallas import tpu as pltpu
from jax.sharding import PartitionSpec as P

FF = 14336
BF16 = jnp.bfloat16
F32 = jnp.float32
VMEM = pltpu.VMEM
SMEM = pltpu.SMEM


def in_vmem():
    return pl.BlockSpec(memory_space=VMEM)


def pinned(*arrays):
    return [pltpu.with_memory_space_constraint(x, VMEM) for x in arrays]


def dot_nn(a, b):
    return lax.dot_general(a, b, (((1,), (0,)), ((), ())), preferred_element_type=F32)


def dot_nt(a, b):
    return lax.dot_general(a, b, (((1,), (1,)), ((), ())), preferred_element_type=F32)


def exchange(x, axis, flip):
    count = lax.axis_size(axis)
    return lax.ppermute(x, axis, [(i, i ^ flip) for i in range(count)])


def densify_body(gi, ui, di, gb, ub, db, wg, wu, wd, sem):
    kept = gb.shape[0]

    def fill(index, blocks, dense, slot):
        cols = dense.shape[1] // blocks.shape[2]
        size = blocks.shape[1]
        dense[...] = jnp.zeros_like(dense)

        def step(i, carry):
            for u in range(8):
                k = i * 8 + u
                b = index[0, k]
                r = pl.multiple_of((b // cols) * size, size)
                c = pl.multiple_of((b % cols) * size, size)
                pltpu.make_async_copy(
                    blocks.at[k], dense.at[pl.ds(r, size), pl.ds(c, size)], sem.at[slot]
                ).start()
            return carry

        lax.fori_loop(0, kept // 8, step, 0)

    fill(gi, gb, wg, 0)
    fill(ui, ub, wu, 1)
    fill(di, db, wd, 2)
    for slot, blocks in enumerate((gb, ub, db)):
        pltpu.make_async_copy(blocks, blocks, sem.at[slot]).wait()


def densify(gate_index, up_index, down_index, gate_blocks, up_blocks, down_blocks, width, hidden):
    smem = pl.BlockSpec(memory_space=SMEM)
    hbm = pl.BlockSpec(memory_space=pltpu.HBM)
    return pl.pallas_call(
        densify_body,
        out_shape=(
            VMEM((width, hidden), BF16),
            VMEM((width, hidden), BF16),
            VMEM((hidden, width), BF16),
        ),
        in_specs=[smem] * 3 + [hbm] * 3,
        out_specs=(in_vmem(),) * 3,
        scratch_shapes=[pltpu.SemaphoreType.DMA((3,))],
        compiler_params=pltpu.CompilerParams(vmem_limit_bytes=2 * 2**20),
        name="densify",
    )(
        gate_index,
        up_index,
        down_index,
        *(pltpu.with_memory_space_constraint(x, pltpu.HBM) for x in (gate_blocks, up_blocks, down_blocks)),
    )


def activations(x, wg, wu, wd, hid, gp, up):
    width = wg.shape[0]
    hidden = wg.shape[1]
    chunk = 256 if hidden % 256 == 0 else 128

    def step(n, carry):
        cols = pl.ds(pl.multiple_of(n * chunk, chunk), chunk)
        g = dot_nn(x[:, :width], wg[:, cols])
        u = dot_nn(x[:, :width], wu[:, cols])
        h = dot_nt(x[:, width:], wd[cols, :])
        s = jax.nn.sigmoid(g)
        hid[:, cols] = (g * s * u).astype(BF16)
        gp[:, cols] = (h * u * s * (1.0 + g * (1.0 - s))).astype(BF16)
        up[:, cols] = (h * g * s).astype(BF16)
        return carry

    lax.fori_loop(0, hidden // chunk, step, 0)


def own_body(x, wg, wu, wd, hid, gp, up, part):
    activations(x, wg, wu, wd, hid, gp, up)
    width = wg.shape[0]
    chunk = 512

    def step(n, carry):
        cols = pl.ds(pl.multiple_of(n * chunk, chunk), chunk)
        later = pl.ds(pl.multiple_of(width + n * chunk, chunk), chunk)
        part[:, cols] = dot_nn(hid[...], wd[:, cols]).astype(BF16)
        part[:, later] = (dot_nt(gp[...], wg[cols, :]) + dot_nt(up[...], wu[cols, :])).astype(BF16)
        return carry

    lax.fori_loop(0, width // chunk, step, 0)


def own_pass(x, wg, wu, wd):
    rows = x.shape[0]
    width, hidden = wg.shape
    act = jax.ShapeDtypeStruct((rows, hidden), BF16)
    return pl.pallas_call(
        own_body,
        out_shape=(act, act, act, jax.ShapeDtypeStruct((rows, 2 * width), BF16)),
        in_specs=[in_vmem()] * 4,
        out_specs=(in_vmem(),) * 4,
        compiler_params=pltpu.CompilerParams(vmem_limit_bytes=8 * 2**20),
        cost_estimate=pl.CostEstimate(
            flops=12 * rows * width * hidden, bytes_accessed=2**20, transcendentals=0
        ),
        name="own_pass",
    )(x, *pinned(wg, wu, wd))


def rest_body(xa, xb, wg, wu, wd, hid, gp, up, x, sem):
    half = xa.shape[0]
    copies = [
        pltpu.make_async_copy(xa, x.at[pl.ds(0, half)], sem.at[0]),
        pltpu.make_async_copy(xb, x.at[pl.ds(half, half)], sem.at[1]),
    ]
    for copy in copies:
        copy.start()
    for copy in copies:
        copy.wait()
    activations(x, wg, wu, wd, hid, gp, up)


def rest_pass(xa, xb, wg, wu, wd):
    rows = 2 * xa.shape[0]
    width, hidden = wg.shape
    act = jax.ShapeDtypeStruct((rows, hidden), BF16)
    need = rows * (2 * width + 3 * hidden) * 2
    return pl.pallas_call(
        rest_body,
        out_shape=(act, act, act),
        in_specs=[pl.BlockSpec(memory_space=pl.ANY)] * 2 + [in_vmem()] * 3,
        out_specs=(in_vmem(),) * 3,
        scratch_shapes=[VMEM((rows, 2 * width), BF16), pltpu.SemaphoreType.DMA((2,))],
        compiler_params=pltpu.CompilerParams(vmem_limit_bytes=need + 4 * 2**20),
        cost_estimate=pl.CostEstimate(
            flops=6 * rows * width * hidden, bytes_accessed=2**20, transcendentals=0
        ),
        name="rest_pass",
    )(xa, xb, *pinned(wg, wu, wd))


def grads_body(
    factor, size, spots, own, xa, xb, hid0, hid1, gp0, gp1, up0, up1,
    gate_out, up_out, down_out, tok, tok_t, hid, hid_t, gp, up, cot, sem,
):
    i = pl.program_id(0)
    per_step = gate_out.shape[0]
    d_cols = tok_t.shape[0]
    ff_cols = hid_t.shape[0]
    width = d_cols * size
    first, half = own.shape[0], xa.shape[0]

    @pl.when(i == 0)
    def _():
        def parts(n, dst, sources):
            at, out = 0, []
            for src in sources:
                rows = src.shape[0]
                out.append(pltpu.make_async_copy(src, dst.at[pl.ds(at, rows)], sem.at[n]))
                at += rows
            return out

        def side(lo):
            return [x.at[:, pl.ds(lo, width)] for x in (own, xa, xb)]

        copies = [
            parts(0, tok, side(0)),
            parts(1, hid, (hid0, hid1)),
            parts(2, gp, (gp0, gp1)),
            parts(3, up, (up0, up1)),
            parts(4, cot, side(width)),
        ]
        for group in copies:
            for copy in group:
                copy.start()

        def turn(src, dst):
            def step(n, carry):
                cols = pl.ds(pl.multiple_of(n * size, size), size)
                dst[n] = src[:, cols].T
                return carry

            lax.fori_loop(0, dst.shape[0], step, 0)

        pltpu.make_async_copy(tok, tok, sem.at[0]).wait()
        turn(tok, tok_t)
        pltpu.make_async_copy(hid, hid, sem.at[1]).wait()
        turn(hid, hid_t)
        for n, ref in ((2, gp), (3, up), (4, cot)):
            pltpu.make_async_copy(ref, ref, sem.at[n]).wait()

    def one(which, left, right, out, cols, j):
        spot = spots[which, i * per_step + j]
        b = jnp.maximum(spot, 0)
        c = pl.multiple_of((b % cols) * size, size)
        value = dot_nn(left[b // cols], right[:, pl.ds(c, size)]) * factor
        out[j] = jnp.where(spot >= 0, value, 0.0)

    for j in range(per_step):
        one(0, tok_t, gp, gate_out, ff_cols, j)
        one(1, tok_t, up, up_out, ff_cols, j)
        one(2, hid_t, cot, down_out, d_cols, j)


def grads(spots, own, xa, xb, acts0, acts1, size, cap, factor):
    per_step = max(n for n in range(1, 18) if cap % n == 0 and (cap > n or cap < 18))
    per_step = min(per_step, 10) if cap % 10 == 0 else per_step
    width = own.shape[1] // 2
    hidden = acts0[0].shape[1]
    rows = own.shape[0] + 2 * xa.shape[0]
    out = jax.ShapeDtypeStruct((cap, size, size), F32)
    block = pl.BlockSpec((per_step, size, size), lambda i: (i, 0, 0))
    scratch = [
        VMEM((rows, width), BF16),
        VMEM((width // size, size, rows), BF16),
        VMEM((rows, hidden), BF16),
        VMEM((hidden // size, size, rows), BF16),
        VMEM((rows, hidden), BF16),
        VMEM((rows, hidden), BF16),
        VMEM((rows, width), BF16),
    ]
    need = rows * (3 * width + 4 * hidden) * 2 + per_step * 6 * size * size * 4
    return pl.pallas_call(
        functools.partial(grads_body, factor, size),
        out_shape=(out, out, out),
        grid=(cap // per_step,),
        in_specs=[pl.BlockSpec(memory_space=SMEM)] + [pl.BlockSpec(memory_space=pl.ANY)] * 9,
        out_specs=(block, block, block),
        scratch_shapes=scratch + [pltpu.SemaphoreType.DMA((5,))],
        compiler_params=pltpu.CompilerParams(vmem_limit_bytes=need + 2**20),
        cost_estimate=pl.CostEstimate(
            flops=6 * cap * size * size * rows, bytes_accessed=12 * cap * size * size, transcendentals=0
        ),
        name="grads",
    )(spots, own, xa, xb, acts0[0], acts1[0], acts0[1], acts1[1], acts0[2], acts1[2])


def local(
    tokens,
    out_grad,
    gate_blocks,
    up_blocks,
    down_blocks,
    gate_index,
    up_index,
    down_index,
    gate_slot,
    up_slot,
    down_slot,
):
    rows, width = tokens.shape
    size = gate_blocks.shape[1]
    kept_count = gate_blocks.shape[0]
    groups = lax.axis_size("dp")
    slices = lax.axis_size("tensor")
    hidden = FF // slices
    cap = (kept_count + groups - 1) // groups + kept_count // (4 * groups)
    factor = 1.0 / math.sqrt(rows * slices * groups)

    wg, wu, wd = densify(
        gate_index, up_index, down_index, gate_blocks, up_blocks, down_blocks, width, hidden
    )

    mine = lax.axis_index("dp") * cap + jnp.arange(cap, dtype=jnp.int32)
    slots = jnp.concatenate([gate_slot, up_slot, down_slot])
    index = jnp.concatenate([gate_index, up_index, down_index])
    hit = slots[:, None, :] == mine[None, :, None]
    spots = jnp.sum(jnp.where(hit, index[:, None, :] + 1, 0), axis=2) - 1

    both = jnp.concatenate([tokens, out_grad], axis=1)
    pairs = range(2, slices, 2)

    def over_chips(x):
        return jnp.concatenate([x] + [exchange(x, "tensor", d) for d in pairs], axis=0)

    own_half = over_chips(both)
    own = jnp.concatenate([own_half, exchange(own_half, "tensor", 1)], axis=0)
    others = jnp.concatenate([exchange(both, "dp", a) for a in range(1, groups)], axis=0)
    xa = over_chips(others)
    xb = exchange(xa, "tensor", 1)

    *acts0, part = own_pass(own, wg, wu, wd)
    acts1 = rest_pass(xa, xb, wg, wu, wd)

    half = own_half.shape[0]
    chip = part[:half].astype(F32) + exchange(part[half:], "tensor", 1).astype(F32)
    chip = chip.astype(BF16).reshape(slices // 2, rows, 2 * width)
    total = chip[0].astype(F32)
    for n, d in enumerate(pairs):
        total = total + exchange(chip[n + 1], "tensor", d).astype(F32)
    total = total.astype(BF16)

    gate_out, up_out, down_out = grads(spots, own, xa, xb, acts0, acts1, size, cap, factor)
    return (total[:, :width], total[:, width:], gate_out[None], up_out[None], down_out[None])


def solution(mesh):
    in_specs = (
        P(("dp", "tensor"), None),
        P(("dp", "tensor"), None),
        P("tensor", None, None),
        P("tensor", None, None),
        P("tensor", None, None),
        P("tensor", None),
        P("tensor", None),
        P("tensor", None),
        P("tensor", None),
        P("tensor", None),
        P("tensor", None),
    )
    out_specs = (
        P(("dp", "tensor"), None),
        P(("dp", "tensor"), None),
        P("tensor", "dp", None, None),
        P("tensor", "dp", None, None),
        P("tensor", "dp", None, None),
    )
    return jax.shard_map(local, mesh=mesh, in_specs=in_specs, out_specs=out_specs, check_vma=False)
```

time: 726 us -> 153 us (0.21); the launches traced: 716 us -> 152 us
  waiting for transfers between devices: 345 us -> 22.8 us
  local copies, waits for them, and re-layouts: 168 us -> 50.1 us
  matrix products: 115 us -> 0 us
  Pallas kernels: 0 us -> 61.5 us
  other arithmetic: 50.8 us -> 0.46 us
  blocking collectives: 21.3 us -> 0 us
  starting transfers between devices: 0.59 us -> 16.6 us
  between operations: 14.3 us -> 0.93 us
    reduce_scatter x5 -> x0, waiting for transfers between devices: 345 us -> none  [the longest x1 156 us: local(): lax.psum_scatter(owner_buffer(down_terms, down_slot[0], slot_total).astyp...]
    scatter x3 -> x0, local copies, waits for them, and re-layouts: 122 us -> none  [owner_buffer(): jnp.zeros((slot_total,) + terms.shape[1:], jnp.float32).at[slots].set(terms)]
    dot_general x15 -> x0, matrix products: 115 us -> none  [the longest x3 33.3 us: block_terms(): jnp.einsum('tkd,tke->kde', picked_left, picked_right, preferred_element_t...]
    pallas_call x0 -> x4, Pallas kernels: none -> 61.5 us  [the longest x1 22.9 us: own_pass(): pl.pallas_call(own_body, out_shape=(act, act, act, jax.ShapeDtypeStruct((...]
    unnamed x24 -> x50, local copies, waits for them, and re-layouts: 2.62 us -> 48.4 us
    convert_element_type x4 -> x2, other arithmetic: 34.8 us -> 0.19 us  [the longest x1 0.12 us: local(): chip = chip.astype(BF16).reshape(slices // 2, rows, 2 * width)]
    another operation x3 -> x0, local copies, waits for them, and re-layouts: 26 us -> none
    ppermute x0 -> x15, waiting for transfers between devices: none -> 22.8 us  [exchange(): return lax.ppermute(x, axis, [(i, i ^ flip) for i in range(count)])]
  transfers between devices with their start and end apart: 5 -> 15, of which waited for: 4 -> 6; matrix products, arithmetic and copies ran while one was open for 29% -> 1% of each run, Pallas kernels for 0% -> 22%
where the time goes in v1:
time: 153 us; the launch traced here: 152 us
  Pallas kernels  61.5 us (40%)
  local copies, waits for them, and re-layouts  50.1 us (33%)
  waiting for transfers between devices  22.8 us (15%)
  starting transfers between devices  16.6 us (11%)
    unnamed x50, local copies, waits for them, and re-layouts  48.4 us
    pallas_call x1, Pallas kernels, own_pass(): pl.pallas_call(own_body, out_shape=(act, act, act, jax.ShapeDtypeStruct((...  22.9 us
    ppermute x15, waiting for transfers between devices, exchange(): return lax.ppermute(x, axis, [(i, i ^ flip) for i in range(count)])  22.8 us
    ppermute x15, starting transfers between devices, exchange(): return lax.ppermute(x, axis, [(i, i ^ flip) for i in range(count)])  16.6 us
    pallas_call x1, Pallas kernels, grads(): pl.pallas_call(functools.partial(grads_body, factor, size), out_shape=(ou...  13.9 us
    pallas_call x1, Pallas kernels, rest_pass(): pl.pallas_call(rest_body, out_shape=(act, act, act), in_specs=[pl.BlockSp...  13.8 us
    pallas_call x1, Pallas kernels, densify(): pl.pallas_call(densify_body, out_shape=(VMEM((width, hidden), BF16), VMEM...  10.9 us
  transfers between devices with their start and end apart: 15, of which 6 were waited for; matrix products, arithmetic and copies ran while one was open for 1% of the time, Pallas kernels for 22%

profile of v1, /device:TPU:0, one launch (start us, length us, event | category | flops | bytes accessed | tf_op | source)
XLA Modules:
  0.0 152.2 jit_solution(9727912149863560395)
XLA Ops:
  0.6 0.8 constant_dynamic-update-slice_fusion.1
  1.5 0.9 constant_dynamic-update-slice_fusion
  2.3 3.0 %collective-permute-start = (bf16[8,8192]{1,0:T(8,128)(2,1)S(1)}, bf16[8,8192]{1,0:T(8,128)(2,1)S(1)}, u32[]{:S(2)}, u32[]{:S(2)}) collective-permute-start(bf16[8,8192]{1,0:T(8,128)(2,1)S(1)} %get-tuple-element.42), channel_id=1, source_target_pairs={{0,2},{1,3},{2,0},{3,1},{4,6},{5,7},{6,4},{7,5},{8,10},{9,11},{10,... | collective-permute-start | bytes 393224 | tf_op jit(solution)/shard_map/ppermute | solution.py:36
  5.3 1.5 collective-permute-start.1
  6.9 2.0 %collective-permute-start.8 = (bf16[8,8192]{1,0:T(8,128)(2,1)S(1)}, bf16[8,8192]{1,0:T(8,128)(2,1)S(1)}, u32[]{:S(2)}, u32[]{:S(2)}) collective-permute-start(bf16[8,8192]{1,0:T(8,128)(2,1)S(1)} %get-tuple-element.42), channel_id=1, source_target_pairs={{0,8},{8,0},{16,24},{24,16},{1,9},{9,1},{17,25},{25,17},{2,10},{10... | collective-permute-start | bytes 393224 | tf_op jit(solution)/shard_map/ppermute | solution.py:36
  8.9 2.6 %collective-permute-start.9 = (bf16[8,8192]{1,0:T(8,128)(2,1)S(1)}, bf16[8,8192]{1,0:T(8,128)(2,1)S(1)}, u32[]{:S(2)}, u32[]{:S(2)}) collective-permute-start(bf16[8,8192]{1,0:T(8,128)(2,1)S(1)} %get-tuple-element.42), channel_id=1, source_target_pairs={{0,16},{8,24},{16,0},{24,8},{1,17},{9,25},{17,1},{25,9},{2,18},{10... | collective-permute-start | bytes 393224 | tf_op jit(solution)/shard_map/ppermute | solution.py:36
  11.5 0.7 copy-done.12
  12.2 0.7 copy-done.14
  12.9 0.7 copy-done.16
  13.6 10.9 %densify.1 = (bf16[4096,1792]{1,0:T(8,128)(2,1)S(1)}, bf16[4096,1792]{1,0:T(8,128)(2,1)S(1)}, bf16[1792,4096]{1,0:T(8,128)(2,1)S(1)}) custom-call(s32[1,224]{1,0:T(1,128)S(1)} %copy-done.12, s32[1,224]{1,0:T(1,128)S(1)} %copy-done.14, s32[1,224]{1,0:T(1,128)S(1)} %copy-done.16, bf16[224,128,128]{2,1,0:T(8,128)(2,1)} %gb.1, bf16[224,128,128]{2,1,0:T(8,128)(2,1)} %ub.1, ...), custom_call_target="tpu_custom_call" | custom-call | tf_op jit(solution)/shard_map/densify/pallas_call | solution.py:70
  24.5 5.2 %copy-done = bf16[4096,1792]{1,0:T(8,128)(2,1)} copy-done((bf16[4096,1792]{1,0:T(8,128)(2,1)}, bf16[4096,1792]{1,0:T(8,128)(2,1)S(1)}, u32[]{:S(2)}) %copy-start) | copy-done | bytes 14680088
  29.7 5.2 %copy-done.3 = bf16[4096,1792]{1,0:T(8,128)(2,1)} copy-done((bf16[4096,1792]{1,0:T(8,128)(2,1)}, bf16[4096,1792]{1,0:T(8,128)(2,1)S(1)}, u32[]{:S(2)}) %copy-start.3) | copy-done | bytes 14680088
  35.3 6.8 %collective-permute-done.10 = bf16[8,8192]{1,0:T(8,128)(2,1)S(1)} collective-permute-done((bf16[8,8192]{1,0:T(8,128)(2,1)S(1)}, bf16[8,8192]{1,0:T(8,128)(2,1)S(1)}, u32[]{:S(2)}, u32[]{:S(2)}) %collective-permute-start.10) | collective-permute-done | bytes 131104 | tf_op jit(solution)/shard_map/ppermute | solution.py:36
  42.1 1.6 %collective-permute-start.11 = (bf16[24,8192]{1,0:T(8,128)(2,1)S(1)}, bf16[24,8192]{1,0:T(8,128)(2,1)S(1)}, u32[]{:S(2)}, u32[]{:S(2)}) collective-permute-start(bf16[24,8192]{1,0:T(8,128)(2,1)S(1)} %get-tuple-element.34), channel_id=1, source_target_pairs={{0,2},{1,3},{2,0},{3,1},{4,6},{5,7},{6,4},{7,5},{8,10},{9,11},{10,... | collective-permute-start | bytes 1179656 | tf_op jit(solution)/shard_map/ppermute | solution.py:36
  43.7 1.5 collective-permute-start.12
  45.9 8.4 %collective-permute-done.11 = bf16[24,8192]{1,0:T(8,128)(2,1)S(1)} collective-permute-done((bf16[24,8192]{1,0:T(8,128)(2,1)S(1)}, bf16[24,8192]{1,0:T(8,128)(2,1)S(1)}, u32[]{:S(2)}, u32[]{:S(2)}) %collective-permute-start.11) | collective-permute-done | bytes 393248 | tf_op jit(solution)/shard_map/ppermute | solution.py:36
  54.3 5.2 %copy-done.1 = bf16[4096,1792]{1,0:T(8,128)(2,1)S(1)} copy-done((bf16[4096,1792]{1,0:T(8,128)(2,1)S(1)}, bf16[4096,1792]{1,0:T(8,128)(2,1)}, u32[]{:S(2)}) %copy-start.1) | copy-done | bytes 14680088
  59.5 5.2 %copy-done.4 = bf16[4096,1792]{1,0:T(8,128)(2,1)S(1)} copy-done((bf16[4096,1792]{1,0:T(8,128)(2,1)S(1)}, bf16[4096,1792]{1,0:T(8,128)(2,1)}, u32[]{:S(2)}) %copy-start.4) | copy-done | bytes 14680088
  64.7 22.9 %own_pass.1 = (bf16[64,1792]{1,0:T(8,128)(2,1)S(1)}, bf16[64,1792]{1,0:T(8,128)(2,1)S(1)}, bf16[64,1792]{1,0:T(8,128)(2,1)S(1)}, bf16[64,8192]{1,0:T(8,128)(2,1)S(1)}) custom-call(bf16[64,8192]{1,0:T(8,128)(2,1)S(1)} %constant_dynamic-update-slice_fusion.2.x.own, bf16[4096,1792]{1,0:T(8,128)(2,1)S(1)} %copy-done.1, bf16[4096,1792]{1,0:T(8,128)(2,1)S(1)} %copy-done.4, ...), custom_call_target="tpu_custom_call" | custom-call | flops 5637144576 | bytes 1048576 | tf_op jit(solution)/shard_map/own_pass/pallas_call | solution.py:128
  87.6 5.2 %copy-done.6 = bf16[1792,4096]{1,0:T(8,128)(2,1)} copy-done((bf16[1792,4096]{1,0:T(8,128)(2,1)}, bf16[1792,4096]{1,0:T(8,128)(2,1)S(1)}, u32[]{:S(2)}) %copy-start.6) | copy-done | bytes 14680088
  93.0 1.9 %collective-permute-done.4 = bf16[32,8192]{1,0:T(8,128)(2,1)S(1)} collective-permute-done((bf16[32,8192]{1,0:T(8,128)(2,1)S(1)}, bf16[32,8192]{1,0:T(8,128)(2,1)S(1)}, u32[]{:S(2)}, u32[]{:S(2)}) %collective-permute-start.4) | collective-permute-done | bytes 524320 | tf_op jit(solution)/shard_map/ppermute | solution.py:36
  95.0 2.5 %collective-permute-start.7 = (bf16[8,8192]{1,0:T(8,128)(2,1)S(1)}, bf16[8,8192]{1,0:T(8,128)(2,1)S(1)}, u32[]{:S(2)}, u32[]{:S(2)}) collective-permute-start(bf16[8,8192]{1,0:T(8,128)(2,1)S(1)} %get-tuple-element.32), channel_id=1, source_target_pairs={{0,6},{1,7},{2,4},{3,5},{4,2},{5,3},{6,0},{7,1},{8,14},{9,15},{10,... | collective-permute-start | bytes 393224 | tf_op jit(solution)/shard_map/ppermute | solution.py:36
  98.6 3.1 %collective-permute-done.7 = bf16[8,8192]{1,0:T(8,128)(2,1)S(1)} collective-permute-done((bf16[8,8192]{1,0:T(8,128)(2,1)S(1)}, bf16[8,8192]{1,0:T(8,128)(2,1)S(1)}, u32[]{:S(2)}, u32[]{:S(2)}) %collective-permute-start.7) | collective-permute-done | bytes 131104 | tf_op jit(solution)/shard_map/ppermute | solution.py:36
  101.8 2.5 %collective-permute-done.6 = bf16[8,8192]{1,0:T(8,128)(2,1)S(1)} collective-permute-done((bf16[8,8192]{1,0:T(8,128)(2,1)S(1)}, bf16[8,8192]{1,0:T(8,128)(2,1)S(1)}, u32[]{:S(2)}, u32[]{:S(2)}) %collective-permute-start.6) | collective-permute-done | bytes 131104 | tf_op jit(solution)/shard_map/ppermute | solution.py:36
  105.1 1.1 copy-done.10
  106.2 5.2 %copy-done.2 = bf16[4096,1792]{1,0:T(8,128)(2,1)S(1)} copy-done((bf16[4096,1792]{1,0:T(8,128)(2,1)S(1)}, bf16[4096,1792]{1,0:T(8,128)(2,1)}, u32[]{:S(2)}) %copy-start.2) | copy-done | bytes 14680088
  111.4 5.2 %copy-done.5 = bf16[4096,1792]{1,0:T(8,128)(2,1)S(1)} copy-done((bf16[4096,1792]{1,0:T(8,128)(2,1)S(1)}, bf16[4096,1792]{1,0:T(8,128)(2,1)}, u32[]{:S(2)}) %copy-start.5) | copy-done | bytes 14680088
  116.6 5.2 %copy-done.7 = bf16[1792,4096]{1,0:T(8,128)(2,1)S(1)} copy-done((bf16[1792,4096]{1,0:T(8,128)(2,1)S(1)}, bf16[1792,4096]{1,0:T(8,128)(2,1)}, u32[]{:S(2)}) %copy-start.7) | copy-done | bytes 14680088
  121.8 13.8 %rest_pass.1 = (bf16[192,1792]{1,0:T(8,128)(2,1)S(1)}, bf16[192,1792]{1,0:T(8,128)(2,1)S(1)}, bf16[192,1792]{1,0:T(8,128)(2,1)S(1)}) custom-call(bf16[96,8192]{1,0:T(8,128)(2,1)} %copy-done.8, bf16[96,8192]{1,0:T(8,128)(2,1)} %copy-done.10, bf16[4096,1792]{1,0:T(8,128)(2,1)S(1)} %copy-done.2, bf16[4096,1792]{1,0:T(8,128)(2,1)S(1)} %copy-done.5, ...), custom_call_target="tpu_custom_call" | custom-call | flops 8455716864 | bytes 1048576 | tf_op jit(solution)/shard_map/rest_pass/pallas_call | solution.py:159
  135.5 1.4 copy-done.9
  136.9 1.4 copy-done.11
  138.4 13.9 %grads.1 = (f32[70,128,128]{2,1,0:T(8,128)}, f32[70,128,128]{2,1,0:T(8,128)}, f32[70,128,128]{2,1,0:T(8,128)}) custom-call(s32[3,70]{1,0:T(4,128)S(1)} %broadcast_add_fusion.spots, bf16[64,8192]{1,0:T(8,128)(2,1)S(1)} %constant_dynamic-update-slice_fusion.2.x.own, bf16[96,8192]{1,0:T(8,128)(2,1)S(1)} %copy-done.9, bf16[96,8192]{1,0:T(8,128)(2,1)S(1)} %copy-done.11, ...), custom_call_target="tpu_custom_call" | custom-call | flops 1761607680 | bytes 13762560 | tf_op jit(solution)/shard_map/grads/pallas_call | solution.py:254
  (66 shorter events, 3.4 us)
Async XLA Ops:
  2.3 42.9 %collective-permute-start = (bf16[8,8192]{1,0:T(8,128)(2,1)S(1)}, bf16[8,8192]{1,0:T(8,128)(2,1)S(1)}, u32[]{:S(2)}, u32[]{:S(2)}) collective-permute-start(bf16[8,8192]{1,0:T(8,128)(2,1)S(1)} %get-tuple-element.42), channel_id=1, source_target_pairs={{0,2},{1,3},{2,0},{3,1},{4,6},{5,7},{6,4},{7,5},{8,10},{9,11},{10,... | collective-permute-start | bytes 393224 | tf_op jit(solution)/shard_map/ppermute | solution.py:36
  5.3 40.3 %collective-permute-start.1 = (bf16[8,8192]{1,0:T(8,128)(2,1)S(1)}, bf16[8,8192]{1,0:T(8,128)(2,1)S(1)}, u32[]{:S(2)}, u32[]{:S(2)}) collective-permute-start(bf16[8,8192]{1,0:T(8,128)(2,1)S(1)} %get-tuple-element.42), channel_id=1, source_target_pairs={{0,4},{1,5},{2,6},{3,7},{4,0},{5,1},{6,2},{7,3},{8,12},{9,13},{10,... | collective-permute-start | bytes 393224 | tf_op jit(solution)/shard_map/ppermute | solution.py:36
  6.9 38.8 %collective-permute-start.2 = (bf16[8,8192]{1,0:T(8,128)(2,1)S(1)}, bf16[8,8192]{1,0:T(8,128)(2,1)S(1)}, u32[]{:S(2)}, u32[]{:S(2)}) collective-permute-start(bf16[8,8192]{1,0:T(8,128)(2,1)S(1)} %get-tuple-element.42), channel_id=1, source_target_pairs={{0,6},{1,7},{2,4},{3,5},{4,2},{5,3},{6,0},{7,1},{8,14},{9,15},{10,... | collective-permute-start | bytes 393224 | tf_op jit(solution)/shard_map/ppermute | solution.py:36
  6.9 28.3 %collective-permute-start.8 = (bf16[8,8192]{1,0:T(8,128)(2,1)S(1)}, bf16[8,8192]{1,0:T(8,128)(2,1)S(1)}, u32[]{:S(2)}, u32[]{:S(2)}) collective-permute-start(bf16[8,8192]{1,0:T(8,128)(2,1)S(1)} %get-tuple-element.42), channel_id=1, source_target_pairs={{0,8},{8,0},{16,24},{24,16},{1,9},{9,1},{17,25},{25,17},{2,10},{10... | collective-permute-start | bytes 393224 | tf_op jit(solution)/shard_map/ppermute | solution.py:36
  8.9 26.3 %collective-permute-start.9 = (bf16[8,8192]{1,0:T(8,128)(2,1)S(1)}, bf16[8,8192]{1,0:T(8,128)(2,1)S(1)}, u32[]{:S(2)}, u32[]{:S(2)}) collective-permute-start(bf16[8,8192]{1,0:T(8,128)(2,1)S(1)} %get-tuple-element.42), channel_id=1, source_target_pairs={{0,16},{8,24},{16,0},{24,8},{1,17},{9,25},{17,1},{25,9},{2,18},{10... | collective-permute-start | bytes 393224 | tf_op jit(solution)/shard_map/ppermute | solution.py:36
  13.5 21.3 %copy-start.13 = (s32[1,224]{1,0:T(1,128)S(1)}, s32[1,224]{1,0:T(1,128)}, u32[]{:S(2)}) copy-start(s32[1,224]{1,0:T(1,128)} %gi.1) | copy-start | bytes 2692
  13.6 21.3 %copy-start.15 = (s32[1,224]{1,0:T(1,128)S(1)}, s32[1,224]{1,0:T(1,128)}, u32[]{:S(2)}) copy-start(s32[1,224]{1,0:T(1,128)} %ui.1) | copy-start | bytes 2692
  13.6 21.3 %copy-start.17 = (s32[1,224]{1,0:T(1,128)S(1)}, s32[1,224]{1,0:T(1,128)}, u32[]{:S(2)}) copy-start(s32[1,224]{1,0:T(1,128)} %di.1) | copy-start | bytes 2692
  13.6 21.3 %copy-start.18 = (s32[1,224]{1,0:T(1,128)S(1)}, s32[1,224]{1,0:T(1,128)}, u32[]{:S(2)}) copy-start(s32[1,224]{1,0:T(1,128)} %param.21) | copy-start | bytes 2692
  13.6 21.3 %copy-start.19 = (s32[1,224]{1,0:T(1,128)S(1)}, s32[1,224]{1,0:T(1,128)}, u32[]{:S(2)}) copy-start(s32[1,224]{1,0:T(1,128)} %param.20) | copy-start | bytes 2692
  13.6 21.3 %copy-start.20 = (s32[1,224]{1,0:T(1,128)S(1)}, s32[1,224]{1,0:T(1,128)}, u32[]{:S(2)}) copy-start(s32[1,224]{1,0:T(1,128)} %param.19) | copy-start | bytes 2692
  24.5 5.2 %copy-start = (bf16[4096,1792]{1,0:T(8,128)(2,1)}, bf16[4096,1792]{1,0:T(8,128)(2,1)S(1)}, u32[]{:S(2)}) copy-start(bf16[4096,1792]{1,0:T(8,128)(2,1)S(1)} %get-tuple-element.18.wg) | copy-start | bytes 44040196
  29.7 5.2 %copy-start.3 = (bf16[4096,1792]{1,0:T(8,128)(2,1)}, bf16[4096,1792]{1,0:T(8,128)(2,1)S(1)}, u32[]{:S(2)}) copy-start(bf16[4096,1792]{1,0:T(8,128)(2,1)S(1)} %get-tuple-element.19.wu) | copy-start | bytes 44040196
  35.2 6.9 %collective-permute-start.10 = (bf16[8,8192]{1,0:T(8,128)(2,1)S(1)}, bf16[8,8192]{1,0:T(8,128)(2,1)S(1)}, u32[]{:S(2)}, u32[]{:S(2)}) collective-permute-start(bf16[8,8192]{1,0:T(8,128)(2,1)S(1)} %get-tuple-element.42), channel_id=1, source_target_pairs={{0,24},{8,16},{16,8},{24,0},{1,25},{9,17},{17,9},{25,1},{2,26},{10... | collective-permute-start | bytes 393224 | tf_op jit(solution)/shard_map/ppermute | solution.py:36
  42.1 12.1 %collective-permute-start.11 = (bf16[24,8192]{1,0:T(8,128)(2,1)S(1)}, bf16[24,8192]{1,0:T(8,128)(2,1)S(1)}, u32[]{:S(2)}, u32[]{:S(2)}) collective-permute-start(bf16[24,8192]{1,0:T(8,128)(2,1)S(1)} %get-tuple-element.34), channel_id=1, source_target_pairs={{0,2},{1,3},{2,0},{3,1},{4,6},{5,7},{6,4},{7,5},{8,10},{9,11},{10,... | collective-permute-start | bytes 1179656 | tf_op jit(solution)/shard_map/ppermute | solution.py:36
  43.7 49.2 %collective-permute-start.12 = (bf16[24,8192]{1,0:T(8,128)(2,1)S(1)}, bf16[24,8192]{1,0:T(8,128)(2,1)S(1)}, u32[]{:S(2)}, u32[]{:S(2)}) collective-permute-start(bf16[24,8192]{1,0:T(8,128)(2,1)S(1)} %get-tuple-element.34), channel_id=1, source_target_pairs={{0,4},{1,5},{2,6},{3,7},{4,0},{5,1},{6,2},{7,3},{8,12},{9,13},{10,... | collective-permute-start | bytes 1179656 | tf_op jit(solution)/shard_map/ppermute | solution.py:36
  45.2 53.3 %collective-permute-start.13 = (bf16[24,8192]{1,0:T(8,128)(2,1)S(1)}, bf16[24,8192]{1,0:T(8,128)(2,1)S(1)}, u32[]{:S(2)}, u32[]{:S(2)}) collective-permute-start(bf16[24,8192]{1,0:T(8,128)(2,1)S(1)} %get-tuple-element.34), channel_id=1, source_target_pairs={{0,6},{1,7},{2,4},{3,5},{4,2},{5,3},{6,0},{7,1},{8,14},{9,15},{10,... | collective-permute-start | bytes 1179656 | tf_op jit(solution)/shard_map/ppermute | solution.py:36
  45.7 8.5 %collective-permute-start.3 = (bf16[32,8192]{1,0:T(8,128)(2,1)S(1)}, bf16[32,8192]{1,0:T(8,128)(2,1)S(1)}, u32[]{:S(2)}, u32[]{:S(2)}) collective-permute-start(bf16[32,8192]{1,0:T(8,128)(2,1)S(1)} %pad_maximum_fusion), channel_id=1, source_target_pairs={{0,1},{1,0},{2,3},{3,2},{4,5},{5,4},{6,7},{7,6},{8,9},{9,8},{10,11... | collective-permute-start | bytes 1572872 | tf_op jit(solution)/shard_map/ppermute | solution.py:36
  54.3 5.2 %copy-start.1 = (bf16[4096,1792]{1,0:T(8,128)(2,1)S(1)}, bf16[4096,1792]{1,0:T(8,128)(2,1)}, u32[]{:S(2)}) copy-start(bf16[4096,1792]{1,0:T(8,128)(2,1)} %copy-done) | copy-start | bytes 44040196
  59.5 5.2 %copy-start.4 = (bf16[4096,1792]{1,0:T(8,128)(2,1)S(1)}, bf16[4096,1792]{1,0:T(8,128)(2,1)}, u32[]{:S(2)}) copy-start(bf16[4096,1792]{1,0:T(8,128)(2,1)} %copy-done.3) | copy-start | bytes 44040196
  87.6 5.2 %copy-start.6 = (bf16[1792,4096]{1,0:T(8,128)(2,1)}, bf16[1792,4096]{1,0:T(8,128)(2,1)S(1)}, u32[]{:S(2)}) copy-start(bf16[1792,4096]{1,0:T(8,128)(2,1)S(1)} %get-tuple-element.20.wd) | copy-start | bytes 44040196
  92.8 2.0 %collective-permute-start.4 = (bf16[32,8192]{1,0:T(8,128)(2,1)S(1)}, bf16[32,8192]{1,0:T(8,128)(2,1)S(1)}, u32[]{:S(2)}, u32[]{:S(2)}) collective-permute-start(bf16[32,8192]{1,0:T(8,128)(2,1)S(1)} %slice.29), channel_id=1, source_target_pairs={{0,1},{1,0},{2,3},{3,2},{4,5},{5,4},{6,7},{7,6},{8,9},{9,8},{10,11... | collective-permute-start | bytes 1572872 | tf_op jit(solution)/shard_map/ppermute | solution.py:36
  95.0 6.8 %collective-permute-start.7 = (bf16[8,8192]{1,0:T(8,128)(2,1)S(1)}, bf16[8,8192]{1,0:T(8,128)(2,1)S(1)}, u32[]{:S(2)}, u32[]{:S(2)}) collective-permute-start(bf16[8,8192]{1,0:T(8,128)(2,1)S(1)} %get-tuple-element.32), channel_id=1, source_target_pairs={{0,6},{1,7},{2,4},{3,5},{4,2},{5,3},{6,0},{7,1},{8,14},{9,15},{10,... | collective-permute-start | bytes 393224 | tf_op jit(solution)/shard_map/ppermute | solution.py:36
  97.5 6.8 %collective-permute-start.6 = (bf16[8,8192]{1,0:T(8,128)(2,1)S(1)}, bf16[8,8192]{1,0:T(8,128)(2,1)S(1)}, u32[]{:S(2)}, u32[]{:S(2)}) collective-permute-start(bf16[8,8192]{1,0:T(8,128)(2,1)S(1)} %get-tuple-element.33), channel_id=1, source_target_pairs={{0,4},{1,5},{2,6},{3,7},{4,0},{5,1},{6,2},{7,3},{8,12},{9,13},{10,... | collective-permute-start | bytes 393224 | tf_op jit(solution)/shard_map/ppermute | solution.py:36
  98.0 6.4 %collective-permute-start.5 = (bf16[8,8192]{1,0:T(8,128)(2,1)S(1)}, bf16[8,8192]{1,0:T(8,128)(2,1)S(1)}, u32[]{:S(2)}, u32[]{:S(2)}) collective-permute-start(bf16[8,8192]{1,0:T(8,128)(2,1)S(1)} %get-tuple-element.31), channel_id=1, source_target_pairs={{0,2},{1,3},{2,0},{3,1},{4,6},{5,7},{6,4},{7,5},{8,10},{9,11},{10,... | collective-permute-start | bytes 393224 | tf_op jit(solution)/shard_map/ppermute | solution.py:36
  98.6 6.5 %copy-start.8 = (bf16[96,8192]{1,0:T(8,128)(2,1)}, bf16[96,8192]{1,0:T(8,128)(2,1)S(1)}, u32[]{:S(2)}) copy-start(bf16[96,8192]{1,0:T(8,128)(2,1)S(1)} %constant_dynamic-update-slice_fusion.11.xa) | copy-start | bytes 4718596
  98.6 6.5 %collective-permute-start.14 = (bf16[96,8192]{1,0:T(8,128)(2,1)S(1)}, bf16[96,8192]{1,0:T(8,128)(2,1)S(1)}, u32[]{:S(2)}, u32[]{:S(2)}) collective-permute-start(bf16[96,8192]{1,0:T(8,128)(2,1)S(1)} %constant_dynamic-update-slice_fusion.11.xa), channel_id=1, source_target_pairs={{0,1},{1,0},{2,3},{3,2},{4,5},{5,4},{6,7},{7,6},{8,9},{9,8},{10,11... | collective-permute-start | bytes 4718600 | tf_op jit(solution)/shard_map/ppermute | solution.py:36
  106.2 5.2 %copy-start.2 = (bf16[4096,1792]{1,0:T(8,128)(2,1)S(1)}, bf16[4096,1792]{1,0:T(8,128)(2,1)}, u32[]{:S(2)}) copy-start(bf16[4096,1792]{1,0:T(8,128)(2,1)} %copy-done) | copy-start | bytes 44040196
  111.4 5.2 %copy-start.5 = (bf16[4096,1792]{1,0:T(8,128)(2,1)S(1)}, bf16[4096,1792]{1,0:T(8,128)(2,1)}, u32[]{:S(2)}) copy-start(bf16[4096,1792]{1,0:T(8,128)(2,1)} %copy-done.3) | copy-start | bytes 44040196
  116.6 5.2 %copy-start.7 = (bf16[1792,4096]{1,0:T(8,128)(2,1)S(1)}, bf16[1792,4096]{1,0:T(8,128)(2,1)}, u32[]{:S(2)}) copy-start(bf16[1792,4096]{1,0:T(8,128)(2,1)} %copy-done.6) | copy-start | bytes 44040196
  135.5 1.4 copy-start.9
  136.9 1.4 copy-start.11
  (4 other events, 3.2 us)

commit v2 on v0

v2 whole, which is shorter than its diff:
```python
import functools
import math

import jax
import jax.numpy as jnp
from jax import lax
from jax.experimental import pallas as pl
from jax.experimental.pallas import tpu as pltpu
from jax.sharding import PartitionSpec as P

FF = 14336
BF16 = jnp.bfloat16
F32 = jnp.float32
VMEM = pltpu.VMEM
SMEM = pltpu.SMEM


SMEM_SPEC = pl.BlockSpec(memory_space=SMEM)
HBM_SPEC = pl.BlockSpec(memory_space=pltpu.HBM)
ANY_SPEC = pl.BlockSpec(memory_space=pl.ANY)
FREE = pl.CostEstimate(flops=0, bytes_accessed=0, transcendentals=0)
LIMIT = pltpu.CompilerParams(vmem_limit_bytes=4 * 2**20)


def in_vmem():
    return pl.BlockSpec(memory_space=VMEM)


def pinned(*arrays):
    return [pltpu.with_memory_space_constraint(x, VMEM) for x in arrays]


def in_hbm(x):
    return pltpu.with_memory_space_constraint(x, pltpu.HBM)


def dot_nn(a, b):
    return lax.dot_general(a, b, (((1,), (0,)), ((), ())), preferred_element_type=F32)


def dot_nt(a, b):
    return lax.dot_general(a, b, (((1,), (1,)), ((), ())), preferred_element_type=F32)


def exchange(x, axis, flip):
    count = lax.axis_size(axis)
    return lax.ppermute(x, axis, [(i, i ^ flip) for i in range(count)])


def assemble(pieces, out):
    chunk = 1024

    def step(n, carry):
        cols = pl.ds(pl.multiple_of(n * chunk, chunk), chunk)
        parts = [x[:, cols].astype(F32) for x in pieces]
        out[:, cols] = jnp.concatenate(parts, axis=0).astype(BF16)
        return carry

    lax.fori_loop(0, out.shape[1] // chunk, step, 0)


def pack(pieces, wait_for=()):
    rows = sum(x.shape[0] for x in pieces)
    width = pieces[0].shape[1]

    def body(*refs):
        assemble(refs[: len(pieces)], refs[-1])

    return pl.pallas_call(
        body,
        out_shape=jax.ShapeDtypeStruct((rows, width), BF16),
        in_specs=[in_vmem()] * len(pieces) + [ANY_SPEC] * len(wait_for),
        out_specs=in_vmem(),
        compiler_params=LIMIT,
        cost_estimate=FREE,
        name="pack",
    )(*pieces, *wait_for)


def side_by_side(left, right):
    rows, width = left.shape

    def body(left_ref, right_ref, out, sem):
        copies = [
            pltpu.make_async_copy(left_ref, out.at[:, pl.ds(0, width)], sem.at[0]),
            pltpu.make_async_copy(right_ref, out.at[:, pl.ds(width, width)], sem.at[1]),
        ]
        for copy in copies:
            copy.start()
        for copy in copies:
            copy.wait()

    return pl.pallas_call(
        body,
        out_shape=jax.ShapeDtypeStruct((rows, 2 * width), BF16),
        in_specs=[HBM_SPEC] * 2,
        out_specs=in_vmem(),
        scratch_shapes=[pltpu.SemaphoreType.DMA((2,))],
        compiler_params=LIMIT,
        name="side_by_side",
    )(in_hbm(left), in_hbm(right))


def add_and_cut(parts, sent, pieces):
    rows, width = sent[0].shape
    height = rows // pieces
    count = len(parts)

    def body(*refs):
        outs = refs[2 * count :]
        chunk = 1024
        for m in range(count):

            def step(n, carry):
                cols = pl.ds(pl.multiple_of(n * chunk, chunk), chunk)
                there = pl.ds(pl.multiple_of(m * width + n * chunk, chunk), chunk)
                total = refs[m][:, cols].astype(F32) + refs[count + m][:, cols].astype(F32)
                for i, out in enumerate(outs):
                    out[:, there] = total[i * height : (i + 1) * height].astype(BF16)
                return carry

            lax.fori_loop(0, width // chunk, step, 0)

    out = (jax.ShapeDtypeStruct((height, count * width), BF16),) * pieces
    return pl.pallas_call(
        body,
        out_shape=out,
        in_specs=[in_vmem()] * (2 * count),
        out_specs=(in_vmem(),) * pieces,
        compiler_params=LIMIT,
        cost_estimate=FREE,
        name="add_and_cut",
    )(*parts, *sent)


def scatter(index, blocks, dense, sem, other=None):
    kept, size = blocks.shape[0], blocks.shape[1]
    cols = dense.shape[1] // size
    unroll = 8 if kept % 8 == 0 else 1
    scale = 2**16 // cols + 1
    steps = kept // unroll
    rows = 0 if other is None else other.shape[0] // steps // 16 * 16

    def step(i, carry):
        for u in range(unroll):
            k = i * unroll + u
            b = index[0, k]
            r = lax.shift_right_logical(b * scale, 16)
            c = b - r * cols
            r, c = pl.multiple_of(r * size, size), pl.multiple_of(c * size, size)
            pltpu.make_async_copy(
                blocks.at[k], dense.at[pl.ds(r, size), pl.ds(c, size)], sem
            ).start()
        if rows:
            part = pl.ds(pl.multiple_of(i * rows, rows), rows)
            other[part] = jnp.zeros((rows, other.shape[1]), BF16)
        return carry

    lax.fori_loop(0, steps, step, 0)
    if other is not None and other.shape[0] > steps * rows:
        left = other.shape[0] - steps * rows
        other[pl.ds(steps * rows, left)] = jnp.zeros((left, other.shape[1]), BF16)


def dense_gate_body(index, blocks, *refs):
    wg, sem = refs[-2:]
    wg[...] = jnp.zeros_like(wg)
    scatter(index, blocks, wg, sem)
    pltpu.make_async_copy(blocks, blocks, sem).wait()


def dense_both_body(ui, di, ub, db, wu, wd, stage, sem):
    stage[...] = jnp.zeros_like(stage)
    scatter(di, db, stage, sem.at[0], wu)
    scatter(ui, ub, wu, sem.at[2])
    pltpu.make_async_copy(db, db, sem.at[0]).wait()
    pltpu.make_async_copy(stage, wd, sem.at[1]).start()
    pltpu.make_async_copy(ub, ub, sem.at[2]).wait()
    pltpu.make_async_copy(stage, wd, sem.at[1]).wait()


def dense_gate(index, blocks, width, hidden, wait_for):
    return pl.pallas_call(
        dense_gate_body,
        out_shape=VMEM((width, hidden), BF16),
        in_specs=[SMEM_SPEC, HBM_SPEC] + [ANY_SPEC] * len(wait_for),
        out_specs=in_vmem(),
        scratch_shapes=[pltpu.SemaphoreType.DMA],
        compiler_params=pltpu.CompilerParams(vmem_limit_bytes=2**20),
        cost_estimate=FREE,
        name="dense_gate",
    )(index, in_hbm(blocks), *wait_for)


def dense_both(up_index, down_index, up_blocks, down_blocks, width, hidden):
    return pl.pallas_call(
        dense_both_body,
        out_shape=(VMEM((width, hidden), BF16), pltpu.HBM((hidden, width), BF16)),
        in_specs=[SMEM_SPEC] * 2 + [HBM_SPEC] * 2,
        out_specs=(in_vmem(), HBM_SPEC),
        scratch_shapes=[VMEM((hidden, width), BF16), pltpu.SemaphoreType.DMA((3,))],
        compiler_params=pltpu.CompilerParams(vmem_limit_bytes=2 * hidden * width + 2**20),
        cost_estimate=FREE,
        name="dense_both",
    )(up_index, down_index, in_hbm(up_blocks), in_hbm(down_blocks))


def chunk_of(hidden):
    return 256 if hidden % 256 == 0 else 128


def activations(tok, cot, wg, wu, wd):
    g = dot_nn(tok[...], wg)
    u = dot_nn(tok[...], wu)
    h = dot_nt(cot[...], wd)
    s = jax.nn.sigmoid(g)
    hid = (g * s * u).astype(BF16)
    gp = (h * u * s * (1.0 + g * (1.0 - s))).astype(BF16)
    up = (h * g * s).astype(BF16)
    return hid, gp, up


def acts_body(count, *refs):
    pieces, (wg, wu, wd), (hid, gp, up, x) = refs[:count], refs[count : count + 3], refs[-4:]
    n = pl.program_id(0)
    width, chunk = wg.shape[0], wd.shape[0]

    @pl.when(n == 0)
    def _():
        assemble(pieces, x)

    cols = pl.ds(pl.multiple_of(n * chunk, chunk), chunk)
    tok, cot = x.at[:, pl.ds(0, width)], x.at[:, pl.ds(width, width)]
    hid[...], gp[...], up[...] = activations(tok, cot, wg[:, cols], wu[:, cols], wd[...])


def acts_pass(pieces, wg, wu, wd, name, wait_for=()):
    rows = sum(x.shape[0] for x in pieces)
    width, hidden = wg.shape
    chunk = chunk_of(hidden)
    act = jax.ShapeDtypeStruct((rows, hidden), BF16)
    piece = pl.BlockSpec((rows, chunk), lambda n: (0, n))
    need = 84 * rows * chunk + 4 * chunk * width
    return pl.pallas_call(
        functools.partial(acts_body, len(pieces)),
        out_shape=(act, act, act, VMEM((rows, 2 * width), BF16)),
        grid=(hidden // chunk,),
        in_specs=[in_vmem()] * (len(pieces) + 2)
        + [pl.BlockSpec((chunk, width), lambda n: (n, 0))]
        + [ANY_SPEC] * len(wait_for),
        out_specs=(piece, piece, piece, in_vmem()),
        compiler_params=pltpu.CompilerParams(vmem_limit_bytes=max(need, 8 * 2**20)),
        cost_estimate=pl.CostEstimate(
            flops=6 * rows * width * hidden, bytes_accessed=2 * width * hidden, transcendentals=0
        ),
        name=name,
    )(*pieces, *pinned(wg, wu), in_hbm(wd), *wait_for)


def own_out_body(hid, gp, up, wg, wu, wd, part, back):
    n = pl.program_id(0)
    chunk = wd.shape[1]
    width = wg.shape[0]
    half = part.shape[0]
    out = pl.ds(pl.multiple_of(n * chunk, chunk), chunk)
    later = pl.ds(pl.multiple_of(width + n * chunk, chunk), chunk)
    left = dot_nn(hid[...], wd[...]).astype(BF16)
    right = (dot_nt(gp[...], wg[out, :]) + dot_nt(up[...], wu[out, :])).astype(BF16)
    part[:, out] = left[:half]
    back[:, out] = left[half:]
    part[:, later] = right[:half]
    back[:, later] = right[half:]


def own_out(hid, gp, up, wg, wu, wd):
    rows = hid.shape[0]
    width, hidden = wg.shape
    chunk = 512
    return pl.pallas_call(
        own_out_body,
        out_shape=(jax.ShapeDtypeStruct((rows // 2, 2 * width), BF16),) * 2,
        grid=(width // chunk,),
        in_specs=[in_vmem()] * 5 + [pl.BlockSpec((hidden, chunk), lambda n: (0, n))],
        out_specs=(in_vmem(), in_vmem()),
        compiler_params=pltpu.CompilerParams(
            vmem_limit_bytes=max(4 * chunk * hidden + 16 * rows * chunk + 2**21, 7 * 2**20)
        ),
        cost_estimate=pl.CostEstimate(
            flops=6 * rows * width * hidden, bytes_accessed=2 * width * hidden, transcendentals=0
        ),
        name="own_out",
    )(hid, gp, up, *pinned(wg, wu), in_hbm(wd))


def grads_body(
    factor, size, spots, own, rest, hid0, hid1, gp0, gp1, up0, up1,
    gate_out, up_out, down_out, tok_t, hid_t,
):
    i = pl.program_id(0)
    steps = pl.num_programs(0) // 2
    per_step = gate_out.shape[0]
    d_cols = tok_t.shape[0]
    ff_cols = hid_t.shape[0]
    width = d_cols * size

    def column(first, second, start):
        cols = pl.ds(pl.multiple_of(start, size), size)
        return jnp.concatenate([first[:, cols], second[:, cols]], axis=0)

    def one(which, left, first, second, base, out, cols, at, j):
        spot = spots[which, at * per_step + j]
        b = jnp.maximum(spot, 0)
        r = lax.shift_right_logical(b * (2**16 // cols + 1), 16)
        c = b - r * cols
        value = dot_nn(left[r], column(first, second, base + c * size)) * factor
        out[j] = jnp.where(spot >= 0, value, 0.0)

    @pl.when(i == 0)
    def _():
        def step(n, carry):
            hid_t[n] = column(hid0, hid1, n * size).T
            return carry

        lax.fori_loop(0, ff_cols, step, 0)

    @pl.when(i < steps)
    def _():
        turns = -(-d_cols // (spots.shape[1] // per_step))
        for j in range(max(per_step, turns)):
            if j < turns:
                n = jnp.minimum(i * turns + j, d_cols - 1)
                tok_t[n] = column(own, rest, n * size).T
            if j < per_step:
                one(2, hid_t, own, rest, width, down_out, d_cols, i, j)

    @pl.when(i >= steps)
    def _():
        for j in range(per_step):
            one(0, tok_t, gp0, gp1, 0, gate_out, ff_cols, i - steps, j)
            one(1, tok_t, up0, up1, 0, up_out, ff_cols, i - steps, j)


def grads(spots, own, rest, acts0, acts1, size, cap, factor):
    per_step = max(n for n in range(1, 18) if cap % n == 0)
    per_step = 10 if cap % 10 == 0 else per_step
    steps = cap // per_step
    width = own.shape[1] // 2
    hidden = acts0[0].shape[1]
    rows = own.shape[0] + rest.shape[0]
    out = jax.ShapeDtypeStruct((cap, size, size), F32)
    early = pl.BlockSpec((per_step, size, size), lambda i: (jnp.minimum(i, steps - 1), 0, 0))
    late = pl.BlockSpec((per_step, size, size), lambda i: (jnp.maximum(i - steps, 0), 0, 0))
    need = rows * (6 * width + 8 * hidden) + per_step * 6 * size * size * 4
    return pl.pallas_call(
        functools.partial(grads_body, factor, size),
        out_shape=(out, out, out),
        grid=(2 * steps,),
        in_specs=[SMEM_SPEC] + [in_vmem()] * 8,
        out_specs=(late, late, early),
        scratch_shapes=[
            VMEM((width // size, size, rows), BF16),
            VMEM((hidden // size, size, rows), BF16),
        ],
        compiler_params=pltpu.CompilerParams(vmem_limit_bytes=need + 2**21),
        cost_estimate=pl.CostEstimate(
            flops=6 * cap * size * size * rows, bytes_accessed=12 * cap * size * size, transcendentals=0
        ),
        name="grads",
    )(spots, own, rest, acts0[0], acts1[0], acts0[1], acts1[1], acts0[2], acts1[2])


def local(
    tokens,
    out_grad,
    gate_blocks,
    up_blocks,
    down_blocks,
    gate_index,
    up_index,
    down_index,
    gate_slot,
    up_slot,
    down_slot,
):
    rows, width = tokens.shape
    size = gate_blocks.shape[1]
    kept_count = gate_blocks.shape[0]
    groups = lax.axis_size("dp")
    slices = lax.axis_size("tensor")
    hidden = FF // slices
    cap = (kept_count + groups - 1) // groups + kept_count // (4 * groups)
    factor = 1.0 / math.sqrt(rows * slices * groups)

    mine = lax.axis_index("dp") * cap + jnp.arange(cap, dtype=jnp.int32)
    slots = jnp.concatenate([gate_slot, up_slot, down_slot])
    index = jnp.concatenate([gate_index, up_index, down_index])
    hit = slots[:, None, :] == mine[None, :, None]
    spots = jnp.sum(jnp.where(hit, index[:, None, :] + 1, 0), axis=2) - 1

    both = side_by_side(tokens, out_grad)
    chips = range(2, slices, 2)

    def sibling(x):
        return exchange(x, "tensor", 1)

    far = [exchange(both, "dp", a) for a in range(1, groups)]
    near = [exchange(both, "tensor", d) for d in chips]
    wu, wd = dense_both(up_index, down_index, up_blocks, down_blocks, width, hidden)
    own_half = pack([both, *near], [wu])
    others = pack(far, [wu])
    wg = dense_gate(gate_index, gate_blocks, width, hidden, [own_half, others, spots])
    own_pieces = [own_half, sibling(own_half)]
    other_half = [others, *(exchange(others, "tensor", d) for d in chips)]

    *acts0, own = acts_pass(own_pieces, wg, wu, wd, "own_acts")
    part, back = own_out(*acts0, wg, wu, wd)
    chip = add_and_cut([part], [sibling(back)], slices // 2)
    acts1_in = [*other_half, *(sibling(x) for x in other_half)]
    *acts1, rest = acts_pass(acts1_in, wg, wu, wd, "rest_acts", [chip[0]])

    total = chip[0].astype(F32)
    for piece, d in zip(chip[1:], chips):
        total = total + exchange(piece, "tensor", d).astype(F32)
    total = total.astype(BF16)

    gate_out, up_out, down_out = grads(spots, own, rest, acts0, acts1, size, cap, factor)
    return (total[:, :width], total[:, width:], gate_out[None], up_out[None], down_out[None])


def solution(mesh):
    in_specs = (
        P(("dp", "tensor"), None),
        P(("dp", "tensor"), None),
        P("tensor", None, None),
        P("tensor", None, None),
        P("tensor", None, None),
        P("tensor", None),
        P("tensor", None),
        P("tensor", None),
        P("tensor", None),
        P("tensor", None),
        P("tensor", None),
    )
    out_specs = (
        P(("dp", "tensor"), None),
        P(("dp", "tensor"), None),
        P("tensor", "dp", None, None),
        P("tensor", "dp", None, None),
        P("tensor", "dp", None, None),
    )
    return jax.shard_map(local, mesh=mesh, in_specs=in_specs, out_specs=out_specs, check_vma=False)
```

time: 726 us -> 98.2 us (0.14); the launches traced: 716 us -> 97.7 us
  waiting for transfers between devices: 345 us -> 6.71 us
  local copies, waits for them, and re-layouts: 168 us -> 2.55 us
  matrix products: 115 us -> 0 us
  Pallas kernels: 0 us -> 69.7 us
  other arithmetic: 50.8 us -> 0.31 us
  blocking collectives: 21.3 us -> 0 us
  starting transfers between devices: 0.59 us -> 17.6 us
  between operations: 14.3 us -> 0.86 us
    reduce_scatter x5 -> x0, waiting for transfers between devices: 345 us -> none  [the longest x1 156 us: local(): lax.psum_scatter(owner_buffer(down_terms, down_slot[0], slot_total).astyp...]
    scatter x3 -> x0, local copies, waits for them, and re-layouts: 122 us -> none  [owner_buffer(): jnp.zeros((slot_total,) + terms.shape[1:], jnp.float32).at[slots].set(terms)]
    dot_general x15 -> x0, matrix products: 115 us -> none  [the longest x3 33.3 us: block_terms(): jnp.einsum('tkd,tke->kde', picked_left, picked_right, preferred_element_t...]
    pallas_call x0 -> x10, Pallas kernels: none -> 69.7 us  [the longest x2 26.5 us: acts_pass(): pl.pallas_call(functools.partial(acts_body, len(pieces)), out_shape=(act,...]
    convert_element_type x4 -> x1, other arithmetic: 34.8 us -> 0.07 us  [local(): total = total.astype(BF16)]
    another operation x3 -> x0, local copies, waits for them, and re-layouts: 26 us -> none
    all_gather x2 -> x0, blocking collectives: 21.3 us -> none  [the longest x1 11.6 us: local(): gathered = lax.all_gather(tokens, 'tensor', axis=0, tiled=True)]
    ppermute x0 -> x18, starting transfers between devices: none -> 17.6 us  [exchange(): return lax.ppermute(x, axis, [(i, i ^ flip) for i in range(count)])]
  transfers between devices with their start and end apart: 5 -> 18, of which waited for: 4 -> 2; matrix products, arithmetic and copies ran while one was open for 29% -> 0% of each run, Pallas kernels for 0% -> 70%
where the time goes in v2:
time: 98.2 us; the launch traced here: 97.7 us
  Pallas kernels  69.7 us (71%)
  starting transfers between devices  17.6 us (18%)
  waiting for transfers between devices  6.71 us (7%)
  local copies, waits for them, and re-layouts  2.55 us (3%)
    pallas_call x2, Pallas kernels, acts_pass(): pl.pallas_call(functools.partial(acts_body, len(pieces)), out_shape=(act,...  26.5 us
    ppermute x18, starting transfers between devices, exchange(): return lax.ppermute(x, axis, [(i, i ^ flip) for i in range(count)])  17.6 us
    pallas_call x1, Pallas kernels, own_out(): pl.pallas_call(own_out_body, out_shape=(jax.ShapeDtypeStruct((rows // 2,...  13.9 us
    pallas_call x1, Pallas kernels, grads(): pl.pallas_call(functools.partial(grads_body, factor, size), out_shape=(ou...  12.6 us
    pallas_call x1, Pallas kernels, dense_both(): pl.pallas_call(dense_both_body, out_shape=(VMEM((width, hidden), BF16), p...  11 us
    ppermute x18, waiting for transfers between devices, exchange(): return lax.ppermute(x, axis, [(i, i ^ flip) for i in range(count)])  6.71 us
    pallas_call x1, Pallas kernels, dense_gate(): pl.pallas_call(dense_gate_body, out_shape=VMEM((width, hidden), BF16), in...  4.64 us
  transfers between devices with their start and end apart: 18, of which 2 were waited for; matrix products, arithmetic and copies ran while one was open for 0% of the time, Pallas kernels for 70%

profile of v2, /device:TPU:0, one launch (start us, length us, event | category | flops | bytes accessed | tf_op | source)
XLA Modules:
  0.0 97.7 jit_solution(12424676851830983605)
XLA Ops:
  0.6 0.9 side_by_side.1.refs_0_
  1.5 3.0 %collective-permute-start = (bf16[8,8192]{1,0:T(8,128)(2,1)S(1)}, bf16[8,8192]{1,0:T(8,128)(2,1)S(1)}, u32[]{:S(2)}, u32[]{:S(2)}) collective-permute-start(bf16[8,8192]{1,0:T(8,128)(2,1)S(1)} %side_by_side.1.refs_0_), channel_id=1, source_target_pairs={{0,2},{1,3},{2,0},{3,1},{4,6},{5,7},{6,4},{7,5},{8,10},{9,11},{10,... | collective-permute-start | bytes 393224 | tf_op jit(solution)/shard_map/ppermute | solution.py:47
  4.5 1.5 %collective-permute-start.1 = (bf16[8,8192]{1,0:T(8,128)(2,1)S(1)}, bf16[8,8192]{1,0:T(8,128)(2,1)S(1)}, u32[]{:S(2)}, u32[]{:S(2)}) collective-permute-start(bf16[8,8192]{1,0:T(8,128)(2,1)S(1)} %side_by_side.1.refs_0_), channel_id=1, source_target_pairs={{0,4},{1,5},{2,6},{3,7},{4,0},{5,1},{6,2},{7,3},{8,12},{9,13},{10,... | collective-permute-start | bytes 393224 | tf_op jit(solution)/shard_map/ppermute | solution.py:47
  6.1 2.0 %collective-permute-start.4 = (bf16[8,8192]{1,0:T(8,128)(2,1)S(1)}, bf16[8,8192]{1,0:T(8,128)(2,1)S(1)}, u32[]{:S(2)}, u32[]{:S(2)}) collective-permute-start(bf16[8,8192]{1,0:T(8,128)(2,1)S(1)} %side_by_side.1.refs_0_), channel_id=1, source_target_pairs={{0,8},{8,0},{16,24},{24,16},{1,9},{9,1},{17,25},{25,17},{2,10},{10... | collective-permute-start | bytes 393224 | tf_op jit(solution)/shard_map/ppermute | solution.py:47
  8.1 2.6 %collective-permute-start.5 = (bf16[8,8192]{1,0:T(8,128)(2,1)S(1)}, bf16[8,8192]{1,0:T(8,128)(2,1)S(1)}, u32[]{:S(2)}, u32[]{:S(2)}) collective-permute-start(bf16[8,8192]{1,0:T(8,128)(2,1)S(1)} %side_by_side.1.refs_0_), channel_id=1, source_target_pairs={{0,16},{8,24},{16,0},{24,8},{1,17},{9,25},{17,1},{25,9},{2,18},{10... | collective-permute-start | bytes 393224 | tf_op jit(solution)/shard_map/ppermute | solution.py:47
  10.7 0.7 copy-done
  11.4 0.7 copy-done.1
  12.1 11.0 %dense_both.1 = (bf16[4096,1792]{1,0:T(8,128)(2,1)S(1)}, bf16[1792,4096]{1,0:T(8,128)(2,1)}) custom-call(s32[1,224]{1,0:T(1,128)S(1)} %copy-done, s32[1,224]{1,0:T(1,128)S(1)} %copy-done.1, bf16[224,128,128]{2,1,0:T(8,128)(2,1)} %ub.1, bf16[224,128,128]{2,1,0:T(8,128)(2,1)} %db.1), custom_call_target="tpu_custom_call" | custom-call | tf_op jit(solution)/shard_map/dense_both/pallas_call | solution.py:196
  23.1 0.1 collective-permute-start.6
  23.3 0.1 collective-permute-start.3
  23.3 0.5 copy-done.3
  23.9 0.2 select_reduce_fusion
  24.1 5.9 %collective-permute-done.6.refs_2_ = bf16[8,8192]{1,0:T(8,128)(2,1)S(1)} collective-permute-done((bf16[8,8192]{1,0:T(8,128)(2,1)S(1)}, bf16[8,8192]{1,0:T(8,128)(2,1)S(1)}, u32[]{:S(2)}, u32[]{:S(2)}) %collective-permute-start.6) | collective-permute-done | bytes 131104 | tf_op jit(solution)/shard_map/ppermute | solution.py:47
  30.0 1.6 %collective-permute-start.11 = (bf16[24,8192]{1,0:T(8,128)(2,1)S(1)}, bf16[24,8192]{1,0:T(8,128)(2,1)S(1)}, u32[]{:S(2)}, u32[]{:S(2)}) collective-permute-start(bf16[24,8192]{1,0:T(8,128)(2,1)S(1)} %pack.3.refs_1_.refs_0_), channel_id=1, source_target_pairs={{0,2},{1,3},{2,0},{3,1},{4,6},{5,7},{6,4},{7,5},{8,10},{9,11},{10,... | collective-permute-start | bytes 1179656 | tf_op jit(solution)/shard_map/ppermute | solution.py:47
  31.6 1.5 %collective-permute-start.12 = (bf16[24,8192]{1,0:T(8,128)(2,1)S(1)}, bf16[24,8192]{1,0:T(8,128)(2,1)S(1)}, u32[]{:S(2)}, u32[]{:S(2)}) collective-permute-start(bf16[24,8192]{1,0:T(8,128)(2,1)S(1)} %pack.3.refs_1_.refs_0_), channel_id=1, source_target_pairs={{0,4},{1,5},{2,6},{3,7},{4,0},{5,1},{6,2},{7,3},{8,12},{9,13},{10,... | collective-permute-start | bytes 1179656 | tf_op jit(solution)/shard_map/ppermute | solution.py:47
  33.1 0.5 collective-permute-start.13
  33.6 4.6 %dense_gate.1.refs_2_.wg.refs_8_ = bf16[4096,1792]{1,0:T(8,128)(2,1)S(1)} custom-call(s32[1,224]{1,0:T(1,128)S(1)} %copy-done.2, bf16[224,128,128]{2,1,0:T(8,128)(2,1)} %blocks.1, bf16[32,8192]{1,0:T(8,128)(2,1)S(1)} %pack.2.refs_0_, bf16[24,8192]{1,0:T(8,128)(2,1)S(1)} %pack.3.refs_1_.refs_0_, s32[3,70]{1,0:T(4,128)S(1)} %broadcast_add_fusion.refs_2_.spots), custom_call_target="tpu_custom_call" | custom-call | tf_op jit(solution)/shard_map/dense_gate/pallas_call | solution.py:183
  38.3 12.5 %own_acts.1 = (bf16[64,1792]{1,0:T(8,128)(2,1)S(1)}, bf16[64,1792]{1,0:T(8,128)(2,1)S(1)}, bf16[64,1792]{1,0:T(8,128)(2,1)S(1)}, bf16[64,8192]{1,0:T(8,128)(2,1)S(1)}) custom-call(bf16[32,8192]{1,0:T(8,128)(2,1)S(1)} %pack.2.refs_0_, bf16[32,8192]{1,0:T(8,128)(2,1)S(1)} %collective-permute-done.3.refs_1_, ...), custom_call_target="tpu_custom_call" | custom-call | flops 2818572288 | bytes 14680064 | tf_op jit(solution)/shard_map/own_acts/pallas_call | solution.py:244
  50.8 13.9 %own_out.1 = (bf16[32,8192]{1,0:T(8,128)(2,1)S(1)}, bf16[32,8192]{1,0:T(8,128)(2,1)S(1)}) custom-call(bf16[64,1792]{1,0:T(8,128)(2,1)S(1)} %get-tuple-element.26.hid.hid0, bf16[64,1792]{1,0:T(8,128)(2,1)S(1)} %get-tuple-element.27.gp.gp0, bf16[64,1792]{1,0:T(8,128)(2,1)S(1)} %get-tuple-element.28.up.up0, ...), custom_call_target="tpu_custom_call" | custom-call | flops 2818572288 | bytes 14680064 | tf_op jit(solution)/shard_map/own_out/pallas_call | solution.py:279
  64.7 0.1 collective-permute-start.7
  64.7 0.5 collective-permute-start.14
  65.2 0.1 collective-permute-start.15
  65.3 0.4 collective-permute-start.16
  65.8 0.1 collective-permute-start.17
  65.8 0.8 collective-permute-done.7.refs_1_
  66.6 0.2 add_and_cut.1
  66.8 2.5 %collective-permute-start.10 = (bf16[8,8192]{1,0:T(8,128)(2,1)S(1)}, bf16[8,8192]{1,0:T(8,128)(2,1)S(1)}, u32[]{:S(2)}, u32[]{:S(2)}) collective-permute-start(bf16[8,8192]{1,0:T(8,128)(2,1)S(1)} %get-tuple-element.34), channel_id=1, source_target_pairs={{0,6},{1,7},{2,4},{3,5},{4,2},{5,3},{6,0},{7,1},{8,14},{9,15},{10,... | collective-permute-start | bytes 393224 | tf_op jit(solution)/shard_map/ppermute | solution.py:47
  69.3 0.5 collective-permute-start.9
  69.8 0.5 collective-permute-start.8
  70.4 14.0 %rest_acts.1 = (bf16[192,1792]{1,0:T(8,128)(2,1)S(1)}, bf16[192,1792]{1,0:T(8,128)(2,1)S(1)}, bf16[192,1792]{1,0:T(8,128)(2,1)S(1)}, bf16[192,8192]{1,0:T(8,128)(2,1)S(1)}) custom-call(bf16[24,8192]{1,0:T(8,128)(2,1)S(1)} %pack.3.refs_1_.refs_0_, bf16[24,8192]{1,0:T(8,128)(2,1)S(1)} %collective-permute-done.11.refs_1_, ...), custom_call_target="tpu_custom_call" | custom-call | flops 8455716864 | bytes 14680064 | tf_op jit(solution)/shard_map/rest_acts/pallas_call | solution.py:244
  84.4 12.6 %grads.1 = (f32[70,128,128]{2,1,0:T(8,128)}, f32[70,128,128]{2,1,0:T(8,128)}, f32[70,128,128]{2,1,0:T(8,128)}) custom-call(s32[3,70]{1,0:T(4,128)S(1)} %broadcast_add_fusion.refs_2_.spots, bf16[64,8192]{1,0:T(8,128)(2,1)S(1)} %get-tuple-element.35.own, bf16[192,8192]{1,0:T(8,128)(2,1)S(1)} %get-tuple-element.36.rest, ...), custom_call_target="tpu_custom_call" | custom-call | flops 1761607680 | bytes 13762560 | tf_op jit(solution)/shard_map/grads/pallas_call | solution.py:354
  97.0 0.7 fusion
  (33 shorter events, 0.3 us)
Async XLA Ops:
  1.5 21.5 %collective-permute-start = (bf16[8,8192]{1,0:T(8,128)(2,1)S(1)}, bf16[8,8192]{1,0:T(8,128)(2,1)S(1)}, u32[]{:S(2)}, u32[]{:S(2)}) collective-permute-start(bf16[8,8192]{1,0:T(8,128)(2,1)S(1)} %side_by_side.1.refs_0_), channel_id=1, source_target_pairs={{0,2},{1,3},{2,0},{3,1},{4,6},{5,7},{6,4},{7,5},{8,10},{9,11},{10,... | collective-permute-start | bytes 393224 | tf_op jit(solution)/shard_map/ppermute | solution.py:47
  4.5 18.6 %collective-permute-start.1 = (bf16[8,8192]{1,0:T(8,128)(2,1)S(1)}, bf16[8,8192]{1,0:T(8,128)(2,1)S(1)}, u32[]{:S(2)}, u32[]{:S(2)}) collective-permute-start(bf16[8,8192]{1,0:T(8,128)(2,1)S(1)} %side_by_side.1.refs_0_), channel_id=1, source_target_pairs={{0,4},{1,5},{2,6},{3,7},{4,0},{5,1},{6,2},{7,3},{8,12},{9,13},{10,... | collective-permute-start | bytes 393224 | tf_op jit(solution)/shard_map/ppermute | solution.py:47
  6.1 17.1 %collective-permute-start.2 = (bf16[8,8192]{1,0:T(8,128)(2,1)S(1)}, bf16[8,8192]{1,0:T(8,128)(2,1)S(1)}, u32[]{:S(2)}, u32[]{:S(2)}) collective-permute-start(bf16[8,8192]{1,0:T(8,128)(2,1)S(1)} %side_by_side.1.refs_0_), channel_id=1, source_target_pairs={{0,6},{1,7},{2,4},{3,5},{4,2},{5,3},{6,0},{7,1},{8,14},{9,15},{10,... | collective-permute-start | bytes 393224 | tf_op jit(solution)/shard_map/ppermute | solution.py:47
  6.1 18.0 %collective-permute-start.4 = (bf16[8,8192]{1,0:T(8,128)(2,1)S(1)}, bf16[8,8192]{1,0:T(8,128)(2,1)S(1)}, u32[]{:S(2)}, u32[]{:S(2)}) collective-permute-start(bf16[8,8192]{1,0:T(8,128)(2,1)S(1)} %side_by_side.1.refs_0_), channel_id=1, source_target_pairs={{0,8},{8,0},{16,24},{24,16},{1,9},{9,1},{17,25},{25,17},{2,10},{10... | collective-permute-start | bytes 393224 | tf_op jit(solution)/shard_map/ppermute | solution.py:47
  8.1 16.0 %collective-permute-start.5 = (bf16[8,8192]{1,0:T(8,128)(2,1)S(1)}, bf16[8,8192]{1,0:T(8,128)(2,1)S(1)}, u32[]{:S(2)}, u32[]{:S(2)}) collective-permute-start(bf16[8,8192]{1,0:T(8,128)(2,1)S(1)} %side_by_side.1.refs_0_), channel_id=1, source_target_pairs={{0,16},{8,24},{16,0},{24,8},{1,17},{9,25},{17,1},{25,9},{2,18},{10... | collective-permute-start | bytes 393224 | tf_op jit(solution)/shard_map/ppermute | solution.py:47
  10.7 0.7 copy-start
  11.4 0.7 copy-start.1
  12.1 11.0 %copy-start.2 = (s32[1,224]{1,0:T(1,128)S(1)}, s32[1,224]{1,0:T(1,128)}, u32[]{:S(2)}) copy-start(s32[1,224]{1,0:T(1,128)} %index.1) | copy-start | bytes 2692
  23.1 6.9 %collective-permute-start.6 = (bf16[8,8192]{1,0:T(8,128)(2,1)S(1)}, bf16[8,8192]{1,0:T(8,128)(2,1)S(1)}, u32[]{:S(2)}, u32[]{:S(2)}) collective-permute-start(bf16[8,8192]{1,0:T(8,128)(2,1)S(1)} %side_by_side.1.refs_0_), channel_id=1, source_target_pairs={{0,24},{8,16},{16,8},{24,0},{1,25},{9,17},{17,9},{25,1},{2,26},{10... | collective-permute-start | bytes 393224 | tf_op jit(solution)/shard_map/ppermute | solution.py:47
  23.2 0.7 copy-start.3
  23.2 0.7 copy-start.4
  23.2 0.7 copy-start.5
  23.3 15.0 %collective-permute-start.3 = (bf16[32,8192]{1,0:T(8,128)(2,1)S(1)}, bf16[32,8192]{1,0:T(8,128)(2,1)S(1)}, u32[]{:S(2)}, u32[]{:S(2)}) collective-permute-start(bf16[32,8192]{1,0:T(8,128)(2,1)S(1)} %pack.2.refs_0_), channel_id=1, source_target_pairs={{0,1},{1,0},{2,3},{3,2},{4,5},{5,4},{6,7},{7,6},{8,9},{9,8},{10,11... | collective-permute-start | bytes 1572872 | tf_op jit(solution)/shard_map/ppermute | solution.py:47
  30.0 35.2 %collective-permute-start.11 = (bf16[24,8192]{1,0:T(8,128)(2,1)S(1)}, bf16[24,8192]{1,0:T(8,128)(2,1)S(1)}, u32[]{:S(2)}, u32[]{:S(2)}) collective-permute-start(bf16[24,8192]{1,0:T(8,128)(2,1)S(1)} %pack.3.refs_1_.refs_0_), channel_id=1, source_target_pairs={{0,2},{1,3},{2,0},{3,1},{4,6},{5,7},{6,4},{7,5},{8,10},{9,11},{10,... | collective-permute-start | bytes 1179656 | tf_op jit(solution)/shard_map/ppermute | solution.py:47
  31.6 33.7 %collective-permute-start.12 = (bf16[24,8192]{1,0:T(8,128)(2,1)S(1)}, bf16[24,8192]{1,0:T(8,128)(2,1)S(1)}, u32[]{:S(2)}, u32[]{:S(2)}) collective-permute-start(bf16[24,8192]{1,0:T(8,128)(2,1)S(1)} %pack.3.refs_1_.refs_0_), channel_id=1, source_target_pairs={{0,4},{1,5},{2,6},{3,7},{4,0},{5,1},{6,2},{7,3},{8,12},{9,13},{10,... | collective-permute-start | bytes 1179656 | tf_op jit(solution)/shard_map/ppermute | solution.py:47
  33.1 32.6 %collective-permute-start.13 = (bf16[24,8192]{1,0:T(8,128)(2,1)S(1)}, bf16[24,8192]{1,0:T(8,128)(2,1)S(1)}, u32[]{:S(2)}, u32[]{:S(2)}) collective-permute-start(bf16[24,8192]{1,0:T(8,128)(2,1)S(1)} %pack.3.refs_1_.refs_0_), channel_id=1, source_target_pairs={{0,6},{1,7},{2,4},{3,5},{4,2},{5,3},{6,0},{7,1},{8,14},{9,15},{10,... | collective-permute-start | bytes 1179656 | tf_op jit(solution)/shard_map/ppermute | solution.py:47
  64.7 2.0 %collective-permute-start.7 = (bf16[32,8192]{1,0:T(8,128)(2,1)S(1)}, bf16[32,8192]{1,0:T(8,128)(2,1)S(1)}, u32[]{:S(2)}, u32[]{:S(2)}) collective-permute-start(bf16[32,8192]{1,0:T(8,128)(2,1)S(1)} %get-tuple-element.30), channel_id=1, source_target_pairs={{0,1},{1,0},{2,3},{3,2},{4,5},{5,4},{6,7},{7,6},{8,9},{9,8},{10,11... | collective-permute-start | bytes 1572872 | tf_op jit(solution)/shard_map/ppermute | solution.py:47
  64.7 4.6 %collective-permute-start.14 = (bf16[24,8192]{1,0:T(8,128)(2,1)S(1)}, bf16[24,8192]{1,0:T(8,128)(2,1)S(1)}, u32[]{:S(2)}, u32[]{:S(2)}) collective-permute-start(bf16[24,8192]{1,0:T(8,128)(2,1)S(1)} %pack.3.refs_1_.refs_0_), channel_id=1, source_target_pairs={{0,1},{1,0},{2,3},{3,2},{4,5},{5,4},{6,7},{7,6},{8,9},{9,8},{10,11... | collective-permute-start | bytes 1179656 | tf_op jit(solution)/shard_map/ppermute | solution.py:47
  65.2 4.6 %collective-permute-start.15 = (bf16[24,8192]{1,0:T(8,128)(2,1)S(1)}, bf16[24,8192]{1,0:T(8,128)(2,1)S(1)}, u32[]{:S(2)}, u32[]{:S(2)}) collective-permute-start(bf16[24,8192]{1,0:T(8,128)(2,1)S(1)} %collective-permute-done.11.refs_1_), channel_id=1, source_target_pairs={{0,1},{1,0},{2,3},{3,2},{4,5},{5,4},{6,7},{7,6},{8,9},{9,8},{10,11... | collective-permute-start | bytes 1179656 | tf_op jit(solution)/shard_map/ppermute | solution.py:47
  65.3 5.0 %collective-permute-start.16 = (bf16[24,8192]{1,0:T(8,128)(2,1)S(1)}, bf16[24,8192]{1,0:T(8,128)(2,1)S(1)}, u32[]{:S(2)}, u32[]{:S(2)}) collective-permute-start(bf16[24,8192]{1,0:T(8,128)(2,1)S(1)} %collective-permute-done.12.refs_2_), channel_id=1, source_target_pairs={{0,1},{1,0},{2,3},{3,2},{4,5},{5,4},{6,7},{7,6},{8,9},{9,8},{10,11... | collective-permute-start | bytes 1179656 | tf_op jit(solution)/shard_map/ppermute | solution.py:47
  65.8 4.6 %collective-permute-start.17 = (bf16[24,8192]{1,0:T(8,128)(2,1)S(1)}, bf16[24,8192]{1,0:T(8,128)(2,1)S(1)}, u32[]{:S(2)}, u32[]{:S(2)}) collective-permute-start(bf16[24,8192]{1,0:T(8,128)(2,1)S(1)} %collective-permute-done.13.refs_3_), channel_id=1, source_target_pairs={{0,1},{1,0},{2,3},{3,2},{4,5},{5,4},{6,7},{7,6},{8,9},{9,8},{10,11... | collective-permute-start | bytes 1179656 | tf_op jit(solution)/shard_map/ppermute | solution.py:47
  66.8 30.1 %collective-permute-start.10 = (bf16[8,8192]{1,0:T(8,128)(2,1)S(1)}, bf16[8,8192]{1,0:T(8,128)(2,1)S(1)}, u32[]{:S(2)}, u32[]{:S(2)}) collective-permute-start(bf16[8,8192]{1,0:T(8,128)(2,1)S(1)} %get-tuple-element.34), channel_id=1, source_target_pairs={{0,6},{1,7},{2,4},{3,5},{4,2},{5,3},{6,0},{7,1},{8,14},{9,15},{10,... | collective-permute-start | bytes 393224 | tf_op jit(solution)/shard_map/ppermute | solution.py:47
  69.3 27.6 %collective-permute-start.9 = (bf16[8,8192]{1,0:T(8,128)(2,1)S(1)}, bf16[8,8192]{1,0:T(8,128)(2,1)S(1)}, u32[]{:S(2)}, u32[]{:S(2)}) collective-permute-start(bf16[8,8192]{1,0:T(8,128)(2,1)S(1)} %get-tuple-element.33), channel_id=1, source_target_pairs={{0,4},{1,5},{2,6},{3,7},{4,0},{5,1},{6,2},{7,3},{8,12},{9,13},{10,... | collective-permute-start | bytes 393224 | tf_op jit(solution)/shard_map/ppermute | solution.py:47
  69.8 27.1 %collective-permute-start.8 = (bf16[8,8192]{1,0:T(8,128)(2,1)S(1)}, bf16[8,8192]{1,0:T(8,128)(2,1)S(1)}, u32[]{:S(2)}, u32[]{:S(2)}) collective-permute-start(bf16[8,8192]{1,0:T(8,128)(2,1)S(1)} %get-tuple-element.32), channel_id=1, source_target_pairs={{0,2},{1,3},{2,0},{3,1},{4,6},{5,7},{6,4},{7,5},{8,10},{9,11},{10,... | collective-permute-start | bytes 393224 | tf_op jit(solution)/shard_map/ppermute | solution.py:47

commit v3 on v2

--- a/solution.py
+++ b/solution.py
@@ -20,6 +20,8 @@
 ANY_SPEC = pl.BlockSpec(memory_space=pl.ANY)
 FREE = pl.CostEstimate(flops=0, bytes_accessed=0, transcendentals=0)
 LIMIT = pltpu.CompilerParams(vmem_limit_bytes=4 * 2**20)
+DENSE_LIMIT = 17 * 2**20
+NEXT_LIMIT = 17 * 2**20
 
 
 def in_vmem():
@@ -133,76 +135,58 @@
     )(*parts, *sent)
 
 
-def scatter(index, blocks, dense, sem, other=None):
-    kept, size = blocks.shape[0], blocks.shape[1]
+def scatter(index, blocks, dense, sem, first, count):
+    size = blocks.shape[1]
     cols = dense.shape[1] // size
+    scale = 2**16 // cols + 1
+    for u in range(count):
+        k = first + u
+        b = index[0, k]
+        r = lax.shift_right_logical(b * scale, 16)
+        c = b - r * cols
+        r, c = pl.multiple_of(r * size, size), pl.multiple_of(c * size, size)
+        pltpu.make_async_copy(
+            blocks.at[k], dense.at[pl.ds(r, size), pl.ds(c, size)], sem
+        ).start()
+
+
+def dense_body(again, index_hbm, blocks, *refs):
+    if again:
+        source, dense, copied, index, sem = refs[0], *refs[-4:]
+        copy = pltpu.make_async_copy(source, copied, sem.at[2])
+        copy.start()
+    else:
+        dense, index, sem = refs[-3:]
+    fetch = pltpu.make_async_copy(index_hbm, index, sem.at[1])
+    fetch.start()
+    dense[...] = jnp.zeros_like(dense)
+    fetch.wait()
+    kept = blocks.shape[0]
     unroll = 8 if kept % 8 == 0 else 1
-    scale = 2**16 // cols + 1
-    steps = kept // unroll
-    rows = 0 if other is None else other.shape[0] // steps // 16 * 16
 
     def step(i, carry):
-        for u in range(unroll):
-            k = i * unroll + u
-            b = index[0, k]
-            r = lax.shift_right_logical(b * scale, 16)
-            c = b - r * cols
-            r, c = pl.multiple_of(r * size, size), pl.multiple_of(c * size, size)
-            pltpu.make_async_copy(
-                blocks.at[k], dense.at[pl.ds(r, size), pl.ds(c, size)], sem
-            ).start()
-        if rows:
-            part = pl.ds(pl.multiple_of(i * rows, rows), rows)
-            other[part] = jnp.zeros((rows, other.shape[1]), BF16)
-        return carry
-
-    lax.fori_loop(0, steps, step, 0)
-    if other is not None and other.shape[0] > steps * rows:
-        left = other.shape[0] - steps * rows
-        other[pl.ds(steps * rows, left)] = jnp.zeros((left, other.shape[1]), BF16)
-
-
-def dense_gate_body(index, blocks, *refs):
-    wg, sem = refs[-2:]
-    wg[...] = jnp.zeros_like(wg)
-    scatter(index, blocks, wg, sem)
-    pltpu.make_async_copy(blocks, blocks, sem).wait()
-
-
-def dense_both_body(ui, di, ub, db, wu, wd, stage, sem):
-    stage[...] = jnp.zeros_like(stage)
-    scatter(di, db, stage, sem.at[0], wu)
-    scatter(ui, ub, wu, sem.at[2])
-    pltpu.make_async_copy(db, db, sem.at[0]).wait()
-    pltpu.make_async_copy(stage, wd, sem.at[1]).start()
-    pltpu.make_async_copy(ub, ub, sem.at[2]).wait()
-    pltpu.make_async_copy(stage, wd, sem.at[1]).wait()
-
-
-def dense_gate(index, blocks, width, hidden, wait_for):
-    return pl.pallas_call(
-        dense_gate_body,
-        out_shape=VMEM((width, hidden), BF16),
-        in_specs=[SMEM_SPEC, HBM_SPEC] + [ANY_SPEC] * len(wait_for),
-        out_specs=in_vmem(),
-        scratch_shapes=[pltpu.SemaphoreType.DMA],
-        compiler_params=pltpu.CompilerParams(vmem_limit_bytes=2**20),
+        scatter(index, blocks, dense, sem.at[0], i * unroll, unroll)
+        return carry
+
+    lax.fori_loop(0, kept // unroll, step, 0)
+    if again:
+        copy.wait()
+    pltpu.make_async_copy(blocks, blocks, sem.at[0]).wait()
+
+
+def dense(index, blocks, source, width, hidden, limit, wait_for=()):
+    again = [] if source is None else [source]
+    outs = [VMEM((width, hidden), BF16)] + [VMEM(x.shape, x.dtype) for x in again]
+    return pl.pallas_call(
+        functools.partial(dense_body, bool(again)),
+        out_shape=outs,
+        in_specs=[HBM_SPEC] * 2 + [ANY_SPEC] * (len(again) + len(wait_for)),
+        out_specs=[in_vmem()] * len(outs),
+        scratch_shapes=[pltpu.SMEM(index.shape, jnp.int32), pltpu.SemaphoreType.DMA((3,))],
+        compiler_params=pltpu.CompilerParams(vmem_limit_bytes=limit),
         cost_estimate=FREE,
-        name="dense_gate",
-    )(index, in_hbm(blocks), *wait_for)
-
-
-def dense_both(up_index, down_index, up_blocks, down_blocks, width, hidden):
-    return pl.pallas_call(
-        dense_both_body,
-        out_shape=(VMEM((width, hidden), BF16), pltpu.HBM((hidden, width), BF16)),
-        in_specs=[SMEM_SPEC] * 2 + [HBM_SPEC] * 2,
-        out_specs=(in_vmem(), HBM_SPEC),
-        scratch_shapes=[VMEM((hidden, width), BF16), pltpu.SemaphoreType.DMA((3,))],
-        compiler_params=pltpu.CompilerParams(vmem_limit_bytes=2 * hidden * width + 2**20),
-        cost_estimate=FREE,
-        name="dense_both",
-    )(up_index, down_index, in_hbm(up_blocks), in_hbm(down_blocks))
+        name="dense",
+    )(in_hbm(index), in_hbm(blocks), *again, *wait_for)
 
 
 def chunk_of(hidden):
@@ -257,39 +241,96 @@
     )(*pieces, *pinned(wg, wu), in_hbm(wd), *wait_for)
 
 
-def own_out_body(hid, gp, up, wg, wu, wd, part, back):
-    n = pl.program_id(0)
-    chunk = wd.shape[1]
-    width = wg.shape[0]
+def own_body(count, index_hbm, *refs):
+    pieces, (wg, wu, blocks), refs = refs[:count], refs[count : count + 3], refs[count + 3 :]
+    hid, gp, up, x, part, back, wd_out, wd, g_all, u_all, index, sem = refs
+    width, hidden = wg.shape
+    steps, _, chunk = g_all.shape
+    kept = blocks.shape[0]
+    each = kept // steps
+    fetch = pltpu.make_async_copy(index_hbm, index, sem.at[1])
+    fetch.start()
+    assemble(pieces, x)
+
+    def place(n):
+        return pl.ds(pl.multiple_of(n * chunk, chunk), chunk)
+
+    def gate(n, carry):
+        g_all[n] = dot_nn(x[:, :width], wg[:, place(n)])
+        wd[place(n)] = jnp.zeros((chunk, width), BF16)
+        return carry
+
+    lax.fori_loop(0, steps, gate, 0)
+    fetch.wait()
+
+    def up_proj(n, carry):
+        scatter(index, blocks, wd, sem.at[0], n * each, each)
+        u_all[n] = dot_nn(x[:, :width], wu[:, place(n)])
+        return carry
+
+    lax.fori_loop(0, steps, up_proj, 0)
+    scatter(index, blocks, wd, sem.at[0], steps * each, kept - steps * each)
+    pltpu.make_async_copy(blocks, blocks, sem.at[0]).wait()
+    store = pltpu.make_async_copy(wd, wd_out, sem.at[2])
+    store.start()
+
+    def grad(n, carry):
+        cols = place(n)
+        g, u = g_all[n], u_all[n]
+        h = dot_nt(x[:, width:], wd[cols])
+        s = jax.nn.sigmoid(g)
+        hid[:, cols] = (g * s * u).astype(BF16)
+        gp[:, cols] = (h * u * s * (1.0 + g * (1.0 - s))).astype(BF16)
+        up[:, cols] = (h * g * s).astype(BF16)
+        return carry
+
+    lax.fori_loop(0, steps, grad, 0)
     half = part.shape[0]
-    out = pl.ds(pl.multiple_of(n * chunk, chunk), chunk)
-    later = pl.ds(pl.multiple_of(width + n * chunk, chunk), chunk)
-    left = dot_nn(hid[...], wd[...]).astype(BF16)
-    right = (dot_nt(gp[...], wg[out, :]) + dot_nt(up[...], wu[out, :])).astype(BF16)
-    part[:, out] = left[:half]
-    back[:, out] = left[half:]
-    part[:, later] = right[:half]
-    back[:, later] = right[half:]
-
-
-def own_out(hid, gp, up, wg, wu, wd):
-    rows = hid.shape[0]
+    wide = 512
+
+    def sums(n, carry):
+        out = pl.ds(pl.multiple_of(n * wide, wide), wide)
+        later = pl.ds(pl.multiple_of(width + n * wide, wide), wide)
+        left = dot_nn(hid[...], wd[:, out]).astype(BF16)
+        right = (dot_nt(gp[...], wg[out, :]) + dot_nt(up[...], wu[out, :])).astype(BF16)
+        part[:, out] = left[:half]
+        back[:, out] = left[half:]
+        part[:, later] = right[:half]
+        back[:, later] = right[half:]
+        return carry
+
+    lax.fori_loop(0, width // wide, sums, 0)
+    store.wait()
+
+
+def own_pass(pieces, wg, wu, index, blocks, limit):
+    rows = sum(x.shape[0] for x in pieces)
     width, hidden = wg.shape
-    chunk = 512
-    return pl.pallas_call(
-        own_out_body,
-        out_shape=(jax.ShapeDtypeStruct((rows // 2, 2 * width), BF16),) * 2,
-        grid=(width // chunk,),
-        in_specs=[in_vmem()] * 5 + [pl.BlockSpec((hidden, chunk), lambda n: (0, n))],
-        out_specs=(in_vmem(), in_vmem()),
-        compiler_params=pltpu.CompilerParams(
-            vmem_limit_bytes=max(4 * chunk * hidden + 16 * rows * chunk + 2**21, 7 * 2**20)
+    chunk = chunk_of(hidden)
+    act = VMEM((rows, hidden), BF16)
+    half = VMEM((rows // 2, 2 * width), BF16)
+    kept = VMEM((hidden // chunk, rows, chunk), F32)
+    return pl.pallas_call(
+        functools.partial(own_body, len(pieces)),
+        out_shape=(
+            act, act, act, VMEM((rows, 2 * width), BF16), half, half,
+            pltpu.HBM((hidden, width), BF16),
         ),
+        in_specs=[HBM_SPEC] + [in_vmem()] * (len(pieces) + 2) + [HBM_SPEC],
+        out_specs=(in_vmem(),) * 6 + (HBM_SPEC,),
+        scratch_shapes=[
+            VMEM((hidden, width), BF16),
+            kept,
+            kept,
+            pltpu.SMEM(index.shape, jnp.int32),
+            pltpu.SemaphoreType.DMA((3,)),
+        ],
+        compiler_params=pltpu.CompilerParams(vmem_limit_bytes=limit),
         cost_estimate=pl.CostEstimate(
-            flops=6 * rows * width * hidden, bytes_accessed=2 * width * hidden, transcendentals=0
+            flops=12 * rows * width * hidden, bytes_accessed=2 * width * hidden, transcendentals=0
         ),
-        name="own_out",
-    )(hid, gp, up, *pinned(wg, wu), in_hbm(wd))
+        name="own_pass",
+    )(in_hbm(index), *pieces, *pinned(wg, wu), in_hbm(blocks))
 
 
 def grads_body(
@@ -404,16 +445,19 @@
         return exchange(x, "tensor", 1)
 
     far = [exchange(both, "dp", a) for a in range(1, groups)]
-    near = [exchange(both, "tensor", d) for d in chips]
-    wu, wd = dense_both(up_index, down_index, up_blocks, down_blocks, width, hidden)
-    own_half = pack([both, *near], [wu])
+    near = [exchange(both, "tensor", d) for d in chips[:-1]]
+    stage = 2 * width * hidden
+    wu, later = dense(up_index, up_blocks, both, width, hidden, DENSE_LIMIT)
+    near.append(exchange(later, "tensor", chips[-1]))
     others = pack(far, [wu])
-    wg = dense_gate(gate_index, gate_blocks, width, hidden, [own_half, others, spots])
+    (wg,) = dense(gate_index, gate_blocks, None, width, hidden, NEXT_LIMIT, [spots, others])
+    own_half = pack([both, *near], [wg])
     own_pieces = [own_half, sibling(own_half)]
     other_half = [others, *(exchange(others, "tensor", d) for d in chips)]
 
-    *acts0, own = acts_pass(own_pieces, wg, wu, wd, "own_acts")
-    part, back = own_out(*acts0, wg, wu, wd)
+    *acts0, own, part, back, wd = own_pass(
+        own_pieces, wg, wu, down_index, down_blocks, stage + 3 * 2**20
+    )
     chip = add_and_cut([part], [sibling(back)], slices // 2)
     acts1_in = [*other_half, *(sibling(x) for x in other_half)]
     *acts1, rest = acts_pass(acts1_in, wg, wu, wd, "rest_acts", [chip[0]])

time: 98.2 us -> 90.8 us (0.925)
  Pallas kernels: 69.7 us -> 62.7 us
  waiting for transfers between devices: 6.71 us -> 4.16 us
  other arithmetic: 0.31 us -> 1.73 us
    pallas_call x2 -> x1, Pallas kernels: 26.5 us -> 14.2 us  [acts_pass(): pl.pallas_call(functools.partial(acts_body, len(pieces)), out_shape=(act,...]
    pallas_call x3, Pallas kernels: 29.5 us -> 34.8 us  [the longest x1 26.3 us: own_pass(): pl.pallas_call(functools.partial(own_body, len(pieces)), out_shape=(act,...]
    ppermute x18, waiting for transfers between devices: 6.71 us -> 4.16 us  [exchange(): return lax.ppermute(x, axis, [(i, i ^ flip) for i in range(count)])]
    unnamed x12 -> x4, local copies, waits for them, and re-layouts: 1.89 us -> 2.8 us
  transfers between devices with their start and end apart: 18 -> 18, of which waited for: 2 -> 3; matrix products, arithmetic and copies ran while one was open for 0% -> 2% of each run, Pallas kernels for 70% -> 68%
where the time goes in v3:
time: 90.8 us; the launch traced here: 90.3 us
  Pallas kernels  62.7 us (69%)
  starting transfers between devices  17.5 us (19%)
  waiting for transfers between devices  4.16 us (5%)
  local copies, waits for them, and re-layouts  3.46 us (4%)
  other arithmetic  1.73 us (2%)
    pallas_call x1, Pallas kernels, own_pass(): pl.pallas_call(functools.partial(own_body, len(pieces)), out_shape=(act,...  26.3 us
    ppermute x18, starting transfers between devices, exchange(): return lax.ppermute(x, axis, [(i, i ^ flip) for i in range(count)])  17.5 us
    pallas_call x1, Pallas kernels, acts_pass(): pl.pallas_call(functools.partial(acts_body, len(pieces)), out_shape=(act,...  14.2 us
    pallas_call x1, Pallas kernels, grads(): pl.pallas_call(functools.partial(grads_body, factor, size), out_shape=(ou...  12.6 us
    pallas_call x2, Pallas kernels, dense(): pl.pallas_call(functools.partial(dense_body, bool(again)), out_shape=outs...  8.41 us
    ppermute x18, waiting for transfers between devices, exchange(): return lax.ppermute(x, axis, [(i, i ^ flip) for i in range(count)])  4.16 us
    unnamed x4, local copies, waits for them, and re-layouts  2.8 us
  transfers between devices with their start and end apart: 18, of which 3 were waited for; matrix products, arithmetic and copies ran while one was open for 2% of the time, Pallas kernels for 68%

profile of v3, /device:TPU:0, one launch (start us, length us, event | category | flops | bytes accessed | tf_op | source)
XLA Modules:
  0.0 90.3 jit_solution(6692734428149892182)
XLA Ops:
  0.6 0.9 side_by_side.1.refs_0_
  1.5 3.0 %collective-permute-start = (bf16[8,8192]{1,0:T(8,128)(2,1)S(1)}, bf16[8,8192]{1,0:T(8,128)(2,1)S(1)}, u32[]{:S(2)}, u32[]{:S(2)}) collective-permute-start(bf16[8,8192]{1,0:T(8,128)(2,1)S(1)} %side_by_side.1.refs_0_), channel_id=1, source_target_pairs={{0,2},{1,3},{2,0},{3,1},{4,6},{5,7},{6,4},{7,5},{8,10},{9,11},{10,... | collective-permute-start | bytes 393224 | tf_op jit(solution)/shard_map/ppermute | solution.py:49
  4.5 1.5 %collective-permute-start.1 = (bf16[8,8192]{1,0:T(8,128)(2,1)S(1)}, bf16[8,8192]{1,0:T(8,128)(2,1)S(1)}, u32[]{:S(2)}, u32[]{:S(2)}) collective-permute-start(bf16[8,8192]{1,0:T(8,128)(2,1)S(1)} %side_by_side.1.refs_0_), channel_id=1, source_target_pairs={{0,4},{1,5},{2,6},{3,7},{4,0},{5,1},{6,2},{7,3},{8,12},{9,13},{10,... | collective-permute-start | bytes 393224 | tf_op jit(solution)/shard_map/ppermute | solution.py:49
  6.1 1.6 %collective-permute-start.3 = (bf16[8,8192]{1,0:T(8,128)(2,1)S(1)}, bf16[8,8192]{1,0:T(8,128)(2,1)S(1)}, u32[]{:S(2)}, u32[]{:S(2)}) collective-permute-start(bf16[8,8192]{1,0:T(8,128)(2,1)S(1)} %side_by_side.1.refs_0_), channel_id=1, source_target_pairs={{0,8},{8,0},{16,24},{24,16},{1,9},{9,1},{17,25},{25,17},{2,10},{10... | collective-permute-start | bytes 393224 | tf_op jit(solution)/shard_map/ppermute | solution.py:49
  7.6 2.6 %collective-permute-start.4 = (bf16[8,8192]{1,0:T(8,128)(2,1)S(1)}, bf16[8,8192]{1,0:T(8,128)(2,1)S(1)}, u32[]{:S(2)}, u32[]{:S(2)}) collective-permute-start(bf16[8,8192]{1,0:T(8,128)(2,1)S(1)} %side_by_side.1.refs_0_), channel_id=1, source_target_pairs={{0,16},{8,24},{16,0},{24,8},{1,17},{9,25},{17,1},{25,9},{2,18},{10... | collective-permute-start | bytes 393224 | tf_op jit(solution)/shard_map/ppermute | solution.py:49
  10.2 0.2 collective-permute-start.5
  10.4 0.7 add_add_fusion
  11.2 0.7 pad_add_fusion
  11.9 4.3 %dense.2 = (bf16[4096,1792]{1,0:T(8,128)(2,1)S(1)}, bf16[8,8192]{1,0:T(8,128)(2,1)S(1)}) custom-call(s32[1,224]{1,0:T(1,128)} %index_hbm.3, bf16[224,128,128]{2,1,0:T(8,128)(2,1)} %blocks.2, bf16[8,8192]{1,0:T(8,128)(2,1)S(1)} %side_by_side.1.refs_0_), custom_call_target="tpu_custom_call" | custom-call | tf_op jit(solution)/shard_map/dense/pallas_call | solution.py:180
  16.2 0.2 select_reduce_fusion
  16.4 0.3 collective-permute-start.2
  16.8 3.2 %collective-permute-done.4.refs_1_ = bf16[8,8192]{1,0:T(8,128)(2,1)S(1)} collective-permute-done((bf16[8,8192]{1,0:T(8,128)(2,1)S(1)}, bf16[8,8192]{1,0:T(8,128)(2,1)S(1)}, u32[]{:S(2)}, u32[]{:S(2)}) %collective-permute-start.4) | collective-permute-done | bytes 131104 | tf_op jit(solution)/shard_map/ppermute | solution.py:49
  20.0 1.4 %copy-done = bf16[4096,1792]{1,0:T(8,128)(2,1)} copy-done((bf16[4096,1792]{1,0:T(8,128)(2,1)}, bf16[4096,1792]{1,0:T(8,128)(2,1)S(1)}, u32[]{:S(2)}) %copy-start) | copy-done | bytes 14680088
  21.4 4.1 %dense.3.refs_4_.refs_2_.refs_8_ = bf16[4096,1792]{1,0:T(8,128)(2,1)S(1)} custom-call(s32[1,224]{1,0:T(1,128)} %index_hbm.4, bf16[224,128,128]{2,1,0:T(8,128)(2,1)} %blocks.3, s32[3,70]{1,0:T(4,128)S(1)} %broadcast_add_fusion.refs_0_.spots, bf16[24,8192]{1,0:T(8,128)(2,1)S(1)} %pack.2.refs_1_.refs_0_), custom_call_target="tpu_custom_call" | custom-call | tf_op jit(solution)/shard_map/dense/pallas_call | solution.py:180
  25.7 0.6 collective-permute-start.11
  26.3 0.3 collective-permute-start.12
  26.6 2.7 %collective-permute-start.13 = (bf16[24,8192]{1,0:T(8,128)(2,1)S(1)}, bf16[24,8192]{1,0:T(8,128)(2,1)S(1)}, u32[]{:S(2)}, u32[]{:S(2)}) collective-permute-start(bf16[24,8192]{1,0:T(8,128)(2,1)S(1)} %pack.2.refs_1_.refs_0_), channel_id=1, source_target_pairs={{0,6},{1,7},{2,4},{3,5},{4,2},{5,3},{6,0},{7,1},{8,14},{9,15},{10,... | collective-permute-start | bytes 1179656 | tf_op jit(solution)/shard_map/ppermute | solution.py:49
  29.3 1.4 %copy-done.1 = bf16[4096,1792]{1,0:T(8,128)(2,1)S(1)} copy-done((bf16[4096,1792]{1,0:T(8,128)(2,1)S(1)}, bf16[4096,1792]{1,0:T(8,128)(2,1)}, u32[]{:S(2)}) %copy-start.1) | copy-done | bytes 14680088
  30.7 26.3 %own_pass.1 = (bf16[64,1792]{1,0:T(8,128)(2,1)S(1)}, bf16[64,1792]{1,0:T(8,128)(2,1)S(1)}, bf16[64,1792]{1,0:T(8,128)(2,1)S(1)}, bf16[64,8192]{1,0:T(8,128)(2,1)...) custom-call(s32[1,224]{1,0:T(1,128)} %index_hbm.5, ...), custom_call_target="tpu_custom_call" | custom-call | flops 5637144576 | bytes 14680064 | tf_op jit(solution)/shard_map/own_pass/pallas_call | solution.py:313
  57.2 0.5 collective-permute-start.14
  57.7 0.1 collective-permute-start.15
  57.7 0.4 collective-permute-start.16
  58.2 0.1 collective-permute-start.17
  58.2 0.8 collective-permute-done.7.refs_1_
  59.0 0.2 add_and_cut.1
  59.2 0.3 collective-permute-start.10
  59.5 0.1 collective-permute-done.14.refs_4_
  59.6 1.7 %collective-permute-start.9 = (bf16[8,8192]{1,0:T(8,128)(2,1)S(1)}, bf16[8,8192]{1,0:T(8,128)(2,1)S(1)}, u32[]{:S(2)}, u32[]{:S(2)}) collective-permute-start(bf16[8,8192]{1,0:T(8,128)(2,1)S(1)} %get-tuple-element.31), channel_id=1, source_target_pairs={{0,4},{1,5},{2,6},{3,7},{4,0},{5,1},{6,2},{7,3},{8,12},{9,13},{10,... | collective-permute-start | bytes 393224 | tf_op jit(solution)/shard_map/ppermute | solution.py:49
  61.3 1.5 %collective-permute-start.8 = (bf16[8,8192]{1,0:T(8,128)(2,1)S(1)}, bf16[8,8192]{1,0:T(8,128)(2,1)S(1)}, u32[]{:S(2)}, u32[]{:S(2)}) collective-permute-start(bf16[8,8192]{1,0:T(8,128)(2,1)S(1)} %get-tuple-element.30), channel_id=1, source_target_pairs={{0,2},{1,3},{2,0},{3,1},{4,6},{5,7},{6,4},{7,5},{8,10},{9,11},{10,... | collective-permute-start | bytes 393224 | tf_op jit(solution)/shard_map/ppermute | solution.py:49
  62.8 14.2 %rest_acts.1 = (bf16[192,1792]{1,0:T(8,128)(2,1)S(1)}, bf16[192,1792]{1,0:T(8,128)(2,1)S(1)}, bf16[192,1792]{1,0:T(8,128)(2,1)S(1)}, bf16[192,8192]{1,0:T(8,128)(2,1)S(1)}) custom-call(bf16[24,8192]{1,0:T(8,128)(2,1)S(1)} %pack.2.refs_1_.refs_0_, bf16[24,8192]{1,0:T(8,128)(2,1)S(1)} %collective-permute-done.11.refs_1_, ...), custom_call_target="tpu_custom_call" | custom-call | flops 8455716864 | bytes 14680064 | tf_op jit(solution)/shard_map/rest_acts/pallas_call | solution.py:228
  77.0 12.6 %grads.1 = (f32[70,128,128]{2,1,0:T(8,128)}, f32[70,128,128]{2,1,0:T(8,128)}, f32[70,128,128]{2,1,0:T(8,128)}) custom-call(s32[3,70]{1,0:T(4,128)S(1)} %broadcast_add_fusion.refs_0_.spots, bf16[64,8192]{1,0:T(8,128)(2,1)S(1)} %get-tuple-element.33.own, bf16[192,8192]{1,0:T(8,128)(2,1)S(1)} %get-tuple-element.35.rest, ...), custom_call_target="tpu_custom_call" | custom-call | flops 1761607680 | bytes 13762560 | tf_op jit(solution)/shard_map/grads/pallas_call | solution.py:395
  89.7 0.7 fusion
  (24 shorter events, 0.4 us)
Async XLA Ops:
  1.5 24.0 %collective-permute-start = (bf16[8,8192]{1,0:T(8,128)(2,1)S(1)}, bf16[8,8192]{1,0:T(8,128)(2,1)S(1)}, u32[]{:S(2)}, u32[]{:S(2)}) collective-permute-start(bf16[8,8192]{1,0:T(8,128)(2,1)S(1)} %side_by_side.1.refs_0_), channel_id=1, source_target_pairs={{0,2},{1,3},{2,0},{3,1},{4,6},{5,7},{6,4},{7,5},{8,10},{9,11},{10,... | collective-permute-start | bytes 393224 | tf_op jit(solution)/shard_map/ppermute | solution.py:49
  4.5 21.0 %collective-permute-start.1 = (bf16[8,8192]{1,0:T(8,128)(2,1)S(1)}, bf16[8,8192]{1,0:T(8,128)(2,1)S(1)}, u32[]{:S(2)}, u32[]{:S(2)}) collective-permute-start(bf16[8,8192]{1,0:T(8,128)(2,1)S(1)} %side_by_side.1.refs_0_), channel_id=1, source_target_pairs={{0,4},{1,5},{2,6},{3,7},{4,0},{5,1},{6,2},{7,3},{8,12},{9,13},{10,... | collective-permute-start | bytes 393224 | tf_op jit(solution)/shard_map/ppermute | solution.py:49
  6.1 10.4 %collective-permute-start.3 = (bf16[8,8192]{1,0:T(8,128)(2,1)S(1)}, bf16[8,8192]{1,0:T(8,128)(2,1)S(1)}, u32[]{:S(2)}, u32[]{:S(2)}) collective-permute-start(bf16[8,8192]{1,0:T(8,128)(2,1)S(1)} %side_by_side.1.refs_0_), channel_id=1, source_target_pairs={{0,8},{8,0},{16,24},{24,16},{1,9},{9,1},{17,25},{25,17},{2,10},{10... | collective-permute-start | bytes 393224 | tf_op jit(solution)/shard_map/ppermute | solution.py:49
  7.6 12.4 %collective-permute-start.4 = (bf16[8,8192]{1,0:T(8,128)(2,1)S(1)}, bf16[8,8192]{1,0:T(8,128)(2,1)S(1)}, u32[]{:S(2)}, u32[]{:S(2)}) collective-permute-start(bf16[8,8192]{1,0:T(8,128)(2,1)S(1)} %side_by_side.1.refs_0_), channel_id=1, source_target_pairs={{0,16},{8,24},{16,0},{24,8},{1,17},{9,25},{17,1},{25,9},{2,18},{10... | collective-permute-start | bytes 393224 | tf_op jit(solution)/shard_map/ppermute | solution.py:49
  10.2 9.8 %collective-permute-start.5 = (bf16[8,8192]{1,0:T(8,128)(2,1)S(1)}, bf16[8,8192]{1,0:T(8,128)(2,1)S(1)}, u32[]{:S(2)}, u32[]{:S(2)}) collective-permute-start(bf16[8,8192]{1,0:T(8,128)(2,1)S(1)} %side_by_side.1.refs_0_), channel_id=1, source_target_pairs={{0,24},{8,16},{16,8},{24,0},{1,25},{9,17},{17,9},{25,1},{2,26},{10... | collective-permute-start | bytes 393224 | tf_op jit(solution)/shard_map/ppermute | solution.py:49
  16.2 5.2 %copy-start = (bf16[4096,1792]{1,0:T(8,128)(2,1)}, bf16[4096,1792]{1,0:T(8,128)(2,1)S(1)}, u32[]{:S(2)}) copy-start(bf16[4096,1792]{1,0:T(8,128)(2,1)S(1)} %get-tuple-element.26.refs_3_.refs_9_) | copy-start | bytes 44040196
  16.4 9.2 %collective-permute-start.2 = (bf16[8,8192]{1,0:T(8,128)(2,1)S(1)}, bf16[8,8192]{1,0:T(8,128)(2,1)S(1)}, u32[]{:S(2)}, u32[]{:S(2)}) collective-permute-start(bf16[8,8192]{1,0:T(8,128)(2,1)S(1)} %get-tuple-element.25), channel_id=1, source_target_pairs={{0,6},{1,7},{2,4},{3,5},{4,2},{5,3},{6,0},{7,1},{8,14},{9,15},{10,... | collective-permute-start | bytes 393224 | tf_op jit(solution)/shard_map/ppermute | solution.py:49
  25.5 5.2 %copy-start.1 = (bf16[4096,1792]{1,0:T(8,128)(2,1)S(1)}, bf16[4096,1792]{1,0:T(8,128)(2,1)}, u32[]{:S(2)}) copy-start(bf16[4096,1792]{1,0:T(8,128)(2,1)} %copy-done) | copy-start | bytes 44040196
  25.7 3.6 %collective-permute-start.6 = (bf16[32,8192]{1,0:T(8,128)(2,1)S(1)}, bf16[32,8192]{1,0:T(8,128)(2,1)S(1)}, u32[]{:S(2)}, u32[]{:S(2)}) collective-permute-start(bf16[32,8192]{1,0:T(8,128)(2,1)S(1)} %pack.3.refs_0_), channel_id=1, source_target_pairs={{0,1},{1,0},{2,3},{3,2},{4,5},{5,4},{6,7},{7,6},{8,9},{9,8},{10,11... | collective-permute-start | bytes 1572872 | tf_op jit(solution)/shard_map/ppermute | solution.py:49
  25.7 31.9 %collective-permute-start.11 = (bf16[24,8192]{1,0:T(8,128)(2,1)S(1)}, bf16[24,8192]{1,0:T(8,128)(2,1)S(1)}, u32[]{:S(2)}, u32[]{:S(2)}) collective-permute-start(bf16[24,8192]{1,0:T(8,128)(2,1)S(1)} %pack.2.refs_1_.refs_0_), channel_id=1, source_target_pairs={{0,2},{1,3},{2,0},{3,1},{4,6},{5,7},{6,4},{7,5},{8,10},{9,11},{10,... | collective-permute-start | bytes 1179656 | tf_op jit(solution)/shard_map/ppermute | solution.py:49
  26.3 31.4 %collective-permute-start.12 = (bf16[24,8192]{1,0:T(8,128)(2,1)S(1)}, bf16[24,8192]{1,0:T(8,128)(2,1)S(1)}, u32[]{:S(2)}, u32[]{:S(2)}) collective-permute-start(bf16[24,8192]{1,0:T(8,128)(2,1)S(1)} %pack.2.refs_1_.refs_0_), channel_id=1, source_target_pairs={{0,4},{1,5},{2,6},{3,7},{4,0},{5,1},{6,2},{7,3},{8,12},{9,13},{10,... | collective-permute-start | bytes 1179656 | tf_op jit(solution)/shard_map/ppermute | solution.py:49
  26.6 31.5 %collective-permute-start.13 = (bf16[24,8192]{1,0:T(8,128)(2,1)S(1)}, bf16[24,8192]{1,0:T(8,128)(2,1)S(1)}, u32[]{:S(2)}, u32[]{:S(2)}) collective-permute-start(bf16[24,8192]{1,0:T(8,128)(2,1)S(1)} %pack.2.refs_1_.refs_0_), channel_id=1, source_target_pairs={{0,6},{1,7},{2,4},{3,5},{4,2},{5,3},{6,0},{7,1},{8,14},{9,15},{10,... | collective-permute-start | bytes 1179656 | tf_op jit(solution)/shard_map/ppermute | solution.py:49
  57.1 2.0 %collective-permute-start.7 = (bf16[32,8192]{1,0:T(8,128)(2,1)S(1)}, bf16[32,8192]{1,0:T(8,128)(2,1)S(1)}, u32[]{:S(2)}, u32[]{:S(2)}) collective-permute-start(bf16[32,8192]{1,0:T(8,128)(2,1)S(1)} %get-tuple-element.28), channel_id=1, source_target_pairs={{0,1},{1,0},{2,3},{3,2},{4,5},{5,4},{6,7},{7,6},{8,9},{9,8},{10,11... | collective-permute-start | bytes 1572872 | tf_op jit(solution)/shard_map/ppermute | solution.py:49
  57.2 2.5 %collective-permute-start.14 = (bf16[24,8192]{1,0:T(8,128)(2,1)S(1)}, bf16[24,8192]{1,0:T(8,128)(2,1)S(1)}, u32[]{:S(2)}, u32[]{:S(2)}) collective-permute-start(bf16[24,8192]{1,0:T(8,128)(2,1)S(1)} %pack.2.refs_1_.refs_0_), channel_id=1, source_target_pairs={{0,1},{1,0},{2,3},{3,2},{4,5},{5,4},{6,7},{7,6},{8,9},{9,8},{10,11... | collective-permute-start | bytes 1179656 | tf_op jit(solution)/shard_map/ppermute | solution.py:49
  57.7 3.6 %collective-permute-start.15 = (bf16[24,8192]{1,0:T(8,128)(2,1)S(1)}, bf16[24,8192]{1,0:T(8,128)(2,1)S(1)}, u32[]{:S(2)}, u32[]{:S(2)}) collective-permute-start(bf16[24,8192]{1,0:T(8,128)(2,1)S(1)} %collective-permute-done.11.refs_1_), channel_id=1, source_target_pairs={{0,1},{1,0},{2,3},{3,2},{4,5},{5,4},{6,7},{7,6},{8,9},{9,8},{10,11... | collective-permute-start | bytes 1179656 | tf_op jit(solution)/shard_map/ppermute | solution.py:49
  57.7 5.0 %collective-permute-start.16 = (bf16[24,8192]{1,0:T(8,128)(2,1)S(1)}, bf16[24,8192]{1,0:T(8,128)(2,1)S(1)}, u32[]{:S(2)}, u32[]{:S(2)}) collective-permute-start(bf16[24,8192]{1,0:T(8,128)(2,1)S(1)} %collective-permute-done.12.refs_2_), channel_id=1, source_target_pairs={{0,1},{1,0},{2,3},{3,2},{4,5},{5,4},{6,7},{7,6},{8,9},{9,8},{10,11... | collective-permute-start | bytes 1179656 | tf_op jit(solution)/shard_map/ppermute | solution.py:49
  58.2 4.6 %collective-permute-start.17 = (bf16[24,8192]{1,0:T(8,128)(2,1)S(1)}, bf16[24,8192]{1,0:T(8,128)(2,1)S(1)}, u32[]{:S(2)}, u32[]{:S(2)}) collective-permute-start(bf16[24,8192]{1,0:T(8,128)(2,1)S(1)} %collective-permute-done.13.refs_3_), channel_id=1, source_target_pairs={{0,1},{1,0},{2,3},{3,2},{4,5},{5,4},{6,7},{7,6},{8,9},{9,8},{10,11... | collective-permute-start | bytes 1179656 | tf_op jit(solution)/shard_map/ppermute | solution.py:49
  59.2 30.4 %collective-permute-start.10 = (bf16[8,8192]{1,0:T(8,128)(2,1)S(1)}, bf16[8,8192]{1,0:T(8,128)(2,1)S(1)}, u32[]{:S(2)}, u32[]{:S(2)}) collective-permute-start(bf16[8,8192]{1,0:T(8,128)(2,1)S(1)} %get-tuple-element.32), channel_id=1, source_target_pairs={{0,6},{1,7},{2,4},{3,5},{4,2},{5,3},{6,0},{7,1},{8,14},{9,15},{10,... | collective-permute-start | bytes 393224 | tf_op jit(solution)/shard_map/ppermute | solution.py:49
  59.6 30.0 %collective-permute-start.9 = (bf16[8,8192]{1,0:T(8,128)(2,1)S(1)}, bf16[8,8192]{1,0:T(8,128)(2,1)S(1)}, u32[]{:S(2)}, u32[]{:S(2)}) collective-permute-start(bf16[8,8192]{1,0:T(8,128)(2,1)S(1)} %get-tuple-element.31), channel_id=1, source_target_pairs={{0,4},{1,5},{2,6},{3,7},{4,0},{5,1},{6,2},{7,3},{8,12},{9,13},{10,... | collective-permute-start | bytes 393224 | tf_op jit(solution)/shard_map/ppermute | solution.py:49
  61.3 28.3 %collective-permute-start.8 = (bf16[8,8192]{1,0:T(8,128)(2,1)S(1)}, bf16[8,8192]{1,0:T(8,128)(2,1)S(1)}, u32[]{:S(2)}, u32[]{:S(2)}) collective-permute-start(bf16[8,8192]{1,0:T(8,128)(2,1)S(1)} %get-tuple-element.30), channel_id=1, source_target_pairs={{0,2},{1,3},{2,0},{3,1},{4,6},{5,7},{6,4},{7,5},{8,10},{9,11},{10,... | collective-permute-start | bytes 393224 | tf_op jit(solution)/shard_map/ppermute | solution.py:49

commit v4 on v3

--- a/solution.py
+++ b/solution.py
@@ -286,7 +286,7 @@
 
     lax.fori_loop(0, steps, grad, 0)
     half = part.shape[0]
-    wide = 512
+    wide = 1024
 
     def sums(n, carry):
         out = pl.ds(pl.multiple_of(n * wide, wide), wide)
@@ -334,12 +334,11 @@
 
 
 def grads_body(
-    factor, size, spots, own, rest, hid0, hid1, gp0, gp1, up0, up1,
-    gate_out, up_out, down_out, tok_t, hid_t,
+    factor, size, group, spots, own, rest, hid0, hid1, gp0, gp1, up0, up1,
+    gate_out, up_out, down_out, tok_t, hid_t, gate_buf, up_buf, down_buf, sem,
 ):
-    i = pl.program_id(0)
-    steps = pl.num_programs(0) // 2
-    per_step = gate_out.shape[0]
+    cap = spots.shape[1]
+    groups = cap // group
     d_cols = tok_t.shape[0]
     ff_cols = hid_t.shape[0]
     width = d_cols * size
@@ -348,59 +347,70 @@
         cols = pl.ds(pl.multiple_of(start, size), size)
         return jnp.concatenate([first[:, cols], second[:, cols]], axis=0)
 
-    def one(which, left, first, second, base, out, cols, at, j):
-        spot = spots[which, at * per_step + j]
+    def one(which, left, first, second, base, buf, cols, slot):
+        spot = spots[which, slot]
         b = jnp.maximum(spot, 0)
         r = lax.shift_right_logical(b * (2**16 // cols + 1), 16)
         c = b - r * cols
         value = dot_nn(left[r], column(first, second, base + c * size)) * factor
-        out[j] = jnp.where(spot >= 0, value, 0.0)
-
-    @pl.when(i == 0)
-    def _():
-        def step(n, carry):
-            hid_t[n] = column(hid0, hid1, n * size).T
-            return carry
-
-        lax.fori_loop(0, ff_cols, step, 0)
-
-    @pl.when(i < steps)
-    def _():
-        turns = -(-d_cols // (spots.shape[1] // per_step))
-        for j in range(max(per_step, turns)):
+        buf[slot] = jnp.where(spot >= 0, value, 0.0)
+
+    def send(buf, out, slot, i):
+        part = pl.ds(i * group, group)
+        pltpu.make_async_copy(buf.at[part], out.at[part], sem.at[slot]).start()
+
+    def turn_hidden(n, carry):
+        hid_t[n] = column(hid0, hid1, n * size).T
+        return carry
+
+    lax.fori_loop(0, ff_cols, turn_hidden, 0)
+    turns = -(-d_cols // groups)
+
+    def down_step(i, carry):
+        for j in range(max(group, turns)):
             if j < turns:
                 n = jnp.minimum(i * turns + j, d_cols - 1)
                 tok_t[n] = column(own, rest, n * size).T
-            if j < per_step:
-                one(2, hid_t, own, rest, width, down_out, d_cols, i, j)
-
-    @pl.when(i >= steps)
-    def _():
-        for j in range(per_step):
-            one(0, tok_t, gp0, gp1, 0, gate_out, ff_cols, i - steps, j)
-            one(1, tok_t, up0, up1, 0, up_out, ff_cols, i - steps, j)
+            if j < group:
+                one(2, hid_t, own, rest, width, down_buf, d_cols, i * group + j)
+        send(down_buf, down_out, 2, i)
+        return carry
+
+    lax.fori_loop(0, groups, down_step, 0)
+
+    def step(i, carry):
+        for j in range(group):
+            one(0, tok_t, gp0, gp1, 0, gate_buf, ff_cols, i * group + j)
+            one(1, tok_t, up0, up1, 0, up_buf, ff_cols, i * group + j)
+        send(gate_buf, gate_out, 0, i)
+        send(up_buf, up_out, 1, i)
+        return carry
+
+    lax.fori_loop(0, groups, step, 0)
+    for slot, (buf, out) in enumerate(((gate_buf, gate_out), (up_buf, up_out), (down_buf, down_out))):
+        pltpu.make_async_copy(buf, out, sem.at[slot]).wait()
 
 
 def grads(spots, own, rest, acts0, acts1, size, cap, factor):
-    per_step = max(n for n in range(1, 18) if cap % n == 0)
-    per_step = 10 if cap % 10 == 0 else per_step
-    steps = cap // per_step
+    group = max(n for n in range(1, 18) if cap % n == 0)
     width = own.shape[1] // 2
     hidden = acts0[0].shape[1]
     rows = own.shape[0] + rest.shape[0]
     out = jax.ShapeDtypeStruct((cap, size, size), F32)
-    early = pl.BlockSpec((per_step, size, size), lambda i: (jnp.minimum(i, steps - 1), 0, 0))
-    late = pl.BlockSpec((per_step, size, size), lambda i: (jnp.maximum(i - steps, 0), 0, 0))
-    need = rows * (6 * width + 8 * hidden) + per_step * 6 * size * size * 4
-    return pl.pallas_call(
-        functools.partial(grads_body, factor, size),
+    buf = VMEM((cap, size, size), F32)
+    need = rows * (6 * width + 8 * hidden) + cap * 12 * size * size
+    return pl.pallas_call(
+        functools.partial(grads_body, factor, size, group),
         out_shape=(out, out, out),
-        grid=(2 * steps,),
         in_specs=[SMEM_SPEC] + [in_vmem()] * 8,
-        out_specs=(late, late, early),
+        out_specs=(HBM_SPEC,) * 3,
         scratch_shapes=[
             VMEM((width // size, size, rows), BF16),
             VMEM((hidden // size, size, rows), BF16),
+            buf,
+            buf,
+            buf,
+            pltpu.SemaphoreType.DMA((3,)),
         ],
         compiler_params=pltpu.CompilerParams(vmem_limit_bytes=need + 2**21),
         cost_estimate=pl.CostEstimate(

time: 90.8 us -> 86.2 us (0.949)
  Pallas kernels: 62.7 us -> 58.1 us
    pallas_call x1, Pallas kernels: 12.6 us -> 8.7 us  [grads(): pl.pallas_call(functools.partial(grads_body, factor, size, group), out_sh...]
  transfers between devices with their start and end apart: 18 -> 18, of which waited for: 3 -> 3; matrix products, arithmetic and copies ran while one was open for 2% -> 2% of each run, Pallas kernels for 68% -> 67%
where the time goes in v4:
time: 86.2 us; the launch traced here: 85.7 us
  Pallas kernels  58.1 us (67%)
  starting transfers between devices  17.5 us (20%)
  waiting for transfers between devices  4.16 us (5%)
  local copies, waits for them, and re-layouts  3.46 us (4%)
  other arithmetic  1.73 us (2%)
    pallas_call x1, Pallas kernels, own_pass(): pl.pallas_call(functools.partial(own_body, len(pieces)), out_shape=(act,...  25.8 us
    ppermute x18, starting transfers between devices, exchange(): return lax.ppermute(x, axis, [(i, i ^ flip) for i in range(count)])  17.5 us
    pallas_call x1, Pallas kernels, acts_pass(): pl.pallas_call(functools.partial(acts_body, len(pieces)), out_shape=(act,...  14 us
    pallas_call x1, Pallas kernels, grads(): pl.pallas_call(functools.partial(grads_body, factor, size, group), out_sh...  8.7 us
    pallas_call x2, Pallas kernels, dense(): pl.pallas_call(functools.partial(dense_body, bool(again)), out_shape=outs...  8.41 us
    ppermute x18, waiting for transfers between devices, exchange(): return lax.ppermute(x, axis, [(i, i ^ flip) for i in range(count)])  4.16 us
    unnamed x4, local copies, waits for them, and re-layouts  2.8 us
  transfers between devices with their start and end apart: 18, of which 3 were waited for; matrix products, arithmetic and copies ran while one was open for 2% of the time, Pallas kernels for 67%

profile of v4, /device:TPU:0, one launch (start us, length us, event | category | flops | bytes accessed | tf_op | source)
XLA Modules:
  0.0 85.7 jit_solution(9113251467365108371)
XLA Ops:
  0.6 0.9 %side_by_side.1.refs_0_ = bf16[8,8192]{1,0:T(8,128)(2,1)S(1)} custom-call(bf16[8,4096]{1,0:T(8,128)(2,1)} %left_ref.1, bf16[8,4096]{1,0:T(8,128)(2,1)} %right_ref.1), custom_call_target="tpu_custom_call" | custom-call | tf_op jit(solution)/shard_map/side_by_side/pallas_call | solution.py:95
  1.5 3.0 %collective-permute-start = (bf16[8,8192]{1,0:T(8,128)(2,1)S(1)}, bf16[8,8192]{1,0:T(8,128)(2,1)S(1)}, u32[]{:S(2)}, u32[]{:S(2)}) collective-permute-start(bf16[8,8192]{1,0:T(8,128)(2,1)S(1)} %side_by_side.1.refs_0_), channel_id=1, source_target_pairs={{0,2},{1,3},{2,0},{3,1},{4,6},{5,7},{6,4},{7,5},{8,10},{9,11},{10,... | collective-permute-start | bytes 393224 | tf_op jit(solution)/shard_map/ppermute | solution.py:49
  4.5 1.5 %collective-permute-start.1 = (bf16[8,8192]{1,0:T(8,128)(2,1)S(1)}, bf16[8,8192]{1,0:T(8,128)(2,1)S(1)}, u32[]{:S(2)}, u32[]{:S(2)}) collective-permute-start(bf16[8,8192]{1,0:T(8,128)(2,1)S(1)} %side_by_side.1.refs_0_), channel_id=1, source_target_pairs={{0,4},{1,5},{2,6},{3,7},{4,0},{5,1},{6,2},{7,3},{8,12},{9,13},{10,... | collective-permute-start | bytes 393224 | tf_op jit(solution)/shard_map/ppermute | solution.py:49
  6.1 1.6 %collective-permute-start.3 = (bf16[8,8192]{1,0:T(8,128)(2,1)S(1)}, bf16[8,8192]{1,0:T(8,128)(2,1)S(1)}, u32[]{:S(2)}, u32[]{:S(2)}) collective-permute-start(bf16[8,8192]{1,0:T(8,128)(2,1)S(1)} %side_by_side.1.refs_0_), channel_id=1, source_target_pairs={{0,8},{8,0},{16,24},{24,16},{1,9},{9,1},{17,25},{25,17},{2,10},{10... | collective-permute-start | bytes 393224 | tf_op jit(solution)/shard_map/ppermute | solution.py:49
  7.6 2.6 %collective-permute-start.4 = (bf16[8,8192]{1,0:T(8,128)(2,1)S(1)}, bf16[8,8192]{1,0:T(8,128)(2,1)S(1)}, u32[]{:S(2)}, u32[]{:S(2)}) collective-permute-start(bf16[8,8192]{1,0:T(8,128)(2,1)S(1)} %side_by_side.1.refs_0_), channel_id=1, source_target_pairs={{0,16},{8,24},{16,0},{24,8},{1,17},{9,25},{17,1},{25,9},{2,18},{10... | collective-permute-start | bytes 393224 | tf_op jit(solution)/shard_map/ppermute | solution.py:49
  10.2 0.2 collective-permute-start.5
  10.4 0.7 add_add_fusion
  11.2 0.7 pad_add_fusion
  11.9 4.3 %dense.2 = (bf16[4096,1792]{1,0:T(8,128)(2,1)S(1)}, bf16[8,8192]{1,0:T(8,128)(2,1)S(1)}) custom-call(s32[1,224]{1,0:T(1,128)} %index_hbm.3, bf16[224,128,128]{2,1,0:T(8,128)(2,1)} %blocks.2, bf16[8,8192]{1,0:T(8,128)(2,1)S(1)} %side_by_side.1.refs_0_), custom_call_target="tpu_custom_call" | custom-call | tf_op jit(solution)/shard_map/dense/pallas_call | solution.py:180
  16.2 0.2 select_reduce_fusion
  16.4 0.3 collective-permute-start.2
  16.8 3.2 %collective-permute-done.4.refs_1_ = bf16[8,8192]{1,0:T(8,128)(2,1)S(1)} collective-permute-done((bf16[8,8192]{1,0:T(8,128)(2,1)S(1)}, bf16[8,8192]{1,0:T(8,128)(2,1)S(1)}, u32[]{:S(2)}, u32[]{:S(2)}) %collective-permute-start.4) | collective-permute-done | bytes 131104 | tf_op jit(solution)/shard_map/ppermute | solution.py:49
  20.0 1.4 %copy-done = bf16[4096,1792]{1,0:T(8,128)(2,1)} copy-done((bf16[4096,1792]{1,0:T(8,128)(2,1)}, bf16[4096,1792]{1,0:T(8,128)(2,1)S(1)}, u32[]{:S(2)}) %copy-start) | copy-done | bytes 14680088
  21.4 4.1 %dense.3.refs_4_.refs_2_.refs_8_ = bf16[4096,1792]{1,0:T(8,128)(2,1)S(1)} custom-call(s32[1,224]{1,0:T(1,128)} %index_hbm.4, bf16[224,128,128]{2,1,0:T(8,128)(2,1)} %blocks.3, s32[3,70]{1,0:T(4,128)S(1)} %broadcast_add_fusion.refs_0_.spots, bf16[24,8192]{1,0:T(8,128)(2,1)S(1)} %pack.2.refs_1_.refs_0_), custom_call_target="tpu_custom_call" | custom-call | tf_op jit(solution)/shard_map/dense/pallas_call | solution.py:180
  25.7 0.6 collective-permute-start.11
  26.3 0.3 collective-permute-start.12
  26.6 2.7 %collective-permute-start.13 = (bf16[24,8192]{1,0:T(8,128)(2,1)S(1)}, bf16[24,8192]{1,0:T(8,128)(2,1)S(1)}, u32[]{:S(2)}, u32[]{:S(2)}) collective-permute-start(bf16[24,8192]{1,0:T(8,128)(2,1)S(1)} %pack.2.refs_1_.refs_0_), channel_id=1, source_target_pairs={{0,6},{1,7},{2,4},{3,5},{4,2},{5,3},{6,0},{7,1},{8,14},{9,15},{10,... | collective-permute-start | bytes 1179656 | tf_op jit(solution)/shard_map/ppermute | solution.py:49
  29.3 1.4 %copy-done.1 = bf16[4096,1792]{1,0:T(8,128)(2,1)S(1)} copy-done((bf16[4096,1792]{1,0:T(8,128)(2,1)S(1)}, bf16[4096,1792]{1,0:T(8,128)(2,1)}, u32[]{:S(2)}) %copy-start.1) | copy-done | bytes 14680088
  30.7 25.8 %own_pass.1 = (bf16[64,1792]{1,0:T(8,128)(2,1)S(1)}, bf16[64,1792]{1,0:T(8,128)(2,1)S(1)}, bf16[64,1792]{1,0:T(8,128)(2,1)S(1)}, bf16[64,8192]{1,0:T(8,128)(2,1)...) custom-call(s32[1,224]{1,0:T(1,128)} %index_hbm.5, ...), custom_call_target="tpu_custom_call" | custom-call | flops 5637144576 | bytes 14680064 | tf_op jit(solution)/shard_map/own_pass/pallas_call | solution.py:313
  56.6 0.5 collective-permute-start.14
  57.1 0.1 collective-permute-start.15
  57.2 0.4 collective-permute-start.16
  57.6 0.1 collective-permute-start.17
  57.7 0.8 collective-permute-done.7.refs_1_
  58.5 0.2 add_and_cut.1
  58.7 0.3 collective-permute-start.10
  59.0 0.1 collective-permute-done.14.refs_4_
  59.1 1.7 %collective-permute-start.9 = (bf16[8,8192]{1,0:T(8,128)(2,1)S(1)}, bf16[8,8192]{1,0:T(8,128)(2,1)S(1)}, u32[]{:S(2)}, u32[]{:S(2)}) collective-permute-start(bf16[8,8192]{1,0:T(8,128)(2,1)S(1)} %get-tuple-element.31), channel_id=1, source_target_pairs={{0,4},{1,5},{2,6},{3,7},{4,0},{5,1},{6,2},{7,3},{8,12},{9,13},{10,... | collective-permute-start | bytes 393224 | tf_op jit(solution)/shard_map/ppermute | solution.py:49
  60.7 1.5 %collective-permute-start.8 = (bf16[8,8192]{1,0:T(8,128)(2,1)S(1)}, bf16[8,8192]{1,0:T(8,128)(2,1)S(1)}, u32[]{:S(2)}, u32[]{:S(2)}) collective-permute-start(bf16[8,8192]{1,0:T(8,128)(2,1)S(1)} %get-tuple-element.30), channel_id=1, source_target_pairs={{0,2},{1,3},{2,0},{3,1},{4,6},{5,7},{6,4},{7,5},{8,10},{9,11},{10,... | collective-permute-start | bytes 393224 | tf_op jit(solution)/shard_map/ppermute | solution.py:49
  62.2 14.0 %rest_acts.1 = (bf16[192,1792]{1,0:T(8,128)(2,1)S(1)}, bf16[192,1792]{1,0:T(8,128)(2,1)S(1)}, bf16[192,1792]{1,0:T(8,128)(2,1)S(1)}, bf16[192,8192]{1,0:T(8,128)(2,1)S(1)}) custom-call(bf16[24,8192]{1,0:T(8,128)(2,1)S(1)} %pack.2.refs_1_.refs_0_, bf16[24,8192]{1,0:T(8,128)(2,1)S(1)} %collective-permute-done.11.refs_1_, ...), custom_call_target="tpu_custom_call" | custom-call | flops 8455716864 | bytes 14680064 | tf_op jit(solution)/shard_map/rest_acts/pallas_call | solution.py:228
  76.2 8.7 %grads.1 = (f32[70,128,128]{2,1,0:T(8,128)}, f32[70,128,128]{2,1,0:T(8,128)}, f32[70,128,128]{2,1,0:T(8,128)}) custom-call(s32[3,70]{1,0:T(4,128)S(1)} %broadcast_add_fusion.refs_0_.spots, bf16[64,8192]{1,0:T(8,128)(2,1)S(1)} %get-tuple-element.33.own, bf16[192,8192]{1,0:T(8,128)(2,1)S(1)} %get-tuple-element.35.rest, ...), custom_call_target="tpu_custom_call" | custom-call | flops 1761607680 | bytes 13762560 | tf_op jit(solution)/shard_map/grads/pallas_call | solution.py:402
  85.1 0.7 fusion
  (24 shorter events, 0.4 us)
Async XLA Ops:
  1.5 24.0 %collective-permute-start = (bf16[8,8192]{1,0:T(8,128)(2,1)S(1)}, bf16[8,8192]{1,0:T(8,128)(2,1)S(1)}, u32[]{:S(2)}, u32[]{:S(2)}) collective-permute-start(bf16[8,8192]{1,0:T(8,128)(2,1)S(1)} %side_by_side.1.refs_0_), channel_id=1, source_target_pairs={{0,2},{1,3},{2,0},{3,1},{4,6},{5,7},{6,4},{7,5},{8,10},{9,11},{10,... | collective-permute-start | bytes 393224 | tf_op jit(solution)/shard_map/ppermute | solution.py:49
  4.5 21.0 %collective-permute-start.1 = (bf16[8,8192]{1,0:T(8,128)(2,1)S(1)}, bf16[8,8192]{1,0:T(8,128)(2,1)S(1)}, u32[]{:S(2)}, u32[]{:S(2)}) collective-permute-start(bf16[8,8192]{1,0:T(8,128)(2,1)S(1)} %side_by_side.1.refs_0_), channel_id=1, source_target_pairs={{0,4},{1,5},{2,6},{3,7},{4,0},{5,1},{6,2},{7,3},{8,12},{9,13},{10,... | collective-permute-start | bytes 393224 | tf_op jit(solution)/shard_map/ppermute | solution.py:49
  6.1 10.4 %collective-permute-start.3 = (bf16[8,8192]{1,0:T(8,128)(2,1)S(1)}, bf16[8,8192]{1,0:T(8,128)(2,1)S(1)}, u32[]{:S(2)}, u32[]{:S(2)}) collective-permute-start(bf16[8,8192]{1,0:T(8,128)(2,1)S(1)} %side_by_side.1.refs_0_), channel_id=1, source_target_pairs={{0,8},{8,0},{16,24},{24,16},{1,9},{9,1},{17,25},{25,17},{2,10},{10... | collective-permute-start | bytes 393224 | tf_op jit(solution)/shard_map/ppermute | solution.py:49
  7.6 12.4 %collective-permute-start.4 = (bf16[8,8192]{1,0:T(8,128)(2,1)S(1)}, bf16[8,8192]{1,0:T(8,128)(2,1)S(1)}, u32[]{:S(2)}, u32[]{:S(2)}) collective-permute-start(bf16[8,8192]{1,0:T(8,128)(2,1)S(1)} %side_by_side.1.refs_0_), channel_id=1, source_target_pairs={{0,16},{8,24},{16,0},{24,8},{1,17},{9,25},{17,1},{25,9},{2,18},{10... | collective-permute-start | bytes 393224 | tf_op jit(solution)/shard_map/ppermute | solution.py:49
  10.2 9.8 %collective-permute-start.5 = (bf16[8,8192]{1,0:T(8,128)(2,1)S(1)}, bf16[8,8192]{1,0:T(8,128)(2,1)S(1)}, u32[]{:S(2)}, u32[]{:S(2)}) collective-permute-start(bf16[8,8192]{1,0:T(8,128)(2,1)S(1)} %side_by_side.1.refs_0_), channel_id=1, source_target_pairs={{0,24},{8,16},{16,8},{24,0},{1,25},{9,17},{17,9},{25,1},{2,26},{10... | collective-permute-start | bytes 393224 | tf_op jit(solution)/shard_map/ppermute | solution.py:49
  16.2 5.2 %copy-start = (bf16[4096,1792]{1,0:T(8,128)(2,1)}, bf16[4096,1792]{1,0:T(8,128)(2,1)S(1)}, u32[]{:S(2)}) copy-start(bf16[4096,1792]{1,0:T(8,128)(2,1)S(1)} %get-tuple-element.26.refs_3_.refs_9_) | copy-start | bytes 44040196
  16.4 9.2 %collective-permute-start.2 = (bf16[8,8192]{1,0:T(8,128)(2,1)S(1)}, bf16[8,8192]{1,0:T(8,128)(2,1)S(1)}, u32[]{:S(2)}, u32[]{:S(2)}) collective-permute-start(bf16[8,8192]{1,0:T(8,128)(2,1)S(1)} %get-tuple-element.25), channel_id=1, source_target_pairs={{0,6},{1,7},{2,4},{3,5},{4,2},{5,3},{6,0},{7,1},{8,14},{9,15},{10,... | collective-permute-start | bytes 393224 | tf_op jit(solution)/shard_map/ppermute | solution.py:49
  25.5 5.2 %copy-start.1 = (bf16[4096,1792]{1,0:T(8,128)(2,1)S(1)}, bf16[4096,1792]{1,0:T(8,128)(2,1)}, u32[]{:S(2)}) copy-start(bf16[4096,1792]{1,0:T(8,128)(2,1)} %copy-done) | copy-start | bytes 44040196
  25.7 3.6 %collective-permute-start.6 = (bf16[32,8192]{1,0:T(8,128)(2,1)S(1)}, bf16[32,8192]{1,0:T(8,128)(2,1)S(1)}, u32[]{:S(2)}, u32[]{:S(2)}) collective-permute-start(bf16[32,8192]{1,0:T(8,128)(2,1)S(1)} %pack.3.refs_0_), channel_id=1, source_target_pairs={{0,1},{1,0},{2,3},{3,2},{4,5},{5,4},{6,7},{7,6},{8,9},{9,8},{10,11... | collective-permute-start | bytes 1572872 | tf_op jit(solution)/shard_map/ppermute | solution.py:49
  25.7 31.4 %collective-permute-start.11 = (bf16[24,8192]{1,0:T(8,128)(2,1)S(1)}, bf16[24,8192]{1,0:T(8,128)(2,1)S(1)}, u32[]{:S(2)}, u32[]{:S(2)}) collective-permute-start(bf16[24,8192]{1,0:T(8,128)(2,1)S(1)} %pack.2.refs_1_.refs_0_), channel_id=1, source_target_pairs={{0,2},{1,3},{2,0},{3,1},{4,6},{5,7},{6,4},{7,5},{8,10},{9,11},{10,... | collective-permute-start | bytes 1179656 | tf_op jit(solution)/shard_map/ppermute | solution.py:49
  26.3 30.9 %collective-permute-start.12 = (bf16[24,8192]{1,0:T(8,128)(2,1)S(1)}, bf16[24,8192]{1,0:T(8,128)(2,1)S(1)}, u32[]{:S(2)}, u32[]{:S(2)}) collective-permute-start(bf16[24,8192]{1,0:T(8,128)(2,1)S(1)} %pack.2.refs_1_.refs_0_), channel_id=1, source_target_pairs={{0,4},{1,5},{2,6},{3,7},{4,0},{5,1},{6,2},{7,3},{8,12},{9,13},{10,... | collective-permute-start | bytes 1179656 | tf_op jit(solution)/shard_map/ppermute | solution.py:49
  26.6 31.0 %collective-permute-start.13 = (bf16[24,8192]{1,0:T(8,128)(2,1)S(1)}, bf16[24,8192]{1,0:T(8,128)(2,1)S(1)}, u32[]{:S(2)}, u32[]{:S(2)}) collective-permute-start(bf16[24,8192]{1,0:T(8,128)(2,1)S(1)} %pack.2.refs_1_.refs_0_), channel_id=1, source_target_pairs={{0,6},{1,7},{2,4},{3,5},{4,2},{5,3},{6,0},{7,1},{8,14},{9,15},{10,... | collective-permute-start | bytes 1179656 | tf_op jit(solution)/shard_map/ppermute | solution.py:49
  56.5 2.0 %collective-permute-start.7 = (bf16[32,8192]{1,0:T(8,128)(2,1)S(1)}, bf16[32,8192]{1,0:T(8,128)(2,1)S(1)}, u32[]{:S(2)}, u32[]{:S(2)}) collective-permute-start(bf16[32,8192]{1,0:T(8,128)(2,1)S(1)} %get-tuple-element.28), channel_id=1, source_target_pairs={{0,1},{1,0},{2,3},{3,2},{4,5},{5,4},{6,7},{7,6},{8,9},{9,8},{10,11... | collective-permute-start | bytes 1572872 | tf_op jit(solution)/shard_map/ppermute | solution.py:49
  56.6 2.5 %collective-permute-start.14 = (bf16[24,8192]{1,0:T(8,128)(2,1)S(1)}, bf16[24,8192]{1,0:T(8,128)(2,1)S(1)}, u32[]{:S(2)}, u32[]{:S(2)}) collective-permute-start(bf16[24,8192]{1,0:T(8,128)(2,1)S(1)} %pack.2.refs_1_.refs_0_), channel_id=1, source_target_pairs={{0,1},{1,0},{2,3},{3,2},{4,5},{5,4},{6,7},{7,6},{8,9},{9,8},{10,11... | collective-permute-start | bytes 1179656 | tf_op jit(solution)/shard_map/ppermute | solution.py:49
  57.1 3.6 %collective-permute-start.15 = (bf16[24,8192]{1,0:T(8,128)(2,1)S(1)}, bf16[24,8192]{1,0:T(8,128)(2,1)S(1)}, u32[]{:S(2)}, u32[]{:S(2)}) collective-permute-start(bf16[24,8192]{1,0:T(8,128)(2,1)S(1)} %collective-permute-done.11.refs_1_), channel_id=1, source_target_pairs={{0,1},{1,0},{2,3},{3,2},{4,5},{5,4},{6,7},{7,6},{8,9},{9,8},{10,11... | collective-permute-start | bytes 1179656 | tf_op jit(solution)/shard_map/ppermute | solution.py:49
  57.2 5.0 %collective-permute-start.16 = (bf16[24,8192]{1,0:T(8,128)(2,1)S(1)}, bf16[24,8192]{1,0:T(8,128)(2,1)S(1)}, u32[]{:S(2)}, u32[]{:S(2)}) collective-permute-start(bf16[24,8192]{1,0:T(8,128)(2,1)S(1)} %collective-permute-done.12.refs_2_), channel_id=1, source_target_pairs={{0,1},{1,0},{2,3},{3,2},{4,5},{5,4},{6,7},{7,6},{8,9},{9,8},{10,11... | collective-permute-start | bytes 1179656 | tf_op jit(solution)/shard_map/ppermute | solution.py:49
  57.6 4.6 %collective-permute-start.17 = (bf16[24,8192]{1,0:T(8,128)(2,1)S(1)}, bf16[24,8192]{1,0:T(8,128)(2,1)S(1)}, u32[]{:S(2)}, u32[]{:S(2)}) collective-permute-start(bf16[24,8192]{1,0:T(8,128)(2,1)S(1)} %collective-permute-done.13.refs_3_), channel_id=1, source_target_pairs={{0,1},{1,0},{2,3},{3,2},{4,5},{5,4},{6,7},{7,6},{8,9},{9,8},{10,11... | collective-permute-start | bytes 1179656 | tf_op jit(solution)/shard_map/ppermute | solution.py:49
  58.7 26.3 %collective-permute-start.10 = (bf16[8,8192]{1,0:T(8,128)(2,1)S(1)}, bf16[8,8192]{1,0:T(8,128)(2,1)S(1)}, u32[]{:S(2)}, u32[]{:S(2)}) collective-permute-start(bf16[8,8192]{1,0:T(8,128)(2,1)S(1)} %get-tuple-element.32), channel_id=1, source_target_pairs={{0,6},{1,7},{2,4},{3,5},{4,2},{5,3},{6,0},{7,1},{8,14},{9,15},{10,... | collective-permute-start | bytes 393224 | tf_op jit(solution)/shard_map/ppermute | solution.py:49
  59.1 25.9 %collective-permute-start.9 = (bf16[8,8192]{1,0:T(8,128)(2,1)S(1)}, bf16[8,8192]{1,0:T(8,128)(2,1)S(1)}, u32[]{:S(2)}, u32[]{:S(2)}) collective-permute-start(bf16[8,8192]{1,0:T(8,128)(2,1)S(1)} %get-tuple-element.31), channel_id=1, source_target_pairs={{0,4},{1,5},{2,6},{3,7},{4,0},{5,1},{6,2},{7,3},{8,12},{9,13},{10,... | collective-permute-start | bytes 393224 | tf_op jit(solution)/shard_map/ppermute | solution.py:49
  60.7 24.2 %collective-permute-start.8 = (bf16[8,8192]{1,0:T(8,128)(2,1)S(1)}, bf16[8,8192]{1,0:T(8,128)(2,1)S(1)}, u32[]{:S(2)}, u32[]{:S(2)}) collective-permute-start(bf16[8,8192]{1,0:T(8,128)(2,1)S(1)} %get-tuple-element.30), channel_id=1, source_target_pairs={{0,2},{1,3},{2,0},{3,1},{4,6},{5,7},{6,4},{7,5},{8,10},{9,11},{10,... | collective-permute-start | bytes 393224 | tf_op jit(solution)/shard_map/ppermute | solution.py:49

commit v5 on v4

--- a/solution.py
+++ b/solution.py
@@ -150,89 +150,136 @@
         ).start()
 
 
-def dense_body(again, index_hbm, blocks, *refs):
-    if again:
-        source, dense, copied, index, sem = refs[0], *refs[-4:]
-        copy = pltpu.make_async_copy(source, copied, sem.at[2])
-        copy.start()
-    else:
-        dense, index, sem = refs[-3:]
+def dense_body(index_hbm, blocks, *refs):
+    dense, index, sem = refs[-3:]
     fetch = pltpu.make_async_copy(index_hbm, index, sem.at[1])
     fetch.start()
     dense[...] = jnp.zeros_like(dense)
     fetch.wait()
+    fill_dense(index, blocks, dense, sem.at[0])
+    pltpu.make_async_copy(blocks, blocks, sem.at[0]).wait()
+
+
+def fill_dense(index, blocks, dense, sem):
     kept = blocks.shape[0]
     unroll = 8 if kept % 8 == 0 else 1
 
     def step(i, carry):
-        scatter(index, blocks, dense, sem.at[0], i * unroll, unroll)
+        scatter(index, blocks, dense, sem, i * unroll, unroll)
         return carry
 
     lax.fori_loop(0, kept // unroll, step, 0)
-    if again:
-        copy.wait()
+
+
+def dense_first_body(cap, index_hbm, blocks, source, *refs):
+    lists, (dense, copied, spots, index, rows, sem) = refs[:6], refs[6:]
+    copy = pltpu.make_async_copy(source, copied, sem.at[2])
+    copy.start()
+    fetch = pltpu.make_async_copy(index_hbm, index, sem.at[1])
+    fetch.start()
+    for n, ref in enumerate(lists):
+        pltpu.make_async_copy(ref, rows.at[n], sem.at[3]).start()
+    dense[...] = jnp.zeros_like(dense)
+    fetch.wait()
+    fill_dense(index, blocks, dense, sem.at[0])
+    pltpu.make_async_copy(rows, rows, sem.at[3]).wait()
+    kept = rows.shape[2]
+    room = spots.shape[1]
+    mine = lax.axis_index("dp") * cap + lax.broadcasted_iota(jnp.int32, (room, kept), 0)
+    for n in range(3):
+        held = jnp.where(rows[n] == mine, rows[3 + n] + 1, 0)
+        found = jnp.sum(held, axis=1, keepdims=True) - 1
+        spots[n : n + 1] = jnp.broadcast_to(found, (room, 128)).T[:1]
+    copy.wait()
     pltpu.make_async_copy(blocks, blocks, sem.at[0]).wait()
 
 
-def dense(index, blocks, source, width, hidden, limit, wait_for=()):
-    again = [] if source is None else [source]
-    outs = [VMEM((width, hidden), BF16)] + [VMEM(x.shape, x.dtype) for x in again]
-    return pl.pallas_call(
-        functools.partial(dense_body, bool(again)),
-        out_shape=outs,
-        in_specs=[HBM_SPEC] * 2 + [ANY_SPEC] * (len(again) + len(wait_for)),
-        out_specs=[in_vmem()] * len(outs),
-        scratch_shapes=[pltpu.SMEM(index.shape, jnp.int32), pltpu.SemaphoreType.DMA((3,))],
+def dense_first(index, blocks, source, slots, indexes, cap, width, hidden, limit):
+    return pl.pallas_call(
+        functools.partial(dense_first_body, cap),
+        out_shape=(
+            VMEM((width, hidden), BF16),
+            VMEM(source.shape, source.dtype),
+            jax.ShapeDtypeStruct((3, -(-cap // 128) * 128), jnp.int32),
+        ),
+        in_specs=[HBM_SPEC] * 2 + [ANY_SPEC] + [HBM_SPEC] * 6,
+        out_specs=(in_vmem(),) * 3,
+        scratch_shapes=[
+            pltpu.SMEM(index.shape, jnp.int32),
+            VMEM((6, *index.shape), jnp.int32),
+            pltpu.SemaphoreType.DMA((4,)),
+        ],
+        compiler_params=pltpu.CompilerParams(vmem_limit_bytes=limit),
+        cost_estimate=FREE,
+        name="dense_first",
+    )(in_hbm(index), in_hbm(blocks), source, *(in_hbm(x) for x in (*slots, *indexes)))
+
+
+def dense(index, blocks, width, hidden, limit, wait_for):
+    return pl.pallas_call(
+        dense_body,
+        out_shape=VMEM((width, hidden), BF16),
+        in_specs=[HBM_SPEC] * 2 + [ANY_SPEC] * len(wait_for),
+        out_specs=in_vmem(),
+        scratch_shapes=[pltpu.SMEM(index.shape, jnp.int32), pltpu.SemaphoreType.DMA((2,))],
         compiler_params=pltpu.CompilerParams(vmem_limit_bytes=limit),
         cost_estimate=FREE,
         name="dense",
-    )(in_hbm(index), in_hbm(blocks), *again, *wait_for)
+    )(in_hbm(index), in_hbm(blocks), *wait_for)
 
 
 def chunk_of(hidden):
     return 256 if hidden % 256 == 0 else 128
 
 
-def activations(tok, cot, wg, wu, wd):
-    g = dot_nn(tok[...], wg)
-    u = dot_nn(tok[...], wu)
-    h = dot_nt(cot[...], wd)
-    s = jax.nn.sigmoid(g)
-    hid = (g * s * u).astype(BF16)
-    gp = (h * u * s * (1.0 + g * (1.0 - s))).astype(BF16)
-    up = (h * g * s).astype(BF16)
-    return hid, gp, up
-
-
 def acts_body(count, *refs):
-    pieces, (wg, wu, wd), (hid, gp, up, x) = refs[:count], refs[count : count + 3], refs[-4:]
-    n = pl.program_id(0)
-    width, chunk = wg.shape[0], wd.shape[0]
-
-    @pl.when(n == 0)
-    def _():
-        assemble(pieces, x)
-
-    cols = pl.ds(pl.multiple_of(n * chunk, chunk), chunk)
-    tok, cot = x.at[:, pl.ds(0, width)], x.at[:, pl.ds(width, width)]
-    hid[...], gp[...], up[...] = activations(tok, cot, wg[:, cols], wu[:, cols], wd[...])
+    pieces, (wg, wu, wd_hbm), refs = refs[:count], refs[count : count + 3], refs[count + 3 :]
+    hid, gp, up, x, wd, sem = refs[-6:]
+    width, hidden = wg.shape
+    chunk = wd.shape[1]
+    steps = hidden // chunk
+
+    def place(n):
+        return pl.ds(pl.multiple_of(n * chunk, chunk), chunk)
+
+    def fetch(n):
+        slot = lax.rem(n, 2)
+        return pltpu.make_async_copy(wd_hbm.at[place(n)], wd.at[slot], sem.at[slot])
+
+    fetch(0).start()
+    assemble(pieces, x)
+
+    def step(n, carry):
+        @pl.when(n + 1 < steps)
+        def _():
+            fetch(n + 1).start()
+
+        cols = place(n)
+        g = dot_nn(x[:, :width], wg[:, cols])
+        u = dot_nn(x[:, :width], wu[:, cols])
+        fetch(n).wait()
+        h = dot_nt(x[:, width:], wd[lax.rem(n, 2)])
+        s = jax.nn.sigmoid(g)
+        hid[:, cols] = (g * s * u).astype(BF16)
+        gp[:, cols] = (h * u * s * (1.0 + g * (1.0 - s))).astype(BF16)
+        up[:, cols] = (h * g * s).astype(BF16)
+        return carry
+
+    lax.fori_loop(0, steps, step, 0)
 
 
 def acts_pass(pieces, wg, wu, wd, name, wait_for=()):
     rows = sum(x.shape[0] for x in pieces)
     width, hidden = wg.shape
     chunk = chunk_of(hidden)
-    act = jax.ShapeDtypeStruct((rows, hidden), BF16)
-    piece = pl.BlockSpec((rows, chunk), lambda n: (0, n))
-    need = 84 * rows * chunk + 4 * chunk * width
+    act = VMEM((rows, hidden), BF16)
+    need = 84 * rows * chunk + 4 * chunk * width + 2**20 + (rows > 256) * 18 * 2**20
     return pl.pallas_call(
         functools.partial(acts_body, len(pieces)),
         out_shape=(act, act, act, VMEM((rows, 2 * width), BF16)),
-        grid=(hidden // chunk,),
-        in_specs=[in_vmem()] * (len(pieces) + 2)
-        + [pl.BlockSpec((chunk, width), lambda n: (n, 0))]
-        + [ANY_SPEC] * len(wait_for),
-        out_specs=(piece, piece, piece, in_vmem()),
+        in_specs=[in_vmem()] * (len(pieces) + 2) + [HBM_SPEC] + [ANY_SPEC] * len(wait_for),
+        out_specs=(in_vmem(),) * 4,
+        scratch_shapes=[VMEM((2, chunk, width), BF16), pltpu.SemaphoreType.DMA((2,))],
         compiler_params=pltpu.CompilerParams(vmem_limit_bytes=max(need, 8 * 2**20)),
         cost_estimate=pl.CostEstimate(
             flops=6 * rows * width * hidden, bytes_accessed=2 * width * hidden, transcendentals=0
@@ -334,10 +381,12 @@
 
 
 def grads_body(
-    factor, size, group, spots, own, rest, hid0, hid1, gp0, gp1, up0, up1,
-    gate_out, up_out, down_out, tok_t, hid_t, gate_buf, up_buf, down_buf, sem,
+    factor, size, group, spots, own, rest, hid0, hid1, gp0, gp1, up0, up1, *refs
 ):
-    cap = spots.shape[1]
+    sums = refs[:-11]
+    layer, token_grad, gate_out, up_out, down_out = refs[-11:-6]
+    tok_t, hid_t, gate_buf, up_buf, down_buf, sem = refs[-6:]
+    cap = gate_buf.shape[0]
     groups = cap // group
     d_cols = tok_t.shape[0]
     ff_cols = hid_t.shape[0]
@@ -358,6 +407,19 @@
     def send(buf, out, slot, i):
         part = pl.ds(i * group, group)
         pltpu.make_async_copy(buf.at[part], out.at[part], sem.at[slot]).start()
+
+    def last_sum(n, carry):
+        chunk = 1024
+        for out, base in ((layer, 0), (token_grad, width)):
+            cols = pl.ds(pl.multiple_of(n * chunk, chunk), chunk)
+            there = pl.ds(pl.multiple_of(base + n * chunk, chunk), chunk)
+            total = sums[0][:, there].astype(F32)
+            for piece in sums[1:]:
+                total = total + piece[:, there].astype(F32)
+            out[:, cols] = total.astype(BF16)
+        return carry
+
+    lax.fori_loop(0, width // 1024, last_sum, 0)
 
     def turn_hidden(n, carry):
         hid_t[n] = column(hid0, hid1, n * size).T
@@ -391,7 +453,7 @@
         pltpu.make_async_copy(buf, out, sem.at[slot]).wait()
 
 
-def grads(spots, own, rest, acts0, acts1, size, cap, factor):
+def grads(spots, own, rest, acts0, acts1, sums, size, cap, factor):
     group = max(n for n in range(1, 18) if cap % n == 0)
     width = own.shape[1] // 2
     hidden = acts0[0].shape[1]
@@ -401,9 +463,9 @@
     need = rows * (6 * width + 8 * hidden) + cap * 12 * size * size
     return pl.pallas_call(
         functools.partial(grads_body, factor, size, group),
-        out_shape=(out, out, out),
-        in_specs=[SMEM_SPEC] + [in_vmem()] * 8,
-        out_specs=(HBM_SPEC,) * 3,
+        out_shape=(jax.ShapeDtypeStruct((sums[0].shape[0], width), BF16),) * 2 + (out, out, out),
+        in_specs=[SMEM_SPEC] + [in_vmem()] * (8 + len(sums)),
+        out_specs=(in_vmem(),) * 2 + (HBM_SPEC,) * 3,
         scratch_shapes=[
             VMEM((width // size, size, rows), BF16),
             VMEM((hidden // size, size, rows), BF16),
@@ -417,7 +479,7 @@
             flops=6 * cap * size * size * rows, bytes_accessed=12 * cap * size * size, transcendentals=0
         ),
         name="grads",
-    )(spots, own, rest, acts0[0], acts1[0], acts0[1], acts1[1], acts0[2], acts1[2])
+    )(spots, own, rest, acts0[0], acts1[0], acts0[1], acts1[1], acts0[2], acts1[2], *sums)
 
 
 def local(
@@ -442,12 +504,6 @@
     cap = (kept_count + groups - 1) // groups + kept_count // (4 * groups)
     factor = 1.0 / math.sqrt(rows * slices * groups)
 
-    mine = lax.axis_index("dp") * cap + jnp.arange(cap, dtype=jnp.int32)
-    slots = jnp.concatenate([gate_slot, up_slot, down_slot])
-    index = jnp.concatenate([gate_index, up_index, down_index])
-    hit = slots[:, None, :] == mine[None, :, None]
-    spots = jnp.sum(jnp.where(hit, index[:, None, :] + 1, 0), axis=2) - 1
-
     both = side_by_side(tokens, out_grad)
     chips = range(2, slices, 2)
 
@@ -457,10 +513,20 @@
     far = [exchange(both, "dp", a) for a in range(1, groups)]
     near = [exchange(both, "tensor", d) for d in chips[:-1]]
     stage = 2 * width * hidden
-    wu, later = dense(up_index, up_blocks, both, width, hidden, DENSE_LIMIT)
+    wu, later, spots = dense_first(
+        up_index,
+        up_blocks,
+        both,
+        (gate_slot, up_slot, down_slot),
+        (gate_index, up_index, down_index),
+        cap,
+        width,
+        hidden,
+        DENSE_LIMIT,
+    )
     near.append(exchange(later, "tensor", chips[-1]))
     others = pack(far, [wu])
-    (wg,) = dense(gate_index, gate_blocks, None, width, hidden, NEXT_LIMIT, [spots, others])
+    wg = dense(gate_index, gate_blocks, width, hidden, NEXT_LIMIT, [others])
     own_half = pack([both, *near], [wg])
     own_pieces = [own_half, sibling(own_half)]
     other_half = [others, *(exchange(others, "tensor", d) for d in chips)]
@@ -472,13 +538,11 @@
     acts1_in = [*other_half, *(sibling(x) for x in other_half)]
     *acts1, rest = acts_pass(acts1_in, wg, wu, wd, "rest_acts", [chip[0]])
 
-    total = chip[0].astype(F32)
-    for piece, d in zip(chip[1:], chips):
-        total = total + exchange(piece, "tensor", d).astype(F32)
-    total = total.astype(BF16)
-
-    gate_out, up_out, down_out = grads(spots, own, rest, acts0, acts1, size, cap, factor)
-    return (total[:, :width], total[:, width:], gate_out[None], up_out[None], down_out[None])
+    sums = [chip[0], *(exchange(piece, "tensor", d) for piece, d in zip(chip[1:], chips))]
+    layer_out, token_grad, gate_out, up_out, down_out = grads(
+        spots, own, rest, acts0, acts1, sums, size, cap, factor
+    )
+    return (layer_out, token_grad, gate_out[None], up_out[None], down_out[None])
 
 
 def solution(mesh):

time: 86.2 us -> 84.4 us (0.979)
  other arithmetic: 1.73 us -> 0 us
  transfers between devices with their start and end apart: 18 -> 18, of which waited for: 3 -> 2; matrix products, arithmetic and copies ran while one was open for 2% -> 0% of each run, Pallas kernels for 67% -> 57%
where the time goes in v5:
time: 84.4 us; the launch traced here: 83.9 us
  Pallas kernels  58.5 us (69%)
  starting transfers between devices  17.6 us (21%)
  local copies, waits for them, and re-layouts  3.6 us (4%)
  waiting for transfers between devices  3.42 us (4%)
    pallas_call x1, Pallas kernels, own_pass(): pl.pallas_call(functools.partial(own_body, len(pieces)), out_shape=(act,...  25.8 us
    ppermute x18, starting transfers between devices, exchange(): return lax.ppermute(x, axis, [(i, i ^ flip) for i in range(count)])  17.6 us
    pallas_call x1, Pallas kernels, acts_pass(): pl.pallas_call(functools.partial(acts_body, len(pieces)), out_shape=(act,...  13.7 us
    pallas_call x1, Pallas kernels, grads(): pl.pallas_call(functools.partial(grads_body, factor, size, group), out_sh...  9.45 us
    pallas_call x1, Pallas kernels, dense_first(): pl.pallas_call(functools.partial(dense_first_body, cap), out_shape=(VMEM(...  4.27 us
    pallas_call x1, Pallas kernels, dense(): pl.pallas_call(dense_body, out_shape=VMEM((width, hidden), BF16), in_spec...  4.11 us
    unnamed x4, local copies, waits for them, and re-layouts  3.6 us
    ppermute x18, waiting for transfers between devices, exchange(): return lax.ppermute(x, axis, [(i, i ^ flip) for i in range(count)])  3.42 us
  transfers between devices with their start and end apart: 18, of which 2 were waited for; matrix products, arithmetic and copies ran while one was open for 0% of the time, Pallas kernels for 57%

profile of v5, /device:TPU:0, one launch (start us, length us, event | category | flops | bytes accessed | tf_op | source)
XLA Modules:
  0.0 83.9 jit_solution(15771688407408543093)
XLA Ops:
  0.6 0.9 %side_by_side.1.source.refs_0_ = bf16[8,8192]{1,0:T(8,128)(2,1)S(1)} custom-call(bf16[8,4096]{1,0:T(8,128)(2,1)} %left_ref.1, bf16[8,4096]{1,0:T(8,128)(2,1)} %right_ref.1), custom_call_target="tpu_custom_call" | custom-call | tf_op jit(solution)/shard_map/side_by_side/pallas_call | solution.py:95
  1.5 5.1 %collective-permute-start.5 = (bf16[8,8192]{1,0:T(8,128)(2,1)S(1)}, bf16[8,8192]{1,0:T(8,128)(2,1)S(1)}, u32[]{:S(2)}, u32[]{:S(2)}) collective-permute-start(bf16[8,8192]{1,0:T(8,128)(2,1)S(1)} %side_by_side.1.source.refs_0_), channel_id=1, source_target_pairs={{0,24},{8,16},{16,8},{24,0},{1,25},{9,17},{17,9},{25,1},{2,26},{10... | collective-permute-start | bytes 393224 | tf_op jit(solution)/shard_map/ppermute | solution.py:49
  6.6 0.6 collective-permute-start.3
  7.3 1.7 %collective-permute-start.1 = (bf16[8,8192]{1,0:T(8,128)(2,1)S(1)}, bf16[8,8192]{1,0:T(8,128)(2,1)S(1)}, u32[]{:S(2)}, u32[]{:S(2)}) collective-permute-start(bf16[8,8192]{1,0:T(8,128)(2,1)S(1)} %side_by_side.1.source.refs_0_), channel_id=1, source_target_pairs={{0,4},{1,5},{2,6},{3,7},{4,0},{5,1},{6,2},{7,3},{8,12},{9,13},{10,... | collective-permute-start | bytes 393224 | tf_op jit(solution)/shard_map/ppermute | solution.py:49
  8.9 1.5 %collective-permute-start = (bf16[8,8192]{1,0:T(8,128)(2,1)S(1)}, bf16[8,8192]{1,0:T(8,128)(2,1)S(1)}, u32[]{:S(2)}, u32[]{:S(2)}) collective-permute-start(bf16[8,8192]{1,0:T(8,128)(2,1)S(1)} %side_by_side.1.source.refs_0_), channel_id=1, source_target_pairs={{0,2},{1,3},{2,0},{3,1},{4,6},{5,7},{6,4},{7,5},{8,10},{9,11},{10,... | collective-permute-start | bytes 393224 | tf_op jit(solution)/shard_map/ppermute | solution.py:49
  10.4 4.3 %dense_first.1 = (bf16[4096,1792]{1,0:T(8,128)(2,1)S(1)}, bf16[8,8192]{1,0:T(8,128)(2,1)S(1)}, s32[3,128]{1,0:T(4,128)S(1)}) custom-call(s32[1,224]{1,0:T(1,128)} %refs_4_.2, bf16[224,128,128]{2,1,0:T(8,128)(2,1)} %blocks.2, bf16[8,8192]{1,0:T(8,128)(2,1)S(1)} %side_by_side.1.source.refs_0_, s32[1,224]{1,0:T(1,128)} %refs_0_.1, s32[1,224]{1,0:T(1,128)} %refs_1_.1, ...), custom_call_target="tpu_custom_call" | custom-call | tf_op jit(solution)/shard_map/dense_first/pallas_call | solution.py:198
  14.7 0.0 collective-permute-done.5.refs_2_
  14.7 0.4 collective-permute-start.2
  15.1 2.6 %collective-permute-done.4.refs_1_ = bf16[8,8192]{1,0:T(8,128)(2,1)S(1)} collective-permute-done((bf16[8,8192]{1,0:T(8,128)(2,1)S(1)}, bf16[8,8192]{1,0:T(8,128)(2,1)S(1)}, u32[]{:S(2)}, u32[]{:S(2)}) %collective-permute-start.4) | collective-permute-done | bytes 131104 | tf_op jit(solution)/shard_map/ppermute | solution.py:49
  17.7 0.0 collective-permute-done.3.refs_0_
  17.8 2.2 %copy-done = bf16[4096,1792]{1,0:T(8,128)(2,1)} copy-done((bf16[4096,1792]{1,0:T(8,128)(2,1)}, bf16[4096,1792]{1,0:T(8,128)(2,1)S(1)}, u32[]{:S(2)}) %copy-start) | copy-done | bytes 14680088
  19.9 4.1 %dense.1.refs_4_.refs_2_.refs_8_ = bf16[4096,1792]{1,0:T(8,128)(2,1)S(1)} custom-call(s32[1,224]{1,0:T(1,128)} %index_hbm.4, bf16[224,128,128]{2,1,0:T(8,128)(2,1)} %blocks.3, bf16[24,8192]{1,0:T(8,128)(2,1)S(1)} %pack.2.refs_0_), custom_call_target="tpu_custom_call" | custom-call | tf_op jit(solution)/shard_map/dense/pallas_call | solution.py:219
  24.1 0.0 collective-permute-done.1.refs_2_
  24.1 0.1 pack.3.refs_0_
  24.2 0.1 collective-permute-start.6
  24.2 0.4 collective-permute-start.9
  24.6 1.7 %collective-permute-start.8 = (bf16[24,8192]{1,0:T(8,128)(2,1)S(1)}, bf16[24,8192]{1,0:T(8,128)(2,1)S(1)}, u32[]{:S(2)}, u32[]{:S(2)}) collective-permute-start(bf16[24,8192]{1,0:T(8,128)(2,1)S(1)} %pack.2.refs_0_), channel_id=1, source_target_pairs={{0,4},{1,5},{2,6},{3,7},{4,0},{5,1},{6,2},{7,3},{8,12},{9,13},{10,... | collective-permute-start | bytes 1179656 | tf_op jit(solution)/shard_map/ppermute | solution.py:49
  26.3 1.5 %collective-permute-start.7 = (bf16[24,8192]{1,0:T(8,128)(2,1)S(1)}, bf16[24,8192]{1,0:T(8,128)(2,1)S(1)}, u32[]{:S(2)}, u32[]{:S(2)}) collective-permute-start(bf16[24,8192]{1,0:T(8,128)(2,1)S(1)} %pack.2.refs_0_), channel_id=1, source_target_pairs={{0,2},{1,3},{2,0},{3,1},{4,6},{5,7},{6,4},{7,5},{8,10},{9,11},{10,... | collective-permute-start | bytes 1179656 | tf_op jit(solution)/shard_map/ppermute | solution.py:49
  27.8 1.4 %copy-done.1 = bf16[4096,1792]{1,0:T(8,128)(2,1)S(1)} copy-done((bf16[4096,1792]{1,0:T(8,128)(2,1)S(1)}, bf16[4096,1792]{1,0:T(8,128)(2,1)}, u32[]{:S(2)}) %copy-start.1) | copy-done | bytes 14680088
  29.2 25.8 %own_pass.1 = (bf16[64,1792]{1,0:T(8,128)(2,1)S(1)}, bf16[64,1792]{1,0:T(8,128)(2,1)S(1)}, bf16[64,1792]{1,0:T(8,128)(2,1)S(1)}, bf16[64,8192]{1,0:T(8,128)(2,1)...) custom-call(s32[1,224]{1,0:T(1,128)} %index_hbm.5, ...), custom_call_target="tpu_custom_call" | custom-call | flops 5637144576 | bytes 14680064 | tf_op jit(solution)/shard_map/own_pass/pallas_call | solution.py:360
  55.0 0.1 collective-permute-start.14
  55.1 0.5 collective-permute-start.10
  55.6 0.1 collective-permute-start.13
  55.7 0.4 collective-permute-start.12
  56.1 0.1 collective-permute-start.11
  56.2 0.8 collective-permute-done.14.refs_1_
  57.0 0.2 add_and_cut.1
  57.2 0.6 collective-permute-start.15
  57.8 0.4 collective-permute-start.16
  58.1 2.6 %collective-permute-start.17 = (bf16[8,8192]{1,0:T(8,128)(2,1)S(1)}, bf16[8,8192]{1,0:T(8,128)(2,1)S(1)}, u32[]{:S(2)}, u32[]{:S(2)}) collective-permute-start(bf16[8,8192]{1,0:T(8,128)(2,1)S(1)} %get-tuple-element.45), channel_id=1, source_target_pairs={{0,6},{1,7},{2,4},{3,5},{4,2},{5,3},{6,0},{7,1},{8,14},{9,15},{10,... | collective-permute-start | bytes 393224 | tf_op jit(solution)/shard_map/ppermute | solution.py:49
  60.8 13.7 %rest_acts.1 = (bf16[192,1792]{1,0:T(8,128)(2,1)S(1)}, bf16[192,1792]{1,0:T(8,128)(2,1)S(1)}, bf16[192,1792]{1,0:T(8,128)(2,1)S(1)}, bf16[192,8192]{1,0:T(8,128)(2,1)S(1)}) custom-call(bf16[24,8192]{1,0:T(8,128)(2,1)S(1)} %pack.2.refs_0_, bf16[24,8192]{1,0:T(8,128)(2,1)S(1)} %collective-permute-done.7.refs_1_, ...), custom_call_target="tpu_custom_call" | custom-call | flops 8455716864 | bytes 14680064 | tf_op jit(solution)/shard_map/rest_acts/pallas_call | solution.py:277
  74.5 9.5 %grads.1 = (bf16[8,4096]{1,0:T(8,128)(2,1)}, bf16[8,4096]{1,0:T(8,128)(2,1)}, f32[70,128,128]{2,1,0:T(8,128)}, f32[70,128,128]{2,1,0:T(8,128)}, f32[70,128,128]{2,1,0:T(8,128)}) custom-call(s32[3,128]{1,0:T(4,128)S(1)} %get-tuple-element.28.spots, bf16[64,8192]{1,0:T(8,128)(2,1)S(1)} %get-tuple-element.31.own, bf16[192,8192]{1,0:T(8,128)(2,1)S(1)} %get-tuple-element.36.rest, ...), custom_call_target="tpu_custom_call" | custom-call | flops 1761607680 | bytes 13762560 | tf_op jit(solution)/shard_map/grads/pallas_call | solution.py:464
  (17 shorter events, 0.1 us)
Async XLA Ops:
  1.5 13.2 %collective-permute-start.5 = (bf16[8,8192]{1,0:T(8,128)(2,1)S(1)}, bf16[8,8192]{1,0:T(8,128)(2,1)S(1)}, u32[]{:S(2)}, u32[]{:S(2)}) collective-permute-start(bf16[8,8192]{1,0:T(8,128)(2,1)S(1)} %side_by_side.1.source.refs_0_), channel_id=1, source_target_pairs={{0,24},{8,16},{16,8},{24,0},{1,25},{9,17},{17,9},{25,1},{2,26},{10... | collective-permute-start | bytes 393224 | tf_op jit(solution)/shard_map/ppermute | solution.py:49
  6.6 11.1 %collective-permute-start.4 = (bf16[8,8192]{1,0:T(8,128)(2,1)S(1)}, bf16[8,8192]{1,0:T(8,128)(2,1)S(1)}, u32[]{:S(2)}, u32[]{:S(2)}) collective-permute-start(bf16[8,8192]{1,0:T(8,128)(2,1)S(1)} %side_by_side.1.source.refs_0_), channel_id=1, source_target_pairs={{0,16},{8,24},{16,0},{24,8},{1,17},{9,25},{17,1},{25,9},{2,18},{10... | collective-permute-start | bytes 393224 | tf_op jit(solution)/shard_map/ppermute | solution.py:49
  6.6 11.1 %collective-permute-start.3 = (bf16[8,8192]{1,0:T(8,128)(2,1)S(1)}, bf16[8,8192]{1,0:T(8,128)(2,1)S(1)}, u32[]{:S(2)}, u32[]{:S(2)}) collective-permute-start(bf16[8,8192]{1,0:T(8,128)(2,1)S(1)} %side_by_side.1.source.refs_0_), channel_id=1, source_target_pairs={{0,8},{8,0},{16,24},{24,16},{1,9},{9,1},{17,25},{25,17},{2,10},{10... | collective-permute-start | bytes 393224 | tf_op jit(solution)/shard_map/ppermute | solution.py:49
  7.3 16.8 %collective-permute-start.1 = (bf16[8,8192]{1,0:T(8,128)(2,1)S(1)}, bf16[8,8192]{1,0:T(8,128)(2,1)S(1)}, u32[]{:S(2)}, u32[]{:S(2)}) collective-permute-start(bf16[8,8192]{1,0:T(8,128)(2,1)S(1)} %side_by_side.1.source.refs_0_), channel_id=1, source_target_pairs={{0,4},{1,5},{2,6},{3,7},{4,0},{5,1},{6,2},{7,3},{8,12},{9,13},{10,... | collective-permute-start | bytes 393224 | tf_op jit(solution)/shard_map/ppermute | solution.py:49
  8.9 15.1 %collective-permute-start = (bf16[8,8192]{1,0:T(8,128)(2,1)S(1)}, bf16[8,8192]{1,0:T(8,128)(2,1)S(1)}, u32[]{:S(2)}, u32[]{:S(2)}) collective-permute-start(bf16[8,8192]{1,0:T(8,128)(2,1)S(1)} %side_by_side.1.source.refs_0_), channel_id=1, source_target_pairs={{0,2},{1,3},{2,0},{3,1},{4,6},{5,7},{6,4},{7,5},{8,10},{9,11},{10,... | collective-permute-start | bytes 393224 | tf_op jit(solution)/shard_map/ppermute | solution.py:49
  14.7 5.2 %copy-start = (bf16[4096,1792]{1,0:T(8,128)(2,1)}, bf16[4096,1792]{1,0:T(8,128)(2,1)S(1)}, u32[]{:S(2)}) copy-start(bf16[4096,1792]{1,0:T(8,128)(2,1)S(1)} %get-tuple-element.30.refs_3_.refs_9_) | copy-start | bytes 44040196
  14.7 9.4 %collective-permute-start.2 = (bf16[8,8192]{1,0:T(8,128)(2,1)S(1)}, bf16[8,8192]{1,0:T(8,128)(2,1)S(1)}, u32[]{:S(2)}, u32[]{:S(2)}) collective-permute-start(bf16[8,8192]{1,0:T(8,128)(2,1)S(1)} %get-tuple-element.29), channel_id=1, source_target_pairs={{0,6},{1,7},{2,4},{3,5},{4,2},{5,3},{6,0},{7,1},{8,14},{9,15},{10,... | collective-permute-start | bytes 393224 | tf_op jit(solution)/shard_map/ppermute | solution.py:49
  24.1 5.2 %copy-start.1 = (bf16[4096,1792]{1,0:T(8,128)(2,1)S(1)}, bf16[4096,1792]{1,0:T(8,128)(2,1)}, u32[]{:S(2)}) copy-start(bf16[4096,1792]{1,0:T(8,128)(2,1)} %copy-done) | copy-start | bytes 44040196
  24.2 3.6 %collective-permute-start.6 = (bf16[32,8192]{1,0:T(8,128)(2,1)S(1)}, bf16[32,8192]{1,0:T(8,128)(2,1)S(1)}, u32[]{:S(2)}, u32[]{:S(2)}) collective-permute-start(bf16[32,8192]{1,0:T(8,128)(2,1)S(1)} %pack.3.refs_0_), channel_id=1, source_target_pairs={{0,1},{1,0},{2,3},{3,2},{4,5},{5,4},{6,7},{7,6},{8,9},{9,8},{10,11... | collective-permute-start | bytes 1572872 | tf_op jit(solution)/shard_map/ppermute | solution.py:49
  24.2 31.4 %collective-permute-start.9 = (bf16[24,8192]{1,0:T(8,128)(2,1)S(1)}, bf16[24,8192]{1,0:T(8,128)(2,1)S(1)}, u32[]{:S(2)}, u32[]{:S(2)}) collective-permute-start(bf16[24,8192]{1,0:T(8,128)(2,1)S(1)} %pack.2.refs_0_), channel_id=1, source_target_pairs={{0,6},{1,7},{2,4},{3,5},{4,2},{5,3},{6,0},{7,1},{8,14},{9,15},{10,... | collective-permute-start | bytes 1179656 | tf_op jit(solution)/shard_map/ppermute | solution.py:49
  24.6 31.1 %collective-permute-start.8 = (bf16[24,8192]{1,0:T(8,128)(2,1)S(1)}, bf16[24,8192]{1,0:T(8,128)(2,1)S(1)}, u32[]{:S(2)}, u32[]{:S(2)}) collective-permute-start(bf16[24,8192]{1,0:T(8,128)(2,1)S(1)} %pack.2.refs_0_), channel_id=1, source_target_pairs={{0,4},{1,5},{2,6},{3,7},{4,0},{5,1},{6,2},{7,3},{8,12},{9,13},{10,... | collective-permute-start | bytes 1179656 | tf_op jit(solution)/shard_map/ppermute | solution.py:49
  26.3 29.8 %collective-permute-start.7 = (bf16[24,8192]{1,0:T(8,128)(2,1)S(1)}, bf16[24,8192]{1,0:T(8,128)(2,1)S(1)}, u32[]{:S(2)}, u32[]{:S(2)}) collective-permute-start(bf16[24,8192]{1,0:T(8,128)(2,1)S(1)} %pack.2.refs_0_), channel_id=1, source_target_pairs={{0,2},{1,3},{2,0},{3,1},{4,6},{5,7},{6,4},{7,5},{8,10},{9,11},{10,... | collective-permute-start | bytes 1179656 | tf_op jit(solution)/shard_map/ppermute | solution.py:49
  55.0 2.0 %collective-permute-start.14 = (bf16[32,8192]{1,0:T(8,128)(2,1)S(1)}, bf16[32,8192]{1,0:T(8,128)(2,1)S(1)}, u32[]{:S(2)}, u32[]{:S(2)}) collective-permute-start(bf16[32,8192]{1,0:T(8,128)(2,1)S(1)} %get-tuple-element.34), channel_id=1, source_target_pairs={{0,1},{1,0},{2,3},{3,2},{4,5},{5,4},{6,7},{7,6},{8,9},{9,8},{10,11... | collective-permute-start | bytes 1572872 | tf_op jit(solution)/shard_map/ppermute | solution.py:49
  55.1 2.7 %collective-permute-start.10 = (bf16[24,8192]{1,0:T(8,128)(2,1)S(1)}, bf16[24,8192]{1,0:T(8,128)(2,1)S(1)}, u32[]{:S(2)}, u32[]{:S(2)}) collective-permute-start(bf16[24,8192]{1,0:T(8,128)(2,1)S(1)} %pack.2.refs_0_), channel_id=1, source_target_pairs={{0,1},{1,0},{2,3},{3,2},{4,5},{5,4},{6,7},{7,6},{8,9},{9,8},{10,11... | collective-permute-start | bytes 1179656 | tf_op jit(solution)/shard_map/ppermute | solution.py:49
  55.6 2.5 %collective-permute-start.13 = (bf16[24,8192]{1,0:T(8,128)(2,1)S(1)}, bf16[24,8192]{1,0:T(8,128)(2,1)S(1)}, u32[]{:S(2)}, u32[]{:S(2)}) collective-permute-start(bf16[24,8192]{1,0:T(8,128)(2,1)S(1)} %collective-permute-done.9.refs_3_), channel_id=1, source_target_pairs={{0,1},{1,0},{2,3},{3,2},{4,5},{5,4},{6,7},{7,6},{8,9},{9,8},{10,11... | collective-permute-start | bytes 1179656 | tf_op jit(solution)/shard_map/ppermute | solution.py:49
  55.7 5.0 %collective-permute-start.12 = (bf16[24,8192]{1,0:T(8,128)(2,1)S(1)}, bf16[24,8192]{1,0:T(8,128)(2,1)S(1)}, u32[]{:S(2)}, u32[]{:S(2)}) collective-permute-start(bf16[24,8192]{1,0:T(8,128)(2,1)S(1)} %collective-permute-done.8.refs_2_), channel_id=1, source_target_pairs={{0,1},{1,0},{2,3},{3,2},{4,5},{5,4},{6,7},{7,6},{8,9},{9,8},{10,11... | collective-permute-start | bytes 1179656 | tf_op jit(solution)/shard_map/ppermute | solution.py:49
  56.1 4.6 %collective-permute-start.11 = (bf16[24,8192]{1,0:T(8,128)(2,1)S(1)}, bf16[24,8192]{1,0:T(8,128)(2,1)S(1)}, u32[]{:S(2)}, u32[]{:S(2)}) collective-permute-start(bf16[24,8192]{1,0:T(8,128)(2,1)S(1)} %collective-permute-done.7.refs_1_), channel_id=1, source_target_pairs={{0,1},{1,0},{2,3},{3,2},{4,5},{5,4},{6,7},{7,6},{8,9},{9,8},{10,11... | collective-permute-start | bytes 1179656 | tf_op jit(solution)/shard_map/ppermute | solution.py:49
  57.2 17.2 %collective-permute-start.15 = (bf16[8,8192]{1,0:T(8,128)(2,1)S(1)}, bf16[8,8192]{1,0:T(8,128)(2,1)S(1)}, u32[]{:S(2)}, u32[]{:S(2)}) collective-permute-start(bf16[8,8192]{1,0:T(8,128)(2,1)S(1)} %get-tuple-element.43), channel_id=1, source_target_pairs={{0,2},{1,3},{2,0},{3,1},{4,6},{5,7},{6,4},{7,5},{8,10},{9,11},{10,... | collective-permute-start | bytes 393224 | tf_op jit(solution)/shard_map/ppermute | solution.py:49
  57.8 16.7 %collective-permute-start.16 = (bf16[8,8192]{1,0:T(8,128)(2,1)S(1)}, bf16[8,8192]{1,0:T(8,128)(2,1)S(1)}, u32[]{:S(2)}, u32[]{:S(2)}) collective-permute-start(bf16[8,8192]{1,0:T(8,128)(2,1)S(1)} %get-tuple-element.44), channel_id=1, source_target_pairs={{0,4},{1,5},{2,6},{3,7},{4,0},{5,1},{6,2},{7,3},{8,12},{9,13},{10,... | collective-permute-start | bytes 393224 | tf_op jit(solution)/shard_map/ppermute | solution.py:49
  58.1 16.3 %collective-permute-start.17 = (bf16[8,8192]{1,0:T(8,128)(2,1)S(1)}, bf16[8,8192]{1,0:T(8,128)(2,1)S(1)}, u32[]{:S(2)}, u32[]{:S(2)}) collective-permute-start(bf16[8,8192]{1,0:T(8,128)(2,1)S(1)} %get-tuple-element.45), channel_id=1, source_target_pairs={{0,6},{1,7},{2,4},{3,5},{4,2},{5,3},{6,0},{7,1},{8,14},{9,15},{10,... | collective-permute-start | bytes 393224 | tf_op jit(solution)/shard_map/ppermute | solution.py:49

commit v6 on v5

--- a/solution.py
+++ b/solution.py
@@ -232,6 +232,10 @@
     return 256 if hidden % 256 == 0 else 128
 
 
+def broad_of(hidden):
+    return 896 if hidden % 896 == 0 else 128
+
+
 def acts_body(count, *refs):
     pieces, (wg, wu, wd_hbm), refs = refs[:count], refs[count : count + 3], refs[count + 3 :]
     hid, gp, up, x, wd, sem = refs[-6:]
@@ -292,9 +296,8 @@
     pieces, (wg, wu, blocks), refs = refs[:count], refs[count : count + 3], refs[count + 3 :]
     hid, gp, up, x, part, back, wd_out, wd, g_all, u_all, index, sem = refs
     width, hidden = wg.shape
-    steps, _, chunk = g_all.shape
-    kept = blocks.shape[0]
-    each = kept // steps
+    chunk = chunk_of(hidden)
+    steps = hidden // chunk
     fetch = pltpu.make_async_copy(index_hbm, index, sem.at[1])
     fetch.start()
     assemble(pieces, x)
@@ -302,28 +305,32 @@
     def place(n):
         return pl.ds(pl.multiple_of(n * chunk, chunk), chunk)
 
+    broad = broad_of(hidden)
+
+    def span(n):
+        return pl.ds(pl.multiple_of(n * broad, 128), broad)
+
     def gate(n, carry):
-        g_all[n] = dot_nn(x[:, :width], wg[:, place(n)])
-        wd[place(n)] = jnp.zeros((chunk, width), BF16)
-        return carry
-
-    lax.fori_loop(0, steps, gate, 0)
+        g_all[:, span(n)] = dot_nn(x[:, :width], wg[:, span(n)])
+        wd[span(n)] = jnp.zeros((broad, width), BF16)
+        return carry
+
+    lax.fori_loop(0, hidden // broad, gate, 0)
     fetch.wait()
+    fill_dense(index, blocks, wd, sem.at[0])
 
     def up_proj(n, carry):
-        scatter(index, blocks, wd, sem.at[0], n * each, each)
-        u_all[n] = dot_nn(x[:, :width], wu[:, place(n)])
-        return carry
-
-    lax.fori_loop(0, steps, up_proj, 0)
-    scatter(index, blocks, wd, sem.at[0], steps * each, kept - steps * each)
+        u_all[:, span(n)] = dot_nn(x[:, :width], wu[:, span(n)])
+        return carry
+
+    lax.fori_loop(0, hidden // broad, up_proj, 0)
     pltpu.make_async_copy(blocks, blocks, sem.at[0]).wait()
     store = pltpu.make_async_copy(wd, wd_out, sem.at[2])
     store.start()
 
     def grad(n, carry):
         cols = place(n)
-        g, u = g_all[n], u_all[n]
+        g, u = g_all[:, cols], u_all[:, cols]
         h = dot_nt(x[:, width:], wd[cols])
         s = jax.nn.sigmoid(g)
         hid[:, cols] = (g * s * u).astype(BF16)
@@ -333,7 +340,7 @@
 
     lax.fori_loop(0, steps, grad, 0)
     half = part.shape[0]
-    wide = 1024
+    wide = 2048
 
     def sums(n, carry):
         out = pl.ds(pl.multiple_of(n * wide, wide), wide)
@@ -353,10 +360,9 @@
 def own_pass(pieces, wg, wu, index, blocks, limit):
     rows = sum(x.shape[0] for x in pieces)
     width, hidden = wg.shape
-    chunk = chunk_of(hidden)
     act = VMEM((rows, hidden), BF16)
     half = VMEM((rows // 2, 2 * width), BF16)
-    kept = VMEM((hidden // chunk, rows, chunk), F32)
+    kept = VMEM((rows, hidden), F32)
     return pl.pallas_call(
         functools.partial(own_body, len(pieces)),
         out_shape=(

time: 84.4 us -> 83 us (0.983)
  Pallas kernels: 58.5 us -> 57.2 us
    pallas_call x1, Pallas kernels: 25.8 us -> 24.6 us  [own_pass(): pl.pallas_call(functools.partial(own_body, len(pieces)), out_shape=(act,...]
where the time goes in v6:
time: 83 us; the launch traced here: 82.6 us
  Pallas kernels  57.2 us (69%)
  starting transfers between devices  17.6 us (21%)
  local copies, waits for them, and re-layouts  3.6 us (4%)
  waiting for transfers between devices  3.43 us (4%)
    pallas_call x1, Pallas kernels, own_pass(): pl.pallas_call(functools.partial(own_body, len(pieces)), out_shape=(act,...  24.6 us
    ppermute x18, starting transfers between devices, exchange(): return lax.ppermute(x, axis, [(i, i ^ flip) for i in range(count)])  17.6 us
    pallas_call x1, Pallas kernels, acts_pass(): pl.pallas_call(functools.partial(acts_body, len(pieces)), out_shape=(act,...  13.7 us
    pallas_call x1, Pallas kernels, grads(): pl.pallas_call(functools.partial(grads_body, factor, size, group), out_sh...  9.41 us
    pallas_call x1, Pallas kernels, dense_first(): pl.pallas_call(functools.partial(dense_first_body, cap), out_shape=(VMEM(...  4.27 us
    pallas_call x1, Pallas kernels, dense(): pl.pallas_call(dense_body, out_shape=VMEM((width, hidden), BF16), in_spec...  4.11 us
    unnamed x4, local copies, waits for them, and re-layouts  3.6 us
    ppermute x18, waiting for transfers between devices, exchange(): return lax.ppermute(x, axis, [(i, i ^ flip) for i in range(count)])  3.43 us
  transfers between devices with their start and end apart: 18, of which 2 were waited for; matrix products, arithmetic and copies ran while one was open for 0% of the time, Pallas kernels for 57%

profile of v6, /device:TPU:0, one launch (start us, length us, event | category | flops | bytes accessed | tf_op | source)
XLA Modules:
  0.0 82.6 jit_solution(14946396032398101692)
XLA Ops:
  0.6 0.9 %side_by_side.1.source.refs_0_ = bf16[8,8192]{1,0:T(8,128)(2,1)S(1)} custom-call(bf16[8,4096]{1,0:T(8,128)(2,1)} %left_ref.1, bf16[8,4096]{1,0:T(8,128)(2,1)} %right_ref.1), custom_call_target="tpu_custom_call" | custom-call | tf_op jit(solution)/shard_map/side_by_side/pallas_call | solution.py:95
  1.5 5.1 %collective-permute-start.5 = (bf16[8,8192]{1,0:T(8,128)(2,1)S(1)}, bf16[8,8192]{1,0:T(8,128)(2,1)S(1)}, u32[]{:S(2)}, u32[]{:S(2)}) collective-permute-start(bf16[8,8192]{1,0:T(8,128)(2,1)S(1)} %side_by_side.1.source.refs_0_), channel_id=1, source_target_pairs={{0,24},{8,16},{16,8},{24,0},{1,25},{9,17},{17,9},{25,1},{2,26},{10... | collective-permute-start | bytes 393224 | tf_op jit(solution)/shard_map/ppermute | solution.py:49
  6.6 0.0 collective-permute-start.4
  6.6 0.6 collective-permute-start.3
  7.3 1.7 %collective-permute-start.1 = (bf16[8,8192]{1,0:T(8,128)(2,1)S(1)}, bf16[8,8192]{1,0:T(8,128)(2,1)S(1)}, u32[]{:S(2)}, u32[]{:S(2)}) collective-permute-start(bf16[8,8192]{1,0:T(8,128)(2,1)S(1)} %side_by_side.1.source.refs_0_), channel_id=1, source_target_pairs={{0,4},{1,5},{2,6},{3,7},{4,0},{5,1},{6,2},{7,3},{8,12},{9,13},{10,... | collective-permute-start | bytes 393224 | tf_op jit(solution)/shard_map/ppermute | solution.py:49
  8.9 1.5 %collective-permute-start = (bf16[8,8192]{1,0:T(8,128)(2,1)S(1)}, bf16[8,8192]{1,0:T(8,128)(2,1)S(1)}, u32[]{:S(2)}, u32[]{:S(2)}) collective-permute-start(bf16[8,8192]{1,0:T(8,128)(2,1)S(1)} %side_by_side.1.source.refs_0_), channel_id=1, source_target_pairs={{0,2},{1,3},{2,0},{3,1},{4,6},{5,7},{6,4},{7,5},{8,10},{9,11},{10,... | collective-permute-start | bytes 393224 | tf_op jit(solution)/shard_map/ppermute | solution.py:49
  10.4 4.3 %dense_first.1 = (bf16[4096,1792]{1,0:T(8,128)(2,1)S(1)}, bf16[8,8192]{1,0:T(8,128)(2,1)S(1)}, s32[3,128]{1,0:T(4,128)S(1)}) custom-call(s32[1,224]{1,0:T(1,128)} %refs_4_.2, bf16[224,128,128]{2,1,0:T(8,128)(2,1)} %blocks.2, bf16[8,8192]{1,0:T(8,128)(2,1)S(1)} %side_by_side.1.source.refs_0_, s32[1,224]{1,0:T(1,128)} %refs_0_.1, s32[1,224]{1,0:T(1,128)} %refs_1_.1, ...), custom_call_target="tpu_custom_call" | custom-call | tf_op jit(solution)/shard_map/dense_first/pallas_call | solution.py:198
  14.7 0.0 collective-permute-done.5.refs_2_
  14.7 0.4 collective-permute-start.2
  15.1 2.6 %collective-permute-done.4.refs_1_ = bf16[8,8192]{1,0:T(8,128)(2,1)S(1)} collective-permute-done((bf16[8,8192]{1,0:T(8,128)(2,1)S(1)}, bf16[8,8192]{1,0:T(8,128)(2,1)S(1)}, u32[]{:S(2)}, u32[]{:S(2)}) %collective-permute-start.4) | collective-permute-done | bytes 131104 | tf_op jit(solution)/shard_map/ppermute | solution.py:49
  17.8 2.2 %copy-done = bf16[4096,1792]{1,0:T(8,128)(2,1)} copy-done((bf16[4096,1792]{1,0:T(8,128)(2,1)}, bf16[4096,1792]{1,0:T(8,128)(2,1)S(1)}, u32[]{:S(2)}) %copy-start) | copy-done | bytes 14680088
  19.9 4.1 %dense.1.refs_4_.refs_2_.refs_8_ = bf16[4096,1792]{1,0:T(8,128)(2,1)S(1)} custom-call(s32[1,224]{1,0:T(1,128)} %index_hbm.4, bf16[224,128,128]{2,1,0:T(8,128)(2,1)} %blocks.3, bf16[24,8192]{1,0:T(8,128)(2,1)S(1)} %pack.2.refs_0_), custom_call_target="tpu_custom_call" | custom-call | tf_op jit(solution)/shard_map/dense/pallas_call | solution.py:219
  24.1 0.1 pack.3.refs_0_
  24.2 0.1 collective-permute-start.6
  24.2 0.4 collective-permute-start.9
  24.6 1.7 %collective-permute-start.8 = (bf16[24,8192]{1,0:T(8,128)(2,1)S(1)}, bf16[24,8192]{1,0:T(8,128)(2,1)S(1)}, u32[]{:S(2)}, u32[]{:S(2)}) collective-permute-start(bf16[24,8192]{1,0:T(8,128)(2,1)S(1)} %pack.2.refs_0_), channel_id=1, source_target_pairs={{0,4},{1,5},{2,6},{3,7},{4,0},{5,1},{6,2},{7,3},{8,12},{9,13},{10,... | collective-permute-start | bytes 1179656 | tf_op jit(solution)/shard_map/ppermute | solution.py:49
  26.3 1.5 %collective-permute-start.7 = (bf16[24,8192]{1,0:T(8,128)(2,1)S(1)}, bf16[24,8192]{1,0:T(8,128)(2,1)S(1)}, u32[]{:S(2)}, u32[]{:S(2)}) collective-permute-start(bf16[24,8192]{1,0:T(8,128)(2,1)S(1)} %pack.2.refs_0_), channel_id=1, source_target_pairs={{0,2},{1,3},{2,0},{3,1},{4,6},{5,7},{6,4},{7,5},{8,10},{9,11},{10,... | collective-permute-start | bytes 1179656 | tf_op jit(solution)/shard_map/ppermute | solution.py:49
  27.8 1.4 %copy-done.1 = bf16[4096,1792]{1,0:T(8,128)(2,1)S(1)} copy-done((bf16[4096,1792]{1,0:T(8,128)(2,1)S(1)}, bf16[4096,1792]{1,0:T(8,128)(2,1)}, u32[]{:S(2)}) %copy-start.1) | copy-done | bytes 14680088
  29.2 24.6 %own_pass.1 = (bf16[64,1792]{1,0:T(8,128)(2,1)S(1)}, bf16[64,1792]{1,0:T(8,128)(2,1)S(1)}, bf16[64,1792]{1,0:T(8,128)(2,1)S(1)}, bf16[64,8192]{1,0:T(8,128)(2,1)...) custom-call(s32[1,224]{1,0:T(1,128)} %index_hbm.5, ...), custom_call_target="tpu_custom_call" | custom-call | flops 5637144576 | bytes 14680064 | tf_op jit(solution)/shard_map/own_pass/pallas_call | solution.py:366
  53.8 0.1 collective-permute-start.14
  53.9 0.5 collective-permute-start.10
  54.4 0.1 collective-permute-start.13
  54.5 0.4 collective-permute-start.12
  54.9 0.1 collective-permute-start.11
  55.0 0.8 collective-permute-done.14.refs_1_
  55.8 0.2 add_and_cut.1
  55.9 0.6 collective-permute-start.15
  56.6 0.3 collective-permute-start.16
  56.9 0.0 collective-permute-done.13.refs_7_
  56.9 2.6 %collective-permute-start.17 = (bf16[8,8192]{1,0:T(8,128)(2,1)S(1)}, bf16[8,8192]{1,0:T(8,128)(2,1)S(1)}, u32[]{:S(2)}, u32[]{:S(2)}) collective-permute-start(bf16[8,8192]{1,0:T(8,128)(2,1)S(1)} %get-tuple-element.45), channel_id=1, source_target_pairs={{0,6},{1,7},{2,4},{3,5},{4,2},{5,3},{6,0},{7,1},{8,14},{9,15},{10,... | collective-permute-start | bytes 393224 | tf_op jit(solution)/shard_map/ppermute | solution.py:49
  59.5 13.7 %rest_acts.1 = (bf16[192,1792]{1,0:T(8,128)(2,1)S(1)}, bf16[192,1792]{1,0:T(8,128)(2,1)S(1)}, bf16[192,1792]{1,0:T(8,128)(2,1)S(1)}, bf16[192,8192]{1,0:T(8,128)(2,1)S(1)}) custom-call(bf16[24,8192]{1,0:T(8,128)(2,1)S(1)} %pack.2.refs_0_, bf16[24,8192]{1,0:T(8,128)(2,1)S(1)} %collective-permute-done.7.refs_1_, ...), custom_call_target="tpu_custom_call" | custom-call | flops 8455716864 | bytes 14680064 | tf_op jit(solution)/shard_map/rest_acts/pallas_call | solution.py:281
  73.2 9.4 %grads.1 = (bf16[8,4096]{1,0:T(8,128)(2,1)}, bf16[8,4096]{1,0:T(8,128)(2,1)}, f32[70,128,128]{2,1,0:T(8,128)}, f32[70,128,128]{2,1,0:T(8,128)}, f32[70,128,128]{2,1,0:T(8,128)}) custom-call(s32[3,128]{1,0:T(4,128)S(1)} %get-tuple-element.28.spots, bf16[64,8192]{1,0:T(8,128)(2,1)S(1)} %get-tuple-element.31.own, bf16[192,8192]{1,0:T(8,128)(2,1)S(1)} %get-tuple-element.36.rest, ...), custom_call_target="tpu_custom_call" | custom-call | flops 1761607680 | bytes 13762560 | tf_op jit(solution)/shard_map/grads/pallas_call | solution.py:470
  (17 shorter events, 0.1 us)
Async XLA Ops:
  1.5 13.2 %collective-permute-start.5 = (bf16[8,8192]{1,0:T(8,128)(2,1)S(1)}, bf16[8,8192]{1,0:T(8,128)(2,1)S(1)}, u32[]{:S(2)}, u32[]{:S(2)}) collective-permute-start(bf16[8,8192]{1,0:T(8,128)(2,1)S(1)} %side_by_side.1.source.refs_0_), channel_id=1, source_target_pairs={{0,24},{8,16},{16,8},{24,0},{1,25},{9,17},{17,9},{25,1},{2,26},{10... | collective-permute-start | bytes 393224 | tf_op jit(solution)/shard_map/ppermute | solution.py:49
  6.6 11.1 %collective-permute-start.4 = (bf16[8,8192]{1,0:T(8,128)(2,1)S(1)}, bf16[8,8192]{1,0:T(8,128)(2,1)S(1)}, u32[]{:S(2)}, u32[]{:S(2)}) collective-permute-start(bf16[8,8192]{1,0:T(8,128)(2,1)S(1)} %side_by_side.1.source.refs_0_), channel_id=1, source_target_pairs={{0,16},{8,24},{16,0},{24,8},{1,17},{9,25},{17,1},{25,9},{2,18},{10... | collective-permute-start | bytes 393224 | tf_op jit(solution)/shard_map/ppermute | solution.py:49
  6.6 11.1 %collective-permute-start.3 = (bf16[8,8192]{1,0:T(8,128)(2,1)S(1)}, bf16[8,8192]{1,0:T(8,128)(2,1)S(1)}, u32[]{:S(2)}, u32[]{:S(2)}) collective-permute-start(bf16[8,8192]{1,0:T(8,128)(2,1)S(1)} %side_by_side.1.source.refs_0_), channel_id=1, source_target_pairs={{0,8},{8,0},{16,24},{24,16},{1,9},{9,1},{17,25},{25,17},{2,10},{10... | collective-permute-start | bytes 393224 | tf_op jit(solution)/shard_map/ppermute | solution.py:49
  7.3 16.8 %collective-permute-start.1 = (bf16[8,8192]{1,0:T(8,128)(2,1)S(1)}, bf16[8,8192]{1,0:T(8,128)(2,1)S(1)}, u32[]{:S(2)}, u32[]{:S(2)}) collective-permute-start(bf16[8,8192]{1,0:T(8,128)(2,1)S(1)} %side_by_side.1.source.refs_0_), channel_id=1, source_target_pairs={{0,4},{1,5},{2,6},{3,7},{4,0},{5,1},{6,2},{7,3},{8,12},{9,13},{10,... | collective-permute-start | bytes 393224 | tf_op jit(solution)/shard_map/ppermute | solution.py:49
  8.9 15.1 %collective-permute-start = (bf16[8,8192]{1,0:T(8,128)(2,1)S(1)}, bf16[8,8192]{1,0:T(8,128)(2,1)S(1)}, u32[]{:S(2)}, u32[]{:S(2)}) collective-permute-start(bf16[8,8192]{1,0:T(8,128)(2,1)S(1)} %side_by_side.1.source.refs_0_), channel_id=1, source_target_pairs={{0,2},{1,3},{2,0},{3,1},{4,6},{5,7},{6,4},{7,5},{8,10},{9,11},{10,... | collective-permute-start | bytes 393224 | tf_op jit(solution)/shard_map/ppermute | solution.py:49
  14.7 5.2 %copy-start = (bf16[4096,1792]{1,0:T(8,128)(2,1)}, bf16[4096,1792]{1,0:T(8,128)(2,1)S(1)}, u32[]{:S(2)}) copy-start(bf16[4096,1792]{1,0:T(8,128)(2,1)S(1)} %get-tuple-element.30.refs_3_.refs_9_) | copy-start | bytes 44040196
  14.7 9.4 %collective-permute-start.2 = (bf16[8,8192]{1,0:T(8,128)(2,1)S(1)}, bf16[8,8192]{1,0:T(8,128)(2,1)S(1)}, u32[]{:S(2)}, u32[]{:S(2)}) collective-permute-start(bf16[8,8192]{1,0:T(8,128)(2,1)S(1)} %get-tuple-element.29), channel_id=1, source_target_pairs={{0,6},{1,7},{2,4},{3,5},{4,2},{5,3},{6,0},{7,1},{8,14},{9,15},{10,... | collective-permute-start | bytes 393224 | tf_op jit(solution)/shard_map/ppermute | solution.py:49
  24.1 5.2 %copy-start.1 = (bf16[4096,1792]{1,0:T(8,128)(2,1)S(1)}, bf16[4096,1792]{1,0:T(8,128)(2,1)}, u32[]{:S(2)}) copy-start(bf16[4096,1792]{1,0:T(8,128)(2,1)} %copy-done) | copy-start | bytes 44040196
  24.2 3.6 %collective-permute-start.6 = (bf16[32,8192]{1,0:T(8,128)(2,1)S(1)}, bf16[32,8192]{1,0:T(8,128)(2,1)S(1)}, u32[]{:S(2)}, u32[]{:S(2)}) collective-permute-start(bf16[32,8192]{1,0:T(8,128)(2,1)S(1)} %pack.3.refs_0_), channel_id=1, source_target_pairs={{0,1},{1,0},{2,3},{3,2},{4,5},{5,4},{6,7},{7,6},{8,9},{9,8},{10,11... | collective-permute-start | bytes 1572872 | tf_op jit(solution)/shard_map/ppermute | solution.py:49
  24.2 30.1 %collective-permute-start.9 = (bf16[24,8192]{1,0:T(8,128)(2,1)S(1)}, bf16[24,8192]{1,0:T(8,128)(2,1)S(1)}, u32[]{:S(2)}, u32[]{:S(2)}) collective-permute-start(bf16[24,8192]{1,0:T(8,128)(2,1)S(1)} %pack.2.refs_0_), channel_id=1, source_target_pairs={{0,6},{1,7},{2,4},{3,5},{4,2},{5,3},{6,0},{7,1},{8,14},{9,15},{10,... | collective-permute-start | bytes 1179656 | tf_op jit(solution)/shard_map/ppermute | solution.py:49
  24.6 29.8 %collective-permute-start.8 = (bf16[24,8192]{1,0:T(8,128)(2,1)S(1)}, bf16[24,8192]{1,0:T(8,128)(2,1)S(1)}, u32[]{:S(2)}, u32[]{:S(2)}) collective-permute-start(bf16[24,8192]{1,0:T(8,128)(2,1)S(1)} %pack.2.refs_0_), channel_id=1, source_target_pairs={{0,4},{1,5},{2,6},{3,7},{4,0},{5,1},{6,2},{7,3},{8,12},{9,13},{10,... | collective-permute-start | bytes 1179656 | tf_op jit(solution)/shard_map/ppermute | solution.py:49
  26.3 28.6 %collective-permute-start.7 = (bf16[24,8192]{1,0:T(8,128)(2,1)S(1)}, bf16[24,8192]{1,0:T(8,128)(2,1)S(1)}, u32[]{:S(2)}, u32[]{:S(2)}) collective-permute-start(bf16[24,8192]{1,0:T(8,128)(2,1)S(1)} %pack.2.refs_0_), channel_id=1, source_target_pairs={{0,2},{1,3},{2,0},{3,1},{4,6},{5,7},{6,4},{7,5},{8,10},{9,11},{10,... | collective-permute-start | bytes 1179656 | tf_op jit(solution)/shard_map/ppermute | solution.py:49
  53.8 2.0 %collective-permute-start.14 = (bf16[32,8192]{1,0:T(8,128)(2,1)S(1)}, bf16[32,8192]{1,0:T(8,128)(2,1)S(1)}, u32[]{:S(2)}, u32[]{:S(2)}) collective-permute-start(bf16[32,8192]{1,0:T(8,128)(2,1)S(1)} %get-tuple-element.34), channel_id=1, source_target_pairs={{0,1},{1,0},{2,3},{3,2},{4,5},{5,4},{6,7},{7,6},{8,9},{9,8},{10,11... | collective-permute-start | bytes 1572872 | tf_op jit(solution)/shard_map/ppermute | solution.py:49
  53.9 2.7 %collective-permute-start.10 = (bf16[24,8192]{1,0:T(8,128)(2,1)S(1)}, bf16[24,8192]{1,0:T(8,128)(2,1)S(1)}, u32[]{:S(2)}, u32[]{:S(2)}) collective-permute-start(bf16[24,8192]{1,0:T(8,128)(2,1)S(1)} %pack.2.refs_0_), channel_id=1, source_target_pairs={{0,1},{1,0},{2,3},{3,2},{4,5},{5,4},{6,7},{7,6},{8,9},{9,8},{10,11... | collective-permute-start | bytes 1179656 | tf_op jit(solution)/shard_map/ppermute | solution.py:49
  54.4 2.5 %collective-permute-start.13 = (bf16[24,8192]{1,0:T(8,128)(2,1)S(1)}, bf16[24,8192]{1,0:T(8,128)(2,1)S(1)}, u32[]{:S(2)}, u32[]{:S(2)}) collective-permute-start(bf16[24,8192]{1,0:T(8,128)(2,1)S(1)} %collective-permute-done.9.refs_3_), channel_id=1, source_target_pairs={{0,1},{1,0},{2,3},{3,2},{4,5},{5,4},{6,7},{7,6},{8,9},{9,8},{10,11... | collective-permute-start | bytes 1179656 | tf_op jit(solution)/shard_map/ppermute | solution.py:49
  54.5 5.0 %collective-permute-start.12 = (bf16[24,8192]{1,0:T(8,128)(2,1)S(1)}, bf16[24,8192]{1,0:T(8,128)(2,1)S(1)}, u32[]{:S(2)}, u32[]{:S(2)}) collective-permute-start(bf16[24,8192]{1,0:T(8,128)(2,1)S(1)} %collective-permute-done.8.refs_2_), channel_id=1, source_target_pairs={{0,1},{1,0},{2,3},{3,2},{4,5},{5,4},{6,7},{7,6},{8,9},{9,8},{10,11... | collective-permute-start | bytes 1179656 | tf_op jit(solution)/shard_map/ppermute | solution.py:49
  54.9 4.6 %collective-permute-start.11 = (bf16[24,8192]{1,0:T(8,128)(2,1)S(1)}, bf16[24,8192]{1,0:T(8,128)(2,1)S(1)}, u32[]{:S(2)}, u32[]{:S(2)}) collective-permute-start(bf16[24,8192]{1,0:T(8,128)(2,1)S(1)} %collective-permute-done.7.refs_1_), channel_id=1, source_target_pairs={{0,1},{1,0},{2,3},{3,2},{4,5},{5,4},{6,7},{7,6},{8,9},{9,8},{10,11... | collective-permute-start | bytes 1179656 | tf_op jit(solution)/shard_map/ppermute | solution.py:49
  55.9 17.2 %collective-permute-start.15 = (bf16[8,8192]{1,0:T(8,128)(2,1)S(1)}, bf16[8,8192]{1,0:T(8,128)(2,1)S(1)}, u32[]{:S(2)}, u32[]{:S(2)}) collective-permute-start(bf16[8,8192]{1,0:T(8,128)(2,1)S(1)} %get-tuple-element.43), channel_id=1, source_target_pairs={{0,2},{1,3},{2,0},{3,1},{4,6},{5,7},{6,4},{7,5},{8,10},{9,11},{10,... | collective-permute-start | bytes 393224 | tf_op jit(solution)/shard_map/ppermute | solution.py:49
  56.6 16.7 %collective-permute-start.16 = (bf16[8,8192]{1,0:T(8,128)(2,1)S(1)}, bf16[8,8192]{1,0:T(8,128)(2,1)S(1)}, u32[]{:S(2)}, u32[]{:S(2)}) collective-permute-start(bf16[8,8192]{1,0:T(8,128)(2,1)S(1)} %get-tuple-element.44), channel_id=1, source_target_pairs={{0,4},{1,5},{2,6},{3,7},{4,0},{5,1},{6,2},{7,3},{8,12},{9,13},{10,... | collective-permute-start | bytes 393224 | tf_op jit(solution)/shard_map/ppermute | solution.py:49
  56.9 16.3 %collective-permute-start.17 = (bf16[8,8192]{1,0:T(8,128)(2,1)S(1)}, bf16[8,8192]{1,0:T(8,128)(2,1)S(1)}, u32[]{:S(2)}, u32[]{:S(2)}) collective-permute-start(bf16[8,8192]{1,0:T(8,128)(2,1)S(1)} %get-tuple-element.45), channel_id=1, source_target_pairs={{0,6},{1,7},{2,4},{3,5},{4,2},{5,3},{6,0},{7,1},{8,14},{9,15},{10,... | collective-permute-start | bytes 393224 | tf_op jit(solution)/shard_map/ppermute | solution.py:49

commit v7 on v6

--- a/solution.py
+++ b/solution.py
@@ -296,7 +296,7 @@
     pieces, (wg, wu, blocks), refs = refs[:count], refs[count : count + 3], refs[count + 3 :]
     hid, gp, up, x, part, back, wd_out, wd, g_all, u_all, index, sem = refs
     width, hidden = wg.shape
-    chunk = chunk_of(hidden)
+    chunk = broad_of(hidden)
     steps = hidden // chunk
     fetch = pltpu.make_async_copy(index_hbm, index, sem.at[1])
     fetch.start()

time: 83 us -> 82.4 us (level)
  transfers between devices with their start and end apart: 18 -> 18, of which waited for: 2 -> 2; matrix products, arithmetic and copies ran while one was open for 0% -> 0% of each run, Pallas kernels for 57% -> 56%
where the time goes in v7:
time: 82.4 us; the launch traced here: 82 us
  Pallas kernels  56.5 us (69%)
  starting transfers between devices  17.6 us (21%)
  local copies, waits for them, and re-layouts  3.6 us (4%)
  waiting for transfers between devices  3.42 us (4%)
    pallas_call x1, Pallas kernels, own_pass(): pl.pallas_call(functools.partial(own_body, len(pieces)), out_shape=(act,...  23.9 us
    ppermute x18, starting transfers between devices, exchange(): return lax.ppermute(x, axis, [(i, i ^ flip) for i in range(count)])  17.6 us
    pallas_call x1, Pallas kernels, acts_pass(): pl.pallas_call(functools.partial(acts_body, len(pieces)), out_shape=(act,...  13.7 us
    pallas_call x1, Pallas kernels, grads(): pl.pallas_call(functools.partial(grads_body, factor, size, group), out_sh...  9.45 us
    pallas_call x1, Pallas kernels, dense_first(): pl.pallas_call(functools.partial(dense_first_body, cap), out_shape=(VMEM(...  4.27 us
    pallas_call x1, Pallas kernels, dense(): pl.pallas_call(dense_body, out_shape=VMEM((width, hidden), BF16), in_spec...  4.11 us
    unnamed x4, local copies, waits for them, and re-layouts  3.6 us
    ppermute x18, waiting for transfers between devices, exchange(): return lax.ppermute(x, axis, [(i, i ^ flip) for i in range(count)])  3.42 us
  transfers between devices with their start and end apart: 18, of which 2 were waited for; matrix products, arithmetic and copies ran while one was open for 0% of the time, Pallas kernels for 56%

profile of v7, /device:TPU:0, one launch (start us, length us, event | category | flops | bytes accessed | tf_op | source)
XLA Modules:
  0.0 82.0 jit_solution(11387966859004861880)
XLA Ops:
  0.6 0.9 %side_by_side.1.source.refs_0_ = bf16[8,8192]{1,0:T(8,128)(2,1)S(1)} custom-call(bf16[8,4096]{1,0:T(8,128)(2,1)} %left_ref.1, bf16[8,4096]{1,0:T(8,128)(2,1)} %right_ref.1), custom_call_target="tpu_custom_call" | custom-call | tf_op jit(solution)/shard_map/side_by_side/pallas_call | solution.py:95
  1.5 5.1 %collective-permute-start.5 = (bf16[8,8192]{1,0:T(8,128)(2,1)S(1)}, bf16[8,8192]{1,0:T(8,128)(2,1)S(1)}, u32[]{:S(2)}, u32[]{:S(2)}) collective-permute-start(bf16[8,8192]{1,0:T(8,128)(2,1)S(1)} %side_by_side.1.source.refs_0_), channel_id=1, source_target_pairs={{0,24},{8,16},{16,8},{24,0},{1,25},{9,17},{17,9},{25,1},{2,26},{10... | collective-permute-start | bytes 393224 | tf_op jit(solution)/shard_map/ppermute | solution.py:49
  6.6 0.0 collective-permute-start.4
  6.6 0.6 collective-permute-start.3
  7.3 1.7 %collective-permute-start.1 = (bf16[8,8192]{1,0:T(8,128)(2,1)S(1)}, bf16[8,8192]{1,0:T(8,128)(2,1)S(1)}, u32[]{:S(2)}, u32[]{:S(2)}) collective-permute-start(bf16[8,8192]{1,0:T(8,128)(2,1)S(1)} %side_by_side.1.source.refs_0_), channel_id=1, source_target_pairs={{0,4},{1,5},{2,6},{3,7},{4,0},{5,1},{6,2},{7,3},{8,12},{9,13},{10,... | collective-permute-start | bytes 393224 | tf_op jit(solution)/shard_map/ppermute | solution.py:49
  8.9 1.5 %collective-permute-start = (bf16[8,8192]{1,0:T(8,128)(2,1)S(1)}, bf16[8,8192]{1,0:T(8,128)(2,1)S(1)}, u32[]{:S(2)}, u32[]{:S(2)}) collective-permute-start(bf16[8,8192]{1,0:T(8,128)(2,1)S(1)} %side_by_side.1.source.refs_0_), channel_id=1, source_target_pairs={{0,2},{1,3},{2,0},{3,1},{4,6},{5,7},{6,4},{7,5},{8,10},{9,11},{10,... | collective-permute-start | bytes 393224 | tf_op jit(solution)/shard_map/ppermute | solution.py:49
  10.4 4.3 %dense_first.1 = (bf16[4096,1792]{1,0:T(8,128)(2,1)S(1)}, bf16[8,8192]{1,0:T(8,128)(2,1)S(1)}, s32[3,128]{1,0:T(4,128)S(1)}) custom-call(s32[1,224]{1,0:T(1,128)} %refs_4_.2, bf16[224,128,128]{2,1,0:T(8,128)(2,1)} %blocks.2, bf16[8,8192]{1,0:T(8,128)(2,1)S(1)} %side_by_side.1.source.refs_0_, s32[1,224]{1,0:T(1,128)} %refs_0_.1, s32[1,224]{1,0:T(1,128)} %refs_1_.1, ...), custom_call_target="tpu_custom_call" | custom-call | tf_op jit(solution)/shard_map/dense_first/pallas_call | solution.py:198
  14.7 0.4 collective-permute-start.2
  15.1 2.6 %collective-permute-done.4.refs_1_ = bf16[8,8192]{1,0:T(8,128)(2,1)S(1)} collective-permute-done((bf16[8,8192]{1,0:T(8,128)(2,1)S(1)}, bf16[8,8192]{1,0:T(8,128)(2,1)S(1)}, u32[]{:S(2)}, u32[]{:S(2)}) %collective-permute-start.4) | collective-permute-done | bytes 131104 | tf_op jit(solution)/shard_map/ppermute | solution.py:49
  17.7 0.0 collective-permute-done.3.refs_0_
  17.8 2.2 %copy-done = bf16[4096,1792]{1,0:T(8,128)(2,1)} copy-done((bf16[4096,1792]{1,0:T(8,128)(2,1)}, bf16[4096,1792]{1,0:T(8,128)(2,1)S(1)}, u32[]{:S(2)}) %copy-start) | copy-done | bytes 14680088
  19.9 4.1 %dense.1.refs_4_.refs_2_.refs_8_ = bf16[4096,1792]{1,0:T(8,128)(2,1)S(1)} custom-call(s32[1,224]{1,0:T(1,128)} %index_hbm.4, bf16[224,128,128]{2,1,0:T(8,128)(2,1)} %blocks.3, bf16[24,8192]{1,0:T(8,128)(2,1)S(1)} %pack.2.refs_0_), custom_call_target="tpu_custom_call" | custom-call | tf_op jit(solution)/shard_map/dense/pallas_call | solution.py:219
  24.1 0.0 collective-permute-done.1.refs_2_
  24.1 0.1 pack.3.refs_0_
  24.2 0.1 collective-permute-start.6
  24.2 0.4 collective-permute-start.9
  24.6 1.7 %collective-permute-start.8 = (bf16[24,8192]{1,0:T(8,128)(2,1)S(1)}, bf16[24,8192]{1,0:T(8,128)(2,1)S(1)}, u32[]{:S(2)}, u32[]{:S(2)}) collective-permute-start(bf16[24,8192]{1,0:T(8,128)(2,1)S(1)} %pack.2.refs_0_), channel_id=1, source_target_pairs={{0,4},{1,5},{2,6},{3,7},{4,0},{5,1},{6,2},{7,3},{8,12},{9,13},{10,... | collective-permute-start | bytes 1179656 | tf_op jit(solution)/shard_map/ppermute | solution.py:49
  26.3 1.5 %collective-permute-start.7 = (bf16[24,8192]{1,0:T(8,128)(2,1)S(1)}, bf16[24,8192]{1,0:T(8,128)(2,1)S(1)}, u32[]{:S(2)}, u32[]{:S(2)}) collective-permute-start(bf16[24,8192]{1,0:T(8,128)(2,1)S(1)} %pack.2.refs_0_), channel_id=1, source_target_pairs={{0,2},{1,3},{2,0},{3,1},{4,6},{5,7},{6,4},{7,5},{8,10},{9,11},{10,... | collective-permute-start | bytes 1179656 | tf_op jit(solution)/shard_map/ppermute | solution.py:49
  27.8 1.4 %copy-done.1 = bf16[4096,1792]{1,0:T(8,128)(2,1)S(1)} copy-done((bf16[4096,1792]{1,0:T(8,128)(2,1)S(1)}, bf16[4096,1792]{1,0:T(8,128)(2,1)}, u32[]{:S(2)}) %copy-start.1) | copy-done | bytes 14680088
  29.2 23.9 %own_pass.1 = (bf16[64,1792]{1,0:T(8,128)(2,1)S(1)}, bf16[64,1792]{1,0:T(8,128)(2,1)S(1)}, bf16[64,1792]{1,0:T(8,128)(2,1)S(1)}, bf16[64,8192]{1,0:T(8,128)(2,1)...) custom-call(s32[1,224]{1,0:T(1,128)} %index_hbm.5, ...), custom_call_target="tpu_custom_call" | custom-call | flops 5637144576 | bytes 14680064 | tf_op jit(solution)/shard_map/own_pass/pallas_call | solution.py:366
  53.1 0.1 collective-permute-start.14
  53.2 0.5 collective-permute-start.10
  53.7 0.1 collective-permute-start.13
  53.8 0.4 collective-permute-start.12
  54.2 0.1 collective-permute-start.11
  54.3 0.8 collective-permute-done.14.refs_1_
  55.1 0.2 add_and_cut.1
  55.3 0.6 collective-permute-start.15
  55.9 0.4 collective-permute-start.16
  56.2 2.6 %collective-permute-start.17 = (bf16[8,8192]{1,0:T(8,128)(2,1)S(1)}, bf16[8,8192]{1,0:T(8,128)(2,1)S(1)}, u32[]{:S(2)}, u32[]{:S(2)}) collective-permute-start(bf16[8,8192]{1,0:T(8,128)(2,1)S(1)} %get-tuple-element.45), channel_id=1, source_target_pairs={{0,6},{1,7},{2,4},{3,5},{4,2},{5,3},{6,0},{7,1},{8,14},{9,15},{10,... | collective-permute-start | bytes 393224 | tf_op jit(solution)/shard_map/ppermute | solution.py:49
  58.8 13.7 %rest_acts.1 = (bf16[192,1792]{1,0:T(8,128)(2,1)S(1)}, bf16[192,1792]{1,0:T(8,128)(2,1)S(1)}, bf16[192,1792]{1,0:T(8,128)(2,1)S(1)}, bf16[192,8192]{1,0:T(8,128)(2,1)S(1)}) custom-call(bf16[24,8192]{1,0:T(8,128)(2,1)S(1)} %pack.2.refs_0_, bf16[24,8192]{1,0:T(8,128)(2,1)S(1)} %collective-permute-done.7.refs_1_, ...), custom_call_target="tpu_custom_call" | custom-call | flops 8455716864 | bytes 14680064 | tf_op jit(solution)/shard_map/rest_acts/pallas_call | solution.py:281
  72.6 9.5 %grads.1 = (bf16[8,4096]{1,0:T(8,128)(2,1)}, bf16[8,4096]{1,0:T(8,128)(2,1)}, f32[70,128,128]{2,1,0:T(8,128)}, f32[70,128,128]{2,1,0:T(8,128)}, f32[70,128,128]{2,1,0:T(8,128)}) custom-call(s32[3,128]{1,0:T(4,128)S(1)} %get-tuple-element.28.spots, bf16[64,8192]{1,0:T(8,128)(2,1)S(1)} %get-tuple-element.31.own, bf16[192,8192]{1,0:T(8,128)(2,1)S(1)} %get-tuple-element.36.rest, ...), custom_call_target="tpu_custom_call" | custom-call | flops 1761607680 | bytes 13762560 | tf_op jit(solution)/shard_map/grads/pallas_call | solution.py:470
  (17 shorter events, 0.1 us)
Async XLA Ops:
  1.5 13.2 %collective-permute-start.5 = (bf16[8,8192]{1,0:T(8,128)(2,1)S(1)}, bf16[8,8192]{1,0:T(8,128)(2,1)S(1)}, u32[]{:S(2)}, u32[]{:S(2)}) collective-permute-start(bf16[8,8192]{1,0:T(8,128)(2,1)S(1)} %side_by_side.1.source.refs_0_), channel_id=1, source_target_pairs={{0,24},{8,16},{16,8},{24,0},{1,25},{9,17},{17,9},{25,1},{2,26},{10... | collective-permute-start | bytes 393224 | tf_op jit(solution)/shard_map/ppermute | solution.py:49
  6.6 11.1 %collective-permute-start.4 = (bf16[8,8192]{1,0:T(8,128)(2,1)S(1)}, bf16[8,8192]{1,0:T(8,128)(2,1)S(1)}, u32[]{:S(2)}, u32[]{:S(2)}) collective-permute-start(bf16[8,8192]{1,0:T(8,128)(2,1)S(1)} %side_by_side.1.source.refs_0_), channel_id=1, source_target_pairs={{0,16},{8,24},{16,0},{24,8},{1,17},{9,25},{17,1},{25,9},{2,18},{10... | collective-permute-start | bytes 393224 | tf_op jit(solution)/shard_map/ppermute | solution.py:49
  6.6 11.1 %collective-permute-start.3 = (bf16[8,8192]{1,0:T(8,128)(2,1)S(1)}, bf16[8,8192]{1,0:T(8,128)(2,1)S(1)}, u32[]{:S(2)}, u32[]{:S(2)}) collective-permute-start(bf16[8,8192]{1,0:T(8,128)(2,1)S(1)} %side_by_side.1.source.refs_0_), channel_id=1, source_target_pairs={{0,8},{8,0},{16,24},{24,16},{1,9},{9,1},{17,25},{25,17},{2,10},{10... | collective-permute-start | bytes 393224 | tf_op jit(solution)/shard_map/ppermute | solution.py:49
  7.3 16.8 %collective-permute-start.1 = (bf16[8,8192]{1,0:T(8,128)(2,1)S(1)}, bf16[8,8192]{1,0:T(8,128)(2,1)S(1)}, u32[]{:S(2)}, u32[]{:S(2)}) collective-permute-start(bf16[8,8192]{1,0:T(8,128)(2,1)S(1)} %side_by_side.1.source.refs_0_), channel_id=1, source_target_pairs={{0,4},{1,5},{2,6},{3,7},{4,0},{5,1},{6,2},{7,3},{8,12},{9,13},{10,... | collective-permute-start | bytes 393224 | tf_op jit(solution)/shard_map/ppermute | solution.py:49
  8.9 15.1 %collective-permute-start = (bf16[8,8192]{1,0:T(8,128)(2,1)S(1)}, bf16[8,8192]{1,0:T(8,128)(2,1)S(1)}, u32[]{:S(2)}, u32[]{:S(2)}) collective-permute-start(bf16[8,8192]{1,0:T(8,128)(2,1)S(1)} %side_by_side.1.source.refs_0_), channel_id=1, source_target_pairs={{0,2},{1,3},{2,0},{3,1},{4,6},{5,7},{6,4},{7,5},{8,10},{9,11},{10,... | collective-permute-start | bytes 393224 | tf_op jit(solution)/shard_map/ppermute | solution.py:49
  14.7 5.2 %copy-start = (bf16[4096,1792]{1,0:T(8,128)(2,1)}, bf16[4096,1792]{1,0:T(8,128)(2,1)S(1)}, u32[]{:S(2)}) copy-start(bf16[4096,1792]{1,0:T(8,128)(2,1)S(1)} %get-tuple-element.30.refs_3_.refs_9_) | copy-start | bytes 44040196
  14.7 9.4 %collective-permute-start.2 = (bf16[8,8192]{1,0:T(8,128)(2,1)S(1)}, bf16[8,8192]{1,0:T(8,128)(2,1)S(1)}, u32[]{:S(2)}, u32[]{:S(2)}) collective-permute-start(bf16[8,8192]{1,0:T(8,128)(2,1)S(1)} %get-tuple-element.29), channel_id=1, source_target_pairs={{0,6},{1,7},{2,4},{3,5},{4,2},{5,3},{6,0},{7,1},{8,14},{9,15},{10,... | collective-permute-start | bytes 393224 | tf_op jit(solution)/shard_map/ppermute | solution.py:49
  24.1 5.2 %copy-start.1 = (bf16[4096,1792]{1,0:T(8,128)(2,1)S(1)}, bf16[4096,1792]{1,0:T(8,128)(2,1)}, u32[]{:S(2)}) copy-start(bf16[4096,1792]{1,0:T(8,128)(2,1)} %copy-done) | copy-start | bytes 44040196
  24.2 3.6 %collective-permute-start.6 = (bf16[32,8192]{1,0:T(8,128)(2,1)S(1)}, bf16[32,8192]{1,0:T(8,128)(2,1)S(1)}, u32[]{:S(2)}, u32[]{:S(2)}) collective-permute-start(bf16[32,8192]{1,0:T(8,128)(2,1)S(1)} %pack.3.refs_0_), channel_id=1, source_target_pairs={{0,1},{1,0},{2,3},{3,2},{4,5},{5,4},{6,7},{7,6},{8,9},{9,8},{10,11... | collective-permute-start | bytes 1572872 | tf_op jit(solution)/shard_map/ppermute | solution.py:49
  24.2 29.5 %collective-permute-start.9 = (bf16[24,8192]{1,0:T(8,128)(2,1)S(1)}, bf16[24,8192]{1,0:T(8,128)(2,1)S(1)}, u32[]{:S(2)}, u32[]{:S(2)}) collective-permute-start(bf16[24,8192]{1,0:T(8,128)(2,1)S(1)} %pack.2.refs_0_), channel_id=1, source_target_pairs={{0,6},{1,7},{2,4},{3,5},{4,2},{5,3},{6,0},{7,1},{8,14},{9,15},{10,... | collective-permute-start | bytes 1179656 | tf_op jit(solution)/shard_map/ppermute | solution.py:49
  24.6 29.2 %collective-permute-start.8 = (bf16[24,8192]{1,0:T(8,128)(2,1)S(1)}, bf16[24,8192]{1,0:T(8,128)(2,1)S(1)}, u32[]{:S(2)}, u32[]{:S(2)}) collective-permute-start(bf16[24,8192]{1,0:T(8,128)(2,1)S(1)} %pack.2.refs_0_), channel_id=1, source_target_pairs={{0,4},{1,5},{2,6},{3,7},{4,0},{5,1},{6,2},{7,3},{8,12},{9,13},{10,... | collective-permute-start | bytes 1179656 | tf_op jit(solution)/shard_map/ppermute | solution.py:49
  26.3 27.9 %collective-permute-start.7 = (bf16[24,8192]{1,0:T(8,128)(2,1)S(1)}, bf16[24,8192]{1,0:T(8,128)(2,1)S(1)}, u32[]{:S(2)}, u32[]{:S(2)}) collective-permute-start(bf16[24,8192]{1,0:T(8,128)(2,1)S(1)} %pack.2.refs_0_), channel_id=1, source_target_pairs={{0,2},{1,3},{2,0},{3,1},{4,6},{5,7},{6,4},{7,5},{8,10},{9,11},{10,... | collective-permute-start | bytes 1179656 | tf_op jit(solution)/shard_map/ppermute | solution.py:49
  53.1 2.0 %collective-permute-start.14 = (bf16[32,8192]{1,0:T(8,128)(2,1)S(1)}, bf16[32,8192]{1,0:T(8,128)(2,1)S(1)}, u32[]{:S(2)}, u32[]{:S(2)}) collective-permute-start(bf16[32,8192]{1,0:T(8,128)(2,1)S(1)} %get-tuple-element.34), channel_id=1, source_target_pairs={{0,1},{1,0},{2,3},{3,2},{4,5},{5,4},{6,7},{7,6},{8,9},{9,8},{10,11... | collective-permute-start | bytes 1572872 | tf_op jit(solution)/shard_map/ppermute | solution.py:49
  53.2 2.7 %collective-permute-start.10 = (bf16[24,8192]{1,0:T(8,128)(2,1)S(1)}, bf16[24,8192]{1,0:T(8,128)(2,1)S(1)}, u32[]{:S(2)}, u32[]{:S(2)}) collective-permute-start(bf16[24,8192]{1,0:T(8,128)(2,1)S(1)} %pack.2.refs_0_), channel_id=1, source_target_pairs={{0,1},{1,0},{2,3},{3,2},{4,5},{5,4},{6,7},{7,6},{8,9},{9,8},{10,11... | collective-permute-start | bytes 1179656 | tf_op jit(solution)/shard_map/ppermute | solution.py:49
  53.7 2.5 %collective-permute-start.13 = (bf16[24,8192]{1,0:T(8,128)(2,1)S(1)}, bf16[24,8192]{1,0:T(8,128)(2,1)S(1)}, u32[]{:S(2)}, u32[]{:S(2)}) collective-permute-start(bf16[24,8192]{1,0:T(8,128)(2,1)S(1)} %collective-permute-done.9.refs_3_), channel_id=1, source_target_pairs={{0,1},{1,0},{2,3},{3,2},{4,5},{5,4},{6,7},{7,6},{8,9},{9,8},{10,11... | collective-permute-start | bytes 1179656 | tf_op jit(solution)/shard_map/ppermute | solution.py:49
  53.8 5.0 %collective-permute-start.12 = (bf16[24,8192]{1,0:T(8,128)(2,1)S(1)}, bf16[24,8192]{1,0:T(8,128)(2,1)S(1)}, u32[]{:S(2)}, u32[]{:S(2)}) collective-permute-start(bf16[24,8192]{1,0:T(8,128)(2,1)S(1)} %collective-permute-done.8.refs_2_), channel_id=1, source_target_pairs={{0,1},{1,0},{2,3},{3,2},{4,5},{5,4},{6,7},{7,6},{8,9},{9,8},{10,11... | collective-permute-start | bytes 1179656 | tf_op jit(solution)/shard_map/ppermute | solution.py:49
  54.2 4.6 %collective-permute-start.11 = (bf16[24,8192]{1,0:T(8,128)(2,1)S(1)}, bf16[24,8192]{1,0:T(8,128)(2,1)S(1)}, u32[]{:S(2)}, u32[]{:S(2)}) collective-permute-start(bf16[24,8192]{1,0:T(8,128)(2,1)S(1)} %collective-permute-done.7.refs_1_), channel_id=1, source_target_pairs={{0,1},{1,0},{2,3},{3,2},{4,5},{5,4},{6,7},{7,6},{8,9},{9,8},{10,11... | collective-permute-start | bytes 1179656 | tf_op jit(solution)/shard_map/ppermute | solution.py:49
  55.3 17.2 %collective-permute-start.15 = (bf16[8,8192]{1,0:T(8,128)(2,1)S(1)}, bf16[8,8192]{1,0:T(8,128)(2,1)S(1)}, u32[]{:S(2)}, u32[]{:S(2)}) collective-permute-start(bf16[8,8192]{1,0:T(8,128)(2,1)S(1)} %get-tuple-element.43), channel_id=1, source_target_pairs={{0,2},{1,3},{2,0},{3,1},{4,6},{5,7},{6,4},{7,5},{8,10},{9,11},{10,... | collective-permute-start | bytes 393224 | tf_op jit(solution)/shard_map/ppermute | solution.py:49
  55.9 16.7 %collective-permute-start.16 = (bf16[8,8192]{1,0:T(8,128)(2,1)S(1)}, bf16[8,8192]{1,0:T(8,128)(2,1)S(1)}, u32[]{:S(2)}, u32[]{:S(2)}) collective-permute-start(bf16[8,8192]{1,0:T(8,128)(2,1)S(1)} %get-tuple-element.44), channel_id=1, source_target_pairs={{0,4},{1,5},{2,6},{3,7},{4,0},{5,1},{6,2},{7,3},{8,12},{9,13},{10,... | collective-permute-start | bytes 393224 | tf_op jit(solution)/shard_map/ppermute | solution.py:49
  56.2 16.3 %collective-permute-start.17 = (bf16[8,8192]{1,0:T(8,128)(2,1)S(1)}, bf16[8,8192]{1,0:T(8,128)(2,1)S(1)}, u32[]{:S(2)}, u32[]{:S(2)}) collective-permute-start(bf16[8,8192]{1,0:T(8,128)(2,1)S(1)} %get-tuple-element.45), channel_id=1, source_target_pairs={{0,6},{1,7},{2,4},{3,5},{4,2},{5,3},{6,0},{7,1},{8,14},{9,15},{10,... | collective-permute-start | bytes 393224 | tf_op jit(solution)/shard_map/ppermute | solution.py:49
